TPU v7x, 128 devices: a whole 4x4x4 slice. The times are simulated.
128 devices in a mesh: tm: 4 (over y_hi, core), seq: 32 (over x, y_lo, z).
Axes of the slice: x: 4, y: 4 (y_hi: 2, y_lo: 2; y = y_hi * 2 + y_lo), z: 4, core: 2. Of those that a mesh axis runs over, the one named last changes fastest.
Arguments:
- trajectory: float32 [4, 1024, 5120], P('tm', 'seq'), may hold values from -6 to 6
- qkv_weight: bfloat16 [3, 5120, 4096], P(None, None, 'seq'), may hold values from -1 to 1
- out_weight: bfloat16 [4096, 5120], P('seq'), may hold values from -0.75 to 0.75
- shift_table: float32 [50, 5120], replicated, may hold values from -3 to 3
- scale_table: float32 [50, 5120], replicated, may hold values from -0.9 to 0.9
- gate_table: float32 [50, 5120], replicated, may hold values from 0.5 to 2
- step_sizes: float32 [50], replicated, may hold values from 0.1 to 0.5
- window_start: int32 [1], replicated, may hold values from 0 to 46
Outputs:
- new_trajectory: float32 [4, 1024, 5120], P('tm', 'seq')
All inputs are finite; a program needn't handle non-finite values.
Results may differ from a plain program's by a relative error of at most 0.0056.
Values may be sent and summed in bfloat16 or wider, within the bound.
No kernel may reach another device: no remote copies, remote signals or barrier semaphores. Data moves between devices by JAX's collectives and lax.ppermute only.
A program may use at most 128 MiB of HBM per device.

v0:
```python
import math

import jax
import jax.numpy as jnp
from jax import lax
from jax.sharding import PartitionSpec as P

HDIM = 128


def entering(part, axis, combine, identity):
    place = lax.axis_index(axis)
    gathered = lax.all_gather(part, axis)
    state = jnp.zeros_like(part) + jnp.asarray(identity, part.dtype)

    def one(lap, state):
        return combine(state, lax.dynamic_index_in_dim(gathered, lap, 0, False))

    return lax.fori_loop(0, place, one, state)


def attend_local(stacked, head_dim):
    tokens = stacked.shape[1]
    width = stacked.shape[2]
    local_heads = width // head_dim
    block = min(512, tokens)
    queries = stacked[0].reshape(tokens // block, block, local_heads, head_dim)
    keys = stacked[1].reshape(tokens, local_heads, head_dim)
    values = stacked[2].reshape(tokens, local_heads, head_dim)

    def one_block(query_block):
        scores = jnp.einsum(
            "qhd,khd->hqk", query_block, keys, preferred_element_type=jnp.float32
        ) / math.sqrt(head_dim)
        top = jnp.max(scores, axis=-1, keepdims=True)
        weights = jnp.exp(scores - top)
        probs = (weights / jnp.sum(weights, axis=-1, keepdims=True)).astype(jnp.bfloat16)
        return jnp.einsum("hqk,khd->qhd", probs, values, preferred_element_type=jnp.float32).astype(
            jnp.bfloat16
        )

    attended = lax.map(one_block, queries)
    return attended.reshape(tokens, width)


def add_terms(earlier, later):
    return earlier + later


def on_device(
    trajectory,
    qkv_weight,
    out_weight,
    shift_table,
    scale_table,
    gate_table,
    step_sizes,
    window_start,
):
    steps_dev = trajectory.shape[0]
    group = lax.axis_index("tm")
    index = window_start[0] + group * steps_dev + 0
    shift = lax.dynamic_slice_in_dim(shift_table, index, 1, 0)[0]
    scale = lax.dynamic_slice_in_dim(scale_table, index, 1, 0)[0]
    gates = lax.dynamic_slice_in_dim(gate_table, index, 1, 0)[0]
    steps = lax.dynamic_slice_in_dim(step_sizes, index, 1, 0)[0]
    state = trajectory[0]
    normed = state * lax.rsqrt(jnp.mean(state * state, axis=-1, keepdims=True) + 1e-06)
    modulated_list = [(normed * (1.0 + scale) + shift).astype(jnp.bfloat16)]
    modulated = jnp.stack(modulated_list, axis=0)
    per_head = jnp.einsum(
        "krd,adc->akrc",
        lax.all_gather(modulated, "seq", axis=1, tiled=True),
        qkv_weight,
        preferred_element_type=jnp.float32,
    ).astype(jnp.bfloat16)
    attended = jnp.stack([attend_local(per_head[:, 0], HDIM)], axis=0)
    projected_out = lax.psum_scatter(
        jnp.einsum("krh,hd->rkd", attended, out_weight, preferred_element_type=jnp.float32),
        "seq",
        scatter_dimension=0,
        tiled=True,
    ).transpose(1, 0, 2)
    drift = jnp.stack([steps * (gates * projected_out[0])], axis=0)
    summed = jnp.cumsum(drift, axis=0)
    start_state = jnp.where(group == 0, trajectory[0], jnp.zeros_like(trajectory[0]))
    term = summed[-1] + start_state
    prefix = entering(term, "tm", add_terms, jnp.zeros_like(term))
    return prefix[None] + start_state[None] + summed


def solution(mesh):
    in_specs = (P("tm", "seq", None), P(None, None, "seq"), P("seq", None), P(), P(), P(), P(), P())
    out_specs = P("tm", "seq", None)
    return jax.shard_map(
        on_device, mesh=mesh, in_specs=in_specs, out_specs=out_specs, check_vma=False
    )
```

profile of v0, /device:TPU:17, one launch (start us, length us, event | category | flops | bytes accessed | tf_op | source)
XLA Modules:
  0.0 478.3 jit_solution(17658546959890512122)
XLA Ops:
  7.3 1.2 multiply_reduce_fusion.1
  8.6 1.0 dynamic-slice_add_fusion
  9.6 2.0 add_convert_fusion
  11.6 154.9 %all-gather.3.cloned.1.call-done = bf16[1,1024,5120]{2,1,0:T(8,128)(2,1)} async-done(((bf16[1,32,5120]{2,1,0:T(8,128)(2,1)}), bf16[1,1024,5120]{2,1,0:T(8,128)(2,1)}) %all-gather.3.cloned.1.call-update) | async-done | bytes 10485776 | tf_op jit(solution)/shard_map/all_gather | solution.py:73
  166.5 9.4 %fusion.15 = bf16[3,1,1024,128]{3,2,0,1:T(8,128)(2,1)S(1)} fusion(bf16[3,5120,128]{2,1,0:T(8,128)(2,1)} %param.13, bf16[1,1024,5120]{2,1,0:T(8,128)(2,1)} %all-gather.3.cloned.1.call-done), kind=kOutput, calls=%fused_computation.19 | convolution fusion | flops 4026925056 | bytes 15204352 | tf_op jit(solution)/shard_map/krd,adc->akrc/dot_general | solution.py:71
  176.0 3.4 while.20
  176.1 0.5 multiply_reduce_fusion.3
  176.6 0.5 fusion.30
  177.1 0.6 fusion.31
  177.8 0.5 multiply_reduce_fusion.3
  178.3 0.5 fusion.30
  178.8 0.6 fusion.31
  179.4 8.6 %convolution_bitcast_fusion = f32[1024,1,5120]{2,0,1:T(8,128)} fusion(bf16[1024,128]{1,0:T(8,128)(2,1)S(1)} %bitcast.93, bf16[128,5120]{1,0:T(8,128)(2,1)S(1)} %copy-done), kind=kOutput, calls=%fused_computation.15 | convolution fusion | flops 1342177280 | bytes 22544384 | tf_op jit(solution)/shard_map/krh,hd->rkd/dot_general | solution.py:79
  188.1 0.6 copy-done.3
  188.7 0.6 dynamic_slice.20
  189.3 0.9 constant_dynamic-slice_fusion.1
  190.3 248.9 %reduce-scatter.2.cloned.1.call-done = f32[32,1,5120]{2,0,1:T(8,128)} async-done(((f32[1024,1,5120]{2,0,1:T(8,128)}), f32[32,1,5120]{2,0,1:T(8,128)}) %reduce-scatter.2.cloned.1.call-update) | async-done | bytes 655376 | tf_op jit(solution)/shard_map/reduce_scatter | solution.py:78
  439.2 2.6 fusion.22
  441.8 24.4 %all-gather.5.cloned.1.call-done = f32[4,32,5120]{2,1,0:T(8,128)} async-done(((f32[1,32,5120]{2,1,0:T(8,128)}), f32[4,32,5120]{2,1,0:T(8,128)}) %all-gather.5.cloned.1.call-update) | async-done | bytes 2621456 | tf_op jit(solution)/shard_map/all_gather | solution.py:13
  466.3 3.8 while.21
  466.3 1.3 bitcast_add_fusion.3
  467.6 1.2 bitcast_add_fusion.3
  468.9 1.2 bitcast_add_fusion.3
  470.1 1.6 fusion.20
  (17 shorter events, 0.3 us)
Async XLA Ops:
  6.5 172.9 %copy-start = (bf16[128,5120]{1,0:T(8,128)(2,1)S(1)}, bf16[128,5120]{1,0:T(8,128)(2,1)}, u32[]{:S(2)}) copy-start(bf16[128,5120]{1,0:T(8,128)(2,1)} %param.14) | copy-start | bytes 3932164
  6.5 160.0 %all-gather.3.cloned.1.call-start = ((), (), s32[]{:S(2)}) async-start(), calls=%async_computation.1 | async-start | bytes 10813440 | tf_op jit(solution)/shard_map/all_gather | solution.py:73
  11.6 427.6 %reduce-scatter.2.cloned.1.call-start = ((), (), s32[]{:S(2)}) async-start(), calls=%async_computation.2 | async-start | bytes 21626880 | tf_op jit(solution)/shard_map/reduce_scatter | solution.py:78
  188.0 0.7 copy-start.3
  188.0 251.1 %copy-start.1 = (f32[1,32,5120]{2,1,0:T(8,128)S(1)}, f32[1,32,5120]{2,1,0:T(8,128)}, u32[]{:S(2)}) copy-start(f32[1,32,5120]{2,1,0:T(8,128)} %param.12) | copy-start | bytes 1966084
  188.1 278.1 %all-gather.5.cloned.1.call-start = ((), (), s32[]{:S(2)}) async-start(), calls=%async_computation.3 | async-start | bytes 3276800 | tf_op jit(solution)/shard_map/all_gather | solution.py:13
  466.3 3.9 copy-start.2
Sparse Core Ops, SparseCore 0:
  11.7 154.7 all-gather.2
  188.2 250.9 reduce-scatter.1
  441.9 24.2 all-gather.4
where the time goes:
time: 480 us; the launch traced here: 478 us
  waiting for transfers between devices  428 us (89%)
  matrix products  20.4 us (4%)
  between operations  14 us (3%)
  other arithmetic  13.3 us (3%)
    reduce_scatter x1, waiting for transfers between devices, on_device(): lax.psum_scatter(jnp.einsum('krh,hd->rkd', attended, out_weight, preferre...  249 us
    all_gather x1, waiting for transfers between devices, on_device(): lax.all_gather(modulated, 'seq', axis=1, tiled=True)  155 us
    all_gather x1, waiting for transfers between devices, entering(): gathered = lax.all_gather(part, axis)  24.4 us
  transfers between devices with their start and end apart: 3, of which 3 were waited for; matrix products, arithmetic and copies ran while one was open for 0% of the time, Pallas kernels for 0%

commit v1 on v0

v1 whole, which is shorter than its diff:
```python
import functools
import math

import jax
import jax.numpy as jnp
from jax import lax
from jax.experimental import pallas as pl
from jax.experimental.pallas import tpu as pltpu
from jax.sharding import PartitionSpec as P

HDIM = 128
XS, YLS, ZS = 4, 2, 4
BF16, F32 = jnp.bfloat16, jnp.float32
VMEM = pl.BlockSpec(memory_space=pltpu.VMEM)
SMEM = pl.BlockSpec(memory_space=pltpu.SMEM)
PARAMS = pltpu.CompilerParams(vmem_limit_bytes=56 * 1024 * 1024)


def moves(rule):
    pairs = []
    for yh in range(2):
        for core in range(2):
            for x in range(XS):
                for yl in range(YLS):
                    for z in range(ZS):
                        to = rule(yh, core, x, yl, z)
                        if to is not None:
                            pairs.append((flat(yh, core, x, yl, z), flat(*to)))
    return pairs


def flat(yh, core, x, yl, z):
    return (((yh * 2 + core) * XS + x) * YLS + yl) * ZS + z


def send(value, rule):
    return lax.ppermute(value, ("tm", "seq"), moves(rule))


def along_x(step):
    return lambda yh, core, x, yl, z: (yh, core, (x + step) % XS, yl, z)


def along_z(step):
    return lambda yh, core, x, yl, z: (yh, core, x, yl, (z + step) % ZS)


def to_other_core(yh, core, x, yl, z):
    return (yh, 1 - core, x, yl, z)


def to_partner(yh, core, x, yl, z):
    return (yh, core, x, 1 - yl, z)


def to_both_sides(yh, core, x, yl, z):
    return (yh if core == 0 else 1 - yh, core, x, 1 - yl, z)


def to_later_half(yh, core, x, yl, z):
    return (1, core, x, yl, z) if yh == 0 else None


def to_later_core(yh, core, x, yl, z):
    return (yh, 1, x, yl, z) if core == 0 else None


def modulate_kernel(index, state, scale, shift, out):
    row = index[0]
    value = state[...]
    mean = jnp.mean(value * value, axis=-1, keepdims=True)
    normed = value * lax.rsqrt(mean + 1e-06)
    out[...] = (normed * (1.0 + scale[pl.ds(row, 1), :]) + shift[pl.ds(row, 1), :]).astype(BF16)


def modulate(index, state, scale, shift):
    return pl.pallas_call(
        modulate_kernel,
        out_shape=jax.ShapeDtypeStruct(state.shape, BF16),
        in_specs=[SMEM, VMEM, VMEM, VMEM],
        out_specs=VMEM,
        compiler_params=PARAMS,
    )(index, state, scale, shift)


def project_kernel(count, chunk, *refs):
    core_ref, pieces, (own, mine, theirs), outs, total = (
        refs[0],
        refs[1 : 1 + count],
        refs[1 + count : 4 + count],
        refs[4 + count : 7 + count],
        refs[-1],
    )
    depth = own.shape[1]
    half = depth // 2
    first = core_ref[0] * half
    total[...] = jnp.zeros_like(total)

    def side(weight, start):
        def one(step, carry):
            at = pl.multiple_of(step * chunk, chunk)
            column = pl.multiple_of(start + at, 128)
            rows = jnp.concatenate([piece[:, pl.ds(column, chunk)] for piece in pieces], axis=0)
            for kind in range(3):
                both = jnp.concatenate(
                    [own[kind, pl.ds(column, chunk), :], weight[kind, pl.ds(at, chunk), :]], axis=-1
                )
                total[kind] += jnp.dot(rows, both, preferred_element_type=F32)
            return carry

        lax.fori_loop(0, half // chunk, one, 0)

    side(mine, first)
    side(theirs, half - first)
    for kind in range(3):
        outs[kind][...] = total[kind].astype(BF16)


def project(core, pieces, own, mine, theirs):
    tokens = sum(piece.shape[0] for piece in pieces)
    wide = 2 * HDIM
    return pl.pallas_call(
        functools.partial(project_kernel, len(pieces), 512),
        out_shape=[jax.ShapeDtypeStruct((tokens, wide), BF16)] * 3,
        in_specs=[SMEM] + [VMEM] * (len(pieces) + 3),
        out_specs=[VMEM] * 3,
        scratch_shapes=[pltpu.VMEM((3, tokens, wide), F32)],
        compiler_params=PARAMS,
    )(core, *pieces, own, mine, theirs)


def attend_kernel(cuts, queries, keys, values, far_keys, far_values, own, other, *refs):
    outs, attended = refs[:-1], refs[-1]
    scale = 1.0 / math.sqrt(HDIM)
    contract = (((1,), (1,)), ((), ()))
    tokens = queries.shape[0]
    rows = 256
    for head in range(2):
        here = slice(head * HDIM, (head + 1) * HDIM)
        there = slice((1 - head) * HDIM, (2 - head) * HDIM)
        all_keys = jnp.concatenate([keys[:, here], far_keys[:, there]], axis=0)
        all_values = jnp.concatenate([values[:, here], far_values[:, there]], axis=0)
        for start in range(0, tokens, rows):
            scores = lax.dot_general(
                queries[start : start + rows, here], all_keys, contract, preferred_element_type=F32
            )
            top = jnp.max(scores, axis=-1, keepdims=True)
            weights = jnp.exp((scores - top) * scale)
            total = jnp.sum(weights, axis=-1, keepdims=True)
            mixed = jnp.dot(weights.astype(BF16), all_values, preferred_element_type=F32)
            attended[start : start + rows, here] = (mixed / total).astype(BF16)
    width = own.shape[1]
    step = 512

    def one(block, carry):
        column = pl.ds(pl.multiple_of(block * step, step), step)
        weight = jnp.concatenate([own[:, column], other[:, column]], axis=0)
        result = jnp.dot(attended[...], weight, preferred_element_type=F32).astype(BF16)
        at = 0
        for out, size in zip(outs, cuts):
            out[:, column] = result[at : at + size]
            at += size
        return carry

    lax.fori_loop(0, width // step, one, 0)


def attend(queries, keys, values, far_keys, far_values, own, other, cuts):
    width = own.shape[1]
    return pl.pallas_call(
        functools.partial(attend_kernel, cuts),
        out_shape=[jax.ShapeDtypeStruct((size, width), BF16) for size in cuts],
        in_specs=[VMEM] * 7,
        out_specs=[VMEM] * len(cuts),
        scratch_shapes=[pltpu.VMEM((queries.shape[0], 2 * HDIM), BF16)],
        compiler_params=PARAMS,
    )(queries, keys, values, far_keys, far_values, own, other)


def gather_plane(part, first, second):
    near = jnp.concatenate(
        [part, send(part, first(1)), send(part, first(-1)), send(part, first(2))], axis=0
    )
    half = near.shape[0] // 2
    before, after = send(near, second(1)), send(near, second(-1))
    opposite_low = send(before[:half], second(1))
    opposite_high = send(after[half:], second(-1))
    return [near, before, after, opposite_low, opposite_high]


def scatter_plane(parts, first, second):
    near, before, after, opposite_low, opposite_high = parts
    half = near.shape[0] // 2
    low, high = send(opposite_low, second(1)), send(opposite_high, second(-1))
    to_after = jnp.concatenate(
        [(after[:half].astype(F32) + low.astype(F32)).astype(BF16), after[half:]], axis=0
    )
    to_before = jnp.concatenate(
        [before[:half], (before[half:].astype(F32) + high.astype(F32)).astype(BF16)], axis=0
    )
    from_before, from_after = send(to_after, second(1)), send(to_before, second(-1))
    total = near.astype(F32) + from_before.astype(F32) + from_after.astype(F32)
    size = near.shape[0] // 4
    kept, to_minus, to_plus, to_opposite = [total[i * size : (i + 1) * size] for i in range(4)]
    arrived = [
        send(to_plus.astype(BF16), first(1)),
        send(to_minus.astype(BF16), first(-1)),
        send(to_opposite.astype(BF16), first(2)),
    ]
    for value in arrived:
        kept = kept + value.astype(F32)
    return kept


def swap_weights(core, weight, axis):
    half = weight.shape[axis] // 2
    mine = send(lax.dynamic_slice_in_dim(weight, core * half, half, axis), to_both_sides)
    return mine, send(mine, to_other_core)


def on_device(
    trajectory, qkv_weight, out_weight, shift_table, scale_table, gate_table, step_sizes, window_start
):
    group = lax.axis_index("tm")
    core = group % 2
    index = window_start[0] + group
    state = trajectory[0]
    rows = state.shape[0]
    mine, theirs = swap_weights(core, qkv_weight, 1)
    out_mine, out_theirs = swap_weights(core, out_weight, 1)
    out_other = jnp.where(
        core == 0,
        jnp.concatenate([out_mine, out_theirs], axis=1),
        jnp.concatenate([out_theirs, out_mine], axis=1),
    )

    modulated = modulate(index[None], state, scale_table, shift_table)
    low = gather_plane(modulated[: rows // 2], along_x, along_z)
    high = gather_plane(modulated[rows // 2 :], along_z, along_x)
    pieces = low + high
    queries, keys, values = project(core[None], pieces, qkv_weight, mine, theirs)
    far_keys, far_values = send(keys, to_partner), send(values, to_partner)
    partial = attend(
        queries,
        keys,
        values,
        far_keys,
        far_values,
        out_weight,
        out_other,
        [piece.shape[0] for piece in pieces],
    )
    projected = jnp.concatenate(
        [
            scatter_plane(partial[:5], along_x, along_z),
            scatter_plane(partial[5:], along_z, along_x),
        ],
        axis=0,
    )
    gates = lax.dynamic_slice_in_dim(gate_table, index, 1, 0)
    step = lax.dynamic_slice_in_dim(step_sizes, index, 1, 0)[0]
    drift = step * (gates * projected)

    start = jnp.where(core == 0, state, send(state, to_later_core))
    start = jnp.where(group < 2, start, send(start, to_later_half))
    beside = send(drift.astype(BF16), to_other_core).astype(F32)
    earlier = send((drift + beside).astype(BF16), to_later_half).astype(F32)
    summed = drift + earlier + jnp.where(core == 1, beside, 0.0)
    return (start + summed)[None]


def solution(mesh):
    in_specs = (P("tm", "seq", None), P(None, None, "seq"), P("seq", None), P(), P(), P(), P(), P())
    out_specs = P("tm", "seq", None)
    return jax.shard_map(
        on_device, mesh=mesh, in_specs=in_specs, out_specs=out_specs, check_vma=False
    )
```

time: 480 us -> 184 us (0.38)
  waiting for transfers between devices: 428 us -> 83.1 us
  starting transfers between devices: 0.09 us -> 57.4 us
  Pallas kernels: 0 us -> 23.8 us
  matrix products: 20.4 us -> 0 us
  between operations: 14 us -> 1.14 us
  local copies, waits for them, and re-layouts: 2.25 us -> 10.6 us
  other arithmetic: 13.3 us -> 7.25 us
    reduce_scatter x1 -> x0, waiting for transfers between devices: 249 us -> none  [on_device(): lax.psum_scatter(jnp.einsum('krh,hd->rkd', attended, out_weight, preferre...]
    all_gather x2 -> x0, waiting for transfers between devices: 179 us -> none  [the longest x1 155 us: on_device(): lax.all_gather(modulated, 'seq', axis=1, tiled=True)]
    ppermute x0 -> x38, waiting for transfers between devices: none -> 83.1 us  [send(): return lax.ppermute(value, ('tm', 'seq'), moves(rule))]
    ppermute x0 -> x38, starting transfers between devices: none -> 57.4 us  [send(): return lax.ppermute(value, ('tm', 'seq'), moves(rule))]
    pallas_call x0 -> x3, Pallas kernels: none -> 23.8 us  [the longest x1 11.6 us: project(): pl.pallas_call(functools.partial(project_kernel, len(pieces), 512), out_s...]
    dot_general x6 -> x0, matrix products: 20.4 us -> none  [the longest x1 9.45 us: on_device(): jnp.einsum('krd,adc->akrc', lax.all_gather(modulated, 'seq', axis=1, tile...]
    add x6 -> x2, other arithmetic: 9.04 us -> 0.15 us  [scatter_plane(): kept = kept + value.astype(F32)]
    slice x0 -> x11, local copies, waits for them, and re-layouts: none -> 5.56 us  [the longest x2 1.49 us: gather_plane(): opposite_high = send(after[half:], second(-1))]
  transfers between devices with their start and end apart: 3 -> 38, of which waited for: 3 -> 18; matrix products, arithmetic and copies ran while one was open for 0% -> 6% of each run, Pallas kernels for 0% -> 13%
where the time goes in v1:
time: 184 us; the launch traced here: 183 us
  waiting for transfers between devices  83.1 us (45%)
  starting transfers between devices  57.4 us (31%)
  Pallas kernels  23.8 us (13%)
  local copies, waits for them, and re-layouts  10.6 us (6%)
  other arithmetic  7.25 us (4%)
    ppermute x38, waiting for transfers between devices, send(): return lax.ppermute(value, ('tm', 'seq'), moves(rule))  83.1 us
    ppermute x38, starting transfers between devices, send(): return lax.ppermute(value, ('tm', 'seq'), moves(rule))  57.4 us
    pallas_call x1, Pallas kernels, project(): pl.pallas_call(functools.partial(project_kernel, len(pieces), 512), out_s...  11.6 us
    pallas_call x1, Pallas kernels, attend(): pl.pallas_call(functools.partial(attend_kernel, cuts), out_shape=[jax.Sha...  9.39 us
  transfers between devices with their start and end apart: 38, of which 18 were waited for; matrix products, arithmetic and copies ran while one was open for 6% of the time, Pallas kernels for 13%

profile of v1, /device:TPU:17, one launch (start us, length us, event | category | flops | bytes accessed | tf_op | source)
XLA Modules:
  0.0 183.3 jit_solution(17175777181303721723)
XLA Ops:
  0.0 3.1 %constant_dynamic-slice_fusion.1 = bf16[3,2560,128]{2,1,0:T(8,128)(2,1)} fusion(bf16[3,5120,128]{2,1,0:T(8,128)(2,1)} %refs_11_.1, s32[]{:T(128)S(6)} %select_n.51), kind=kLoop, calls=%fused_computation.30 | loop fusion | bytes 3932164 | tf_op jit(solution)/shard_map/dynamic_slice | solution.py:217
  3.9 2.8 %shard_map.82 = bf16[32,5120]{1,0:T(8,128)(2,1)} custom-call(s32[1]{0:T(128)} %bitcast.5.index, f32[32,5120]{1,0:T(8,128)} %bitcast.10, f32[50,5120]{1,0:T(8,128)} %scale.1, f32[50,5120]{1,0:T(8,128)} %shift.1), custom_call_target="tpu_custom_call" | custom-call | tf_op jit(solution)/shard_map/pallas_call | solution.py:77
  7.8 3.8 %collective-permute-start.10 = (bf16[16,5120]{1,0:T(8,128)(2,1)S(1)}, bf16[16,5120]{1,0:T(8,128)(2,1)S(1)}, u32[]{:S(2)}, u32[]{:S(2)}) collective-permute-start(bf16[16,5120]{1,0:T(8,128)(2,1)S(1)} %get-tuple-element.41), channel_id=1, source_target_pairs={{0,3},{1,0},{2,1},{3,2},{4,7},{5,4},{6,5},{7,6},{8,11},{9,8},{10,9... | collective-permute-start | bytes 491528 | tf_op jit(solution)/shard_map/ppermute | solution.py:37
  13.5 4.1 %collective-permute-done.10 = bf16[16,5120]{1,0:T(8,128)(2,1)S(1)} collective-permute-done((bf16[16,5120]{1,0:T(8,128)(2,1)S(1)}, bf16[16,5120]{1,0:T(8,128)(2,1)S(1)}, u32[]{:S(2)}, u32[]{:S(2)}) %collective-permute-start.10) | collective-permute-done | bytes 163872 | tf_op jit(solution)/shard_map/ppermute | solution.py:37
  20.6 6.5 %collective-permute-done.16.refs_12_ = bf16[3,2560,128]{2,1,0:T(8,128)(2,1)} collective-permute-done((bf16[3,2560,128]{2,1,0:T(8,128)(2,1)}, bf16[3,2560,128]{2,1,0:T(8,128)(2,1)}, u32[]{:S(2)}, u32[]{:S(2)}) %collective-permute-start.16) | collective-permute-done | bytes 1966112 | tf_op jit(solution)/shard_map/ppermute | solution.py:37
  33.6 12.8 %collective-permute-done.12.refs_7_ = bf16[64,5120]{1,0:T(8,128)(2,1)S(1)} collective-permute-done((bf16[64,5120]{1,0:T(8,128)(2,1)S(1)}, bf16[64,5120]{1,0:T(8,128)(2,1)S(1)}, u32[]{:S(2)}, u32[]{:S(2)}) %collective-permute-start.12) | collective-permute-done | bytes 655392 | tf_op jit(solution)/shard_map/ppermute | solution.py:37
  46.4 3.8 %collective-permute-start.6 = (bf16[64,5120]{1,0:T(8,128)(2,1)S(1)}, bf16[64,5120]{1,0:T(8,128)(2,1)S(1)}, u32[]{:S(2)}, u32[]{:S(2)}) collective-permute-start(bf16[64,5120]{1,0:T(8,128)(2,1)S(1)} %pad_maximum_fusion.refs_1_), channel_id=1, source_target_pairs={{0,3},{1,0},{2,1},{3,2},{4,7},{5,4},{6,5},{7,6},{8,11},{9,8},{10,9... | collective-permute-start | bytes 1966088 | tf_op jit(solution)/shard_map/ppermute | solution.py:37
  52.4 2.7 %collective-permute-start.15 = (bf16[32,5120]{1,0:T(8,128)(2,1)}, bf16[32,5120]{1,0:T(8,128)(2,1)}, u32[]{:S(2)}, u32[]{:S(2)}) collective-permute-start(bf16[32,5120]{1,0:T(8,128)(2,1)} %slice.99), channel_id=1, source_target_pairs={{0,24},{1,25},{2,26},{3,27},{4,28},{5,29},{6,30},{7,31},{8,0},{9,1... | collective-permute-start | bytes 983048 | tf_op jit(solution)/shard_map/ppermute | solution.py:37
  55.8 7.6 %collective-permute-done.6.refs_3_ = bf16[64,5120]{1,0:T(8,128)(2,1)S(1)} collective-permute-done((bf16[64,5120]{1,0:T(8,128)(2,1)S(1)}, bf16[64,5120]{1,0:T(8,128)(2,1)S(1)}, u32[]{:S(2)}, u32[]{:S(2)}) %collective-permute-start.6) | collective-permute-done | bytes 655392 | tf_op jit(solution)/shard_map/ppermute | solution.py:37
  64.7 3.1 %collective-permute-start.8 = (bf16[32,5120]{1,0:T(8,128)(2,1)}, bf16[32,5120]{1,0:T(8,128)(2,1)}, u32[]{:S(2)}, u32[]{:S(2)}) collective-permute-start(bf16[32,5120]{1,0:T(8,128)(2,1)} %slice.96), channel_id=1, source_target_pairs={{0,3},{1,0},{2,1},{3,2},{4,7},{5,4},{6,5},{7,6},{8,11},{9,8},{10,9... | collective-permute-start | bytes 983048 | tf_op jit(solution)/shard_map/ppermute | solution.py:37
  69.6 3.9 %collective-permute-done.7.refs_4_ = bf16[32,5120]{1,0:T(8,128)(2,1)} collective-permute-done((bf16[32,5120]{1,0:T(8,128)(2,1)}, bf16[32,5120]{1,0:T(8,128)(2,1)}, u32[]{:S(2)}, u32[]{:S(2)}) %collective-permute-start.7) | collective-permute-done | bytes 327712 | tf_op jit(solution)/shard_map/ppermute | solution.py:37
  73.5 11.6 %shard_map.83 = (bf16[512,256]{1,0:T(8,128)(2,1)}, bf16[512,256]{1,0:T(8,128)(2,1)}, bf16[512,256]{1,0:T(8,128)(2,1)}) custom-call(s32[1]{0:T(128)} %bitcast.4.refs_0_, bf16[64,5120]{1,0:T(8,128)(2,1)} %copy-done.3, bf16[64,5120]{1,0:T(8,128)(2,1)} %copy-done.8, bf16[64,5120]{1,0:T(8,128)(2,1)} %copy-done.9, ...), custom_call_target="tpu_custom_call" | custom-call | tf_op jit(solution)/shard_map/pallas_call | solution.py:122
  88.0 2.6 %collective-permute-done.18.far_keys = bf16[512,256]{1,0:T(8,128)(2,1)S(1)} collective-permute-done((bf16[512,256]{1,0:T(8,128)(2,1)}, bf16[512,256]{1,0:T(8,128)(2,1)S(1)}, u32[]{:S(2)}, u32[]{:S(2)}) %collective-permute-start.18) | collective-permute-done | bytes 262176 | tf_op jit(solution)/shard_map/ppermute | solution.py:37
  90.5 5.7 %collective-permute-done.19.far_values = bf16[512,256]{1,0:T(8,128)(2,1)S(1)} collective-permute-done((bf16[512,256]{1,0:T(8,128)(2,1)}, bf16[512,256]{1,0:T(8,128)(2,1)S(1)}, u32[]{:S(2)}, u32[]{:S(2)}) %collective-permute-start.19) | collective-permute-done | bytes 262176 | tf_op jit(solution)/shard_map/ppermute | solution.py:37
  96.9 9.4 %shard_map.84 = (bf16[64,5120]{1,0:T(8,128)(2,1)}, bf16[64,5120]{1,0:T(8,128)(2,1)}, bf16[64,5120]{1,0:T(8,128)(2,1)}, bf16[32,5120]{1,0:T(8,128)(2,1)}, bf16[32...) custom-call(bf16[512,256]{1,0:T(8,128)(2,1)} %get-tuple-element.18.q, ...), custom_call_target="tpu_custom_call" | custom-call | tf_op jit(solution)/shard_map/pallas_call | solution.py:170
  112.3 2.7 %collective-permute-start.31 = (bf16[32,5120]{1,0:T(8,128)(2,1)S(1)}, bf16[32,5120]{1,0:T(8,128)(2,1)S(1)}, u32[]{:S(2)}, u32[]{:S(2)}) collective-permute-start(bf16[32,5120]{1,0:T(8,128)(2,1)S(1)} %copy-done.19), channel_id=1, source_target_pairs={{0,24},{1,25},{2,26},{3,27},{4,28},{5,29},{6,30},{7,31},{8,0},{9,1... | collective-permute-start | bytes 983048 | tf_op jit(solution)/shard_map/ppermute | solution.py:37
  119.9 2.7 %collective-permute-start.32 = (bf16[64,5120]{1,0:T(8,128)(2,1)S(1)}, bf16[64,5120]{1,0:T(8,128)(2,1)S(1)}, u32[]{:S(2)}, u32[]{:S(2)}) collective-permute-start(bf16[64,5120]{1,0:T(8,128)(2,1)S(1)} %pad_maximum_fusion.5), channel_id=1, source_target_pairs={{0,24},{1,25},{2,26},{3,27},{4,28},{5,29},{6,30},{7,31},{8,0},{9,1... | collective-permute-start | bytes 1966088 | tf_op jit(solution)/shard_map/ppermute | solution.py:37
  122.6 5.7 %collective-permute-done.23 = bf16[64,5120]{1,0:T(8,128)(2,1)S(1)} collective-permute-done((bf16[64,5120]{1,0:T(8,128)(2,1)S(1)}, bf16[64,5120]{1,0:T(8,128)(2,1)S(1)}, u32[]{:S(2)}, u32[]{:S(2)}) %collective-permute-start.23) | collective-permute-done | bytes 655392 | tf_op jit(solution)/shard_map/ppermute | solution.py:37
  129.7 2.7 %collective-permute-start.27 = (bf16[16,5120]{1,0:T(8,128)(2,1)S(1)}, bf16[16,5120]{1,0:T(8,128)(2,1)S(1)}, u32[]{:S(2)}, u32[]{:S(2)}) collective-permute-start(bf16[16,5120]{1,0:T(8,128)(2,1)S(1)} %get-tuple-element.37), channel_id=1, source_target_pairs={{0,24},{1,25},{2,26},{3,27},{4,28},{5,29},{6,30},{7,31},{8,0},{9,1... | collective-permute-start | bytes 491528 | tf_op jit(solution)/shard_map/ppermute | solution.py:37
  133.7 3.5 %collective-permute-done.26 = bf16[16,5120]{1,0:T(8,128)(2,1)S(1)} collective-permute-done((bf16[16,5120]{1,0:T(8,128)(2,1)S(1)}, bf16[16,5120]{1,0:T(8,128)(2,1)S(1)}, u32[]{:S(2)}, u32[]{:S(2)}) %collective-permute-start.26) | collective-permute-done | bytes 163872 | tf_op jit(solution)/shard_map/ppermute | solution.py:37
  140.3 3.5 %collective-permute-done.34 = bf16[16,5120]{1,0:T(8,128)(2,1)S(1)} collective-permute-done((bf16[16,5120]{1,0:T(8,128)(2,1)S(1)}, bf16[16,5120]{1,0:T(8,128)(2,1)S(1)}, u32[]{:S(2)}, u32[]{:S(2)}) %collective-permute-start.34) | collective-permute-done | bytes 163872 | tf_op jit(solution)/shard_map/ppermute | solution.py:37
  146.2 7.7 %collective-permute-start.36 = (bf16[32,5120]{1,0:T(8,128)(2,1)S(1)}, bf16[32,5120]{1,0:T(8,128)(2,1)S(1)}, u32[]{:S(2)}, u32[]{:S(2)}) collective-permute-start(bf16[32,5120]{1,0:T(8,128)(2,1)S(1)} %fusion.9), channel_id=1, source_target_pairs={{0,32},{1,33},{2,34},{3,35},{4,36},{5,37},{6,38},{7,39},{8,40},{9,... | collective-permute-start | bytes 983048 | tf_op jit(solution)/shard_map/ppermute | solution.py:37
  157.9 15.7 %collective-permute-done.1 = f32[32,5120]{1,0:T(8,128)S(1)} collective-permute-done((f32[32,5120]{1,0:T(8,128)S(1)}, f32[32,5120]{1,0:T(8,128)S(1)}, u32[]{:S(2)}, u32[]{:S(2)}) %collective-permute-start.1) | collective-permute-done | bytes 655392 | tf_op jit(solution)/shard_map/ppermute | solution.py:37
  173.6 7.1 %collective-permute-done.37 = bf16[32,5120]{1,0:T(8,128)(2,1)} collective-permute-done((bf16[32,5120]{1,0:T(8,128)(2,1)}, bf16[32,5120]{1,0:T(8,128)(2,1)}, u32[]{:S(2)}, u32[]{:S(2)}) %collective-permute-start.37) | collective-permute-done | bytes 327712 | tf_op jit(solution)/shard_map/ppermute | solution.py:37
  (131 shorter events, 47.5 us)
Async XLA Ops:
  3.1 24.1 %collective-permute-start.16 = (bf16[3,2560,128]{2,1,0:T(8,128)(2,1)}, bf16[3,2560,128]{2,1,0:T(8,128)(2,1)}, u32[]{:S(2)}, u32[]{:S(2)}) collective-permute-start(bf16[3,2560,128]{2,1,0:T(8,128)(2,1)} %constant_dynamic-slice_fusion.1), channel_id=1, source_target_pairs={{0,4},{1,5},{2,6},{3,7},{4,0},{5,1},{6,2},{7,3},{8,12},{9,13},{10,... | collective-permute-start | bytes 5898248 | tf_op jit(solution)/shard_map/ppermute | solution.py:37
  11.6 17.1 %collective-permute-start.9 = (bf16[16,5120]{1,0:T(8,128)(2,1)S(1)}, bf16[16,5120]{1,0:T(8,128)(2,1)S(1)}, u32[]{:S(2)}, u32[]{:S(2)}) collective-permute-start(bf16[16,5120]{1,0:T(8,128)(2,1)S(1)} %get-tuple-element.41), channel_id=1, source_target_pairs={{0,1},{1,2},{2,3},{3,0},{4,5},{5,6},{6,7},{7,4},{8,9},{9,10},{10,1... | collective-permute-start | bytes 491528 | tf_op jit(solution)/shard_map/ppermute | solution.py:37
  12.3 17.7 %collective-permute-start.2 = (bf16[16,5120]{1,0:T(8,128)(2,1)S(1)}, bf16[16,5120]{1,0:T(8,128)(2,1)S(1)}, u32[]{:S(2)}, u32[]{:S(2)}) collective-permute-start(bf16[16,5120]{1,0:T(8,128)(2,1)S(1)} %get-tuple-element.42), channel_id=1, source_target_pairs={{0,8},{1,9},{2,10},{3,11},{4,12},{5,13},{6,14},{7,15},{8,16},{9,17... | collective-permute-start | bytes 491528 | tf_op jit(solution)/shard_map/ppermute | solution.py:37
  17.6 12.7 %collective-permute-start.3 = (bf16[16,5120]{1,0:T(8,128)(2,1)S(1)}, bf16[16,5120]{1,0:T(8,128)(2,1)S(1)}, u32[]{:S(2)}, u32[]{:S(2)}) collective-permute-start(bf16[16,5120]{1,0:T(8,128)(2,1)S(1)} %get-tuple-element.42), channel_id=1, source_target_pairs={{0,24},{1,25},{2,26},{3,27},{4,28},{5,29},{6,30},{7,31},{8,0},{9,1... | collective-permute-start | bytes 491528 | tf_op jit(solution)/shard_map/ppermute | solution.py:37
  20.1 11.7 %collective-permute-start.4 = (bf16[16,5120]{1,0:T(8,128)(2,1)S(1)}, bf16[16,5120]{1,0:T(8,128)(2,1)S(1)}, u32[]{:S(2)}, u32[]{:S(2)}) collective-permute-start(bf16[16,5120]{1,0:T(8,128)(2,1)S(1)} %get-tuple-element.42), channel_id=1, source_target_pairs={{0,16},{1,17},{2,18},{3,19},{4,20},{5,21},{6,22},{7,23},{8,24},{9,... | collective-permute-start | bytes 491528 | tf_op jit(solution)/shard_map/ppermute | solution.py:37
  27.2 46.4 %collective-permute-start.17 = (bf16[3,2560,128]{2,1,0:T(8,128)(2,1)}, bf16[3,2560,128]{2,1,0:T(8,128)(2,1)}, u32[]{:S(2)}, u32[]{:S(2)}) collective-permute-start(bf16[3,2560,128]{2,1,0:T(8,128)(2,1)} %collective-permute-done.16.refs_12_), channel_id=1, source_target_pairs={{0,32},{1,33},{2,34},{3,35},{4,36},{5,37},{6,38},{7,39},{8,40},{9,... | collective-permute-start | bytes 5898248 | tf_op jit(solution)/shard_map/ppermute | solution.py:37
  28.7 17.6 %collective-permute-start.12 = (bf16[64,5120]{1,0:T(8,128)(2,1)S(1)}, bf16[64,5120]{1,0:T(8,128)(2,1)S(1)}, u32[]{:S(2)}, u32[]{:S(2)}) collective-permute-start(bf16[64,5120]{1,0:T(8,128)(2,1)S(1)} %pad_maximum_fusion.1.refs_6_), channel_id=1, source_target_pairs={{0,8},{1,9},{2,10},{3,11},{4,12},{5,13},{6,14},{7,15},{8,16},{9,17... | collective-permute-start | bytes 1966088 | tf_op jit(solution)/shard_map/ppermute | solution.py:37
  30.1 20.1 %collective-permute-start.20 = (bf16[128,2560]{1,0:T(8,128)(2,1)S(1)}, bf16[128,2560]{1,0:T(8,128)(2,1)S(1)}, u32[]{:S(2)}, u32[]{:S(2)}) collective-permute-start(bf16[128,2560]{1,0:T(8,128)(2,1)S(1)} %constant_dynamic-slice_fusion), channel_id=1, source_target_pairs={{0,4},{1,5},{2,6},{3,7},{4,0},{5,1},{6,2},{7,3},{8,12},{9,13},{10,... | collective-permute-start | bytes 1966088 | tf_op jit(solution)/shard_map/ppermute | solution.py:37
  30.3 19.9 %collective-permute-start.13 = (bf16[64,5120]{1,0:T(8,128)(2,1)S(1)}, bf16[64,5120]{1,0:T(8,128)(2,1)S(1)}, u32[]{:S(2)}, u32[]{:S(2)}) collective-permute-start(bf16[64,5120]{1,0:T(8,128)(2,1)S(1)} %pad_maximum_fusion.1.refs_6_), channel_id=1, source_target_pairs={{0,24},{1,25},{2,26},{3,27},{4,28},{5,29},{6,30},{7,31},{8,0},{9,1... | collective-permute-start | bytes 1966088 | tf_op jit(solution)/shard_map/ppermute | solution.py:37
  31.9 20.5 %collective-permute-start.5 = (bf16[64,5120]{1,0:T(8,128)(2,1)S(1)}, bf16[64,5120]{1,0:T(8,128)(2,1)S(1)}, u32[]{:S(2)}, u32[]{:S(2)}) collective-permute-start(bf16[64,5120]{1,0:T(8,128)(2,1)S(1)} %pad_maximum_fusion.refs_1_), channel_id=1, source_target_pairs={{0,1},{1,2},{2,3},{3,0},{4,5},{5,6},{6,7},{7,4},{8,9},{9,10},{10,1... | collective-permute-start | bytes 1966088 | tf_op jit(solution)/shard_map/ppermute | solution.py:37
  46.4 17.0 %collective-permute-start.6 = (bf16[64,5120]{1,0:T(8,128)(2,1)S(1)}, bf16[64,5120]{1,0:T(8,128)(2,1)S(1)}, u32[]{:S(2)}, u32[]{:S(2)}) collective-permute-start(bf16[64,5120]{1,0:T(8,128)(2,1)S(1)} %pad_maximum_fusion.refs_1_), channel_id=1, source_target_pairs={{0,3},{1,0},{2,1},{3,2},{4,7},{5,4},{6,5},{7,6},{8,11},{9,8},{10,9... | collective-permute-start | bytes 1966088 | tf_op jit(solution)/shard_map/ppermute | solution.py:37
  50.2 14.4 %collective-permute-start.14 = (bf16[32,5120]{1,0:T(8,128)(2,1)S(1)}, bf16[32,5120]{1,0:T(8,128)(2,1)S(1)}, u32[]{:S(2)}, u32[]{:S(2)}) collective-permute-start(bf16[32,5120]{1,0:T(8,128)(2,1)S(1)} %slice.98), channel_id=1, source_target_pairs={{0,8},{1,9},{2,10},{3,11},{4,12},{5,13},{6,14},{7,15},{8,16},{9,17... | collective-permute-start | bytes 983048 | tf_op jit(solution)/shard_map/ppermute | solution.py:37
  50.3 36.3 %collective-permute-start.21 = (bf16[128,2560]{1,0:T(8,128)(2,1)S(1)}, bf16[128,2560]{1,0:T(8,128)(2,1)S(1)}, u32[]{:S(2)}, u32[]{:S(2)}) collective-permute-start(bf16[128,2560]{1,0:T(8,128)(2,1)S(1)} %collective-permute-done.20), channel_id=1, source_target_pairs={{0,32},{1,33},{2,34},{3,35},{4,36},{5,37},{6,38},{7,39},{8,40},{9,... | collective-permute-start | bytes 1966088 | tf_op jit(solution)/shard_map/ppermute | solution.py:37
  52.4 16.0 %collective-permute-start.15 = (bf16[32,5120]{1,0:T(8,128)(2,1)}, bf16[32,5120]{1,0:T(8,128)(2,1)}, u32[]{:S(2)}, u32[]{:S(2)}) collective-permute-start(bf16[32,5120]{1,0:T(8,128)(2,1)} %slice.99), channel_id=1, source_target_pairs={{0,24},{1,25},{2,26},{3,27},{4,28},{5,29},{6,30},{7,31},{8,0},{9,1... | collective-permute-start | bytes 983048 | tf_op jit(solution)/shard_map/ppermute | solution.py:37
  63.4 10.1 %collective-permute-start.7 = (bf16[32,5120]{1,0:T(8,128)(2,1)}, bf16[32,5120]{1,0:T(8,128)(2,1)}, u32[]{:S(2)}, u32[]{:S(2)}) collective-permute-start(bf16[32,5120]{1,0:T(8,128)(2,1)} %slice.95), channel_id=1, source_target_pairs={{0,1},{1,2},{2,3},{3,0},{4,5},{5,6},{6,7},{7,4},{8,9},{9,10},{10,1... | collective-permute-start | bytes 983048 | tf_op jit(solution)/shard_map/ppermute | solution.py:37
  68.4 85.5 %collective-permute-start = (f32[32,5120]{1,0:T(8,128)S(1)}, f32[32,5120]{1,0:T(8,128)S(1)}, u32[]{:S(2)}, u32[]{:S(2)}) collective-permute-start(f32[32,5120]{1,0:T(8,128)S(1)} %bitcast.11), channel_id=1, source_target_pairs={{0,32},{1,33},{2,34},{3,35},{4,36},{5,37},{6,38},{7,39},{8,40},{9,... | collective-permute-start | bytes 1966088 | tf_op jit(solution)/shard_map/ppermute | solution.py:37
  85.9 10.3 %collective-permute-start.19 = (bf16[512,256]{1,0:T(8,128)(2,1)}, bf16[512,256]{1,0:T(8,128)(2,1)S(1)}, u32[]{:S(2)}, u32[]{:S(2)}) collective-permute-start(bf16[512,256]{1,0:T(8,128)(2,1)} %get-tuple-element.20.values), channel_id=1, source_target_pairs={{0,4},{1,5},{2,6},{3,7},{4,0},{5,1},{6,2},{7,3},{8,12},{9,13},{10,... | collective-permute-start | bytes 786440 | tf_op jit(solution)/shard_map/ppermute | solution.py:37
  115.2 13.2 %collective-permute-start.23 = (bf16[64,5120]{1,0:T(8,128)(2,1)S(1)}, bf16[64,5120]{1,0:T(8,128)(2,1)S(1)}, u32[]{:S(2)}, u32[]{:S(2)}) collective-permute-start(bf16[64,5120]{1,0:T(8,128)(2,1)S(1)} %pad_maximum_fusion.2), channel_id=1, source_target_pairs={{0,1},{1,2},{2,3},{3,0},{4,5},{5,6},{6,7},{7,4},{8,9},{9,10},{10,1... | collective-permute-start | bytes 1966088 | tf_op jit(solution)/shard_map/ppermute | solution.py:37
  116.2 13.0 %collective-permute-start.25 = (bf16[64,5120]{1,0:T(8,128)(2,1)S(1)}, bf16[64,5120]{1,0:T(8,128)(2,1)S(1)}, u32[]{:S(2)}, u32[]{:S(2)}) collective-permute-start(bf16[64,5120]{1,0:T(8,128)(2,1)S(1)} %pad_maximum_fusion.3), channel_id=1, source_target_pairs={{0,3},{1,0},{2,1},{3,2},{4,7},{5,4},{6,5},{7,6},{8,11},{9,8},{10,9... | collective-permute-start | bytes 1966088 | tf_op jit(solution)/shard_map/ppermute | solution.py:37
  119.7 13.0 %collective-permute-start.30 = (bf16[64,5120]{1,0:T(8,128)(2,1)S(1)}, bf16[64,5120]{1,0:T(8,128)(2,1)S(1)}, u32[]{:S(2)}, u32[]{:S(2)}) collective-permute-start(bf16[64,5120]{1,0:T(8,128)(2,1)S(1)} %pad_maximum_fusion.4), channel_id=1, source_target_pairs={{0,8},{1,9},{2,10},{3,11},{4,12},{5,13},{6,14},{7,15},{8,16},{9,17... | collective-permute-start | bytes 1966088 | tf_op jit(solution)/shard_map/ppermute | solution.py:37
  119.9 13.4 %collective-permute-start.32 = (bf16[64,5120]{1,0:T(8,128)(2,1)S(1)}, bf16[64,5120]{1,0:T(8,128)(2,1)S(1)}, u32[]{:S(2)}, u32[]{:S(2)}) collective-permute-start(bf16[64,5120]{1,0:T(8,128)(2,1)S(1)} %pad_maximum_fusion.5), channel_id=1, source_target_pairs={{0,24},{1,25},{2,26},{3,27},{4,28},{5,29},{6,30},{7,31},{8,0},{9,1... | collective-permute-start | bytes 1966088 | tf_op jit(solution)/shard_map/ppermute | solution.py:37
  129.7 10.1 %collective-permute-start.27 = (bf16[16,5120]{1,0:T(8,128)(2,1)S(1)}, bf16[16,5120]{1,0:T(8,128)(2,1)S(1)}, u32[]{:S(2)}, u32[]{:S(2)}) collective-permute-start(bf16[16,5120]{1,0:T(8,128)(2,1)S(1)} %get-tuple-element.37), channel_id=1, source_target_pairs={{0,24},{1,25},{2,26},{3,27},{4,28},{5,29},{6,30},{7,31},{8,0},{9,1... | collective-permute-start | bytes 491528 | tf_op jit(solution)/shard_map/ppermute | solution.py:37
  153.9 19.7 %collective-permute-start.1 = (f32[32,5120]{1,0:T(8,128)S(1)}, f32[32,5120]{1,0:T(8,128)S(1)}, u32[]{:S(2)}, u32[]{:S(2)}) collective-permute-start(f32[32,5120]{1,0:T(8,128)S(1)} %broadcast_select_fusion), channel_id=1, source_target_pairs={{0,64},{1,65},{2,66},{3,67},{4,68},{5,69},{6,70},{7,71},{8,72},{9,... | collective-permute-start | bytes 1966088 | tf_op jit(solution)/shard_map/ppermute | solution.py:37
  156.6 24.2 %collective-permute-start.37 = (bf16[32,5120]{1,0:T(8,128)(2,1)}, bf16[32,5120]{1,0:T(8,128)(2,1)}, u32[]{:S(2)}, u32[]{:S(2)}) collective-permute-start(bf16[32,5120]{1,0:T(8,128)(2,1)} %fusion), channel_id=1, source_target_pairs={{0,64},{1,65},{2,66},{3,67},{4,68},{5,69},{6,70},{7,71},{8,72},{9,... | collective-permute-start | bytes 983048 | tf_op jit(solution)/shard_map/ppermute | solution.py:37
  (35 other events, 462.4 us)

commit v2 on v1

v2 whole, which is shorter than its diff:
```python
import functools
import math

import jax
import jax.numpy as jnp
from jax import lax
from jax.experimental import pallas as pl
from jax.experimental.pallas import tpu as pltpu
from jax.sharding import PartitionSpec as P

HDIM = 128
XS, YLS, ZS = 4, 2, 4
BF16, F32 = jnp.bfloat16, jnp.float32
VMEM = pl.BlockSpec(memory_space=pltpu.VMEM)
SMEM = pl.BlockSpec(memory_space=pltpu.SMEM)
ANY = pl.BlockSpec(memory_space=pl.ANY)
PARAMS = pltpu.CompilerParams(vmem_limit_bytes=24 * 1024 * 1024)


def moves(rule):
    pairs = []
    for yh in range(2):
        for core in range(2):
            for x in range(XS):
                for yl in range(YLS):
                    for z in range(ZS):
                        to = rule(yh, core, x, yl, z)
                        if to is not None:
                            pairs.append((flat(yh, core, x, yl, z), flat(*to)))
    return pairs


def flat(yh, core, x, yl, z):
    return (((yh * 2 + core) * XS + x) * YLS + yl) * ZS + z


def send(value, rule):
    return lax.ppermute(value, ("tm", "seq"), moves(rule))


def first_axis(step):
    return lambda yh, core, x, yl, z: (
        (yh, core, (x + step) % XS, yl, z) if core == 0 else (yh, core, x, yl, (z + step) % ZS)
    )


def second_axis(step):
    return lambda yh, core, x, yl, z: (
        (yh, core, x, yl, (z + step) % ZS) if core == 0 else (yh, core, (x + step) % XS, yl, z)
    )


def to_other_core(yh, core, x, yl, z):
    return (yh, 1 - core, x, yl, z)


def to_partner(yh, core, x, yl, z):
    return (yh, core, x, 1 - yl, z)


def to_both_sides(yh, core, x, yl, z):
    return (yh if core == 0 else 1 - yh, core, x, 1 - yl, z)


def to_later_half(yh, core, x, yl, z):
    return (1, core, x, yl, z) if yh == 0 else None


def to_later_half_other_core(yh, core, x, yl, z):
    return (1, 1 - core, x, yl, z) if yh == 0 else None


def to_later_core(yh, core, x, yl, z):
    return (yh, 1, x, yl, z) if core == 0 else None


def modulate_kernel(index, state, scale, shift, out):
    row = index[0]
    value = state[...]
    mean = jnp.mean(value * value, axis=-1, keepdims=True)
    normed = value * lax.rsqrt(mean + 1e-06)
    out[...] = (normed * (1.0 + scale[pl.ds(row, 1), :]) + shift[pl.ds(row, 1), :]).astype(BF16)


def modulate(index, state, scale, shift):
    return pl.pallas_call(
        modulate_kernel,
        out_shape=jax.ShapeDtypeStruct(state.shape, BF16),
        in_specs=[SMEM, VMEM, VMEM, VMEM],
        out_specs=VMEM,
        compiler_params=PARAMS,
    )(index, state, scale, shift)


def project_kernel(count, chunk, *refs):
    core_ref, pieces, (own, mine, theirs), (queries, both_kv), total = (
        refs[0],
        refs[1 : 1 + count],
        refs[1 + count : 4 + count],
        refs[4 + count : 6 + count],
        refs[-1],
    )
    depth = own.shape[1]
    half = depth // 2
    wide = 2 * HDIM
    first = core_ref[0] * half
    total[...] = jnp.zeros_like(total)

    def side(weight, start):
        def one(step, carry):
            at = pl.multiple_of(step * chunk, chunk)
            column = pl.multiple_of(start + at, 128)
            rows = jnp.concatenate([piece[:, pl.ds(column, chunk)] for piece in pieces], axis=0)
            for kind in range(3):
                both = jnp.concatenate(
                    [own[kind, pl.ds(column, chunk), :], weight[kind, pl.ds(at, chunk), :]], axis=-1
                )
                total[kind] += jnp.dot(rows, both, preferred_element_type=F32)
            return carry

        lax.fori_loop(0, half // chunk, one, 0)

    side(mine, first)
    side(theirs, half - first)
    queries[...] = total[0].astype(BF16)
    both_kv[:, :wide] = total[1].astype(BF16)
    both_kv[:, wide:] = total[2].astype(BF16)


def project(core, pieces, own, mine, theirs):
    tokens = sum(piece.shape[0] for piece in pieces)
    wide = 2 * HDIM
    return pl.pallas_call(
        functools.partial(project_kernel, len(pieces), 512),
        out_shape=[
            jax.ShapeDtypeStruct((tokens, wide), BF16),
            jax.ShapeDtypeStruct((tokens, 2 * wide), BF16),
        ],
        in_specs=[SMEM] + [VMEM] * (len(pieces) + 3),
        out_specs=[VMEM] * 2,
        scratch_shapes=[pltpu.VMEM((3, tokens, wide), F32)],
        compiler_params=PARAMS,
    )(core, *pieces, own, mine, theirs)


def attend_kernel(count, cuts, core_ref, queries, own, mine, theirs, *refs):
    near, far, outs, attended = refs[:count], refs[count : 2 * count], refs[2 * count : -1], refs[-1]
    scale = 1.0 / math.sqrt(HDIM)
    contract = (((1,), (1,)), ((), ()))
    for head in range(2):
        here = slice(head * HDIM, (head + 1) * HDIM)
        there = slice((1 - head) * HDIM, (2 - head) * HDIM)
        here_v = slice((2 + head) * HDIM, (3 + head) * HDIM)
        there_v = slice((3 - head) * HDIM, (4 - head) * HDIM)
        all_keys = jnp.concatenate([r[:, here] for r in near] + [r[:, there] for r in far], axis=0)
        all_values = jnp.concatenate(
            [r[:, here_v] for r in near] + [r[:, there_v] for r in far], axis=0
        )
        scores = lax.dot_general(queries[:, here], all_keys, contract, preferred_element_type=F32)
        top = jnp.max(scores, axis=-1, keepdims=True)
        weights = jnp.exp((scores - top) * scale)
        total = jnp.sum(weights, axis=-1, keepdims=True)
        mixed = jnp.dot(weights.astype(BF16), all_values, preferred_element_type=F32)
        attended[:, here] = (mixed / total).astype(BF16)
    half = own.shape[1] // 2
    step = 512
    first = core_ref[0] * half

    def side(weight, start):
        def one(block, carry):
            at = pl.multiple_of(block * step, step)
            column = pl.ds(pl.multiple_of(start + at, 128), step)
            both = jnp.concatenate([own[:, column], weight[:, pl.ds(at, step)]], axis=0)
            result = jnp.dot(attended[...], both, preferred_element_type=F32).astype(BF16)
            row = 0
            for out, size in zip(outs, cuts):
                out[:, column] = result[row : row + size]
                row += size
            return carry

        lax.fori_loop(0, half // step, one, 0)

    side(mine, first)
    side(theirs, half - first)


def attend(core, queries, near, far, own, mine, theirs, cuts):
    width = own.shape[1]
    return pl.pallas_call(
        functools.partial(attend_kernel, len(near), cuts),
        out_shape=[jax.ShapeDtypeStruct((size, width), BF16) for size in cuts],
        in_specs=[SMEM] + [VMEM] * (4 + 2 * len(near)),
        out_specs=[VMEM] * len(cuts),
        scratch_shapes=[pltpu.VMEM((queries.shape[0], 2 * HDIM), BF16)],
        compiler_params=PARAMS,
    )(core, queries, own, mine, theirs, *near, *far)


def join_kernel(before, after, low, high, unused, to_before, to_after):
    half = low.shape[0]
    to_after[:half] = (after[:half].astype(F32) + low[...].astype(F32)).astype(BF16)
    to_after[half:] = after[half:]
    to_before[:half] = before[:half]
    to_before[half:] = (before[half:].astype(F32) + high[...].astype(F32)).astype(BF16)


def join(before, after, low, high, start):
    return pl.pallas_call(
        join_kernel,
        out_shape=[jax.ShapeDtypeStruct(before.shape, BF16)] * 2,
        in_specs=[VMEM] * 4 + [ANY],
        out_specs=[VMEM] * 2,
        compiler_params=PARAMS,
    )(before, after, low, high, start)


def split_kernel(near, one, two, kept, *outs):
    size = kept.shape[0]
    for place in range(4):
        rows = slice(place * size, (place + 1) * size)
        total = near[rows].astype(F32) + one[rows].astype(F32) + two[rows].astype(F32)
        if place == 0:
            kept[...] = total
        else:
            outs[place - 1][...] = total.astype(BF16)


def split(near, one, two):
    size, width = near.shape[0] // 4, near.shape[1]
    return pl.pallas_call(
        split_kernel,
        out_shape=[jax.ShapeDtypeStruct((size, width), F32)]
        + [jax.ShapeDtypeStruct((size, width), BF16)] * 3,
        in_specs=[VMEM] * 3,
        out_specs=[VMEM] * 4,
        compiler_params=PARAMS,
    )(near, one, two)


def swap_weights(core, weight, axis):
    half = weight.shape[axis] // 2
    mine = send(lax.dynamic_slice_in_dim(weight, core * half, half, axis), to_both_sides)
    return mine, send(mine, to_other_core)


def on_device(
    trajectory, qkv_weight, out_weight, shift_table, scale_table, gate_table, step_sizes, window_start
):
    group = lax.axis_index("tm")
    core = group % 2
    index = window_start[0] + group
    state = trajectory[0]
    rows = state.shape[0]
    mine, theirs = swap_weights(core, qkv_weight, 1)
    out_mine, out_theirs = swap_weights(core, out_weight, 1)

    modulated = modulate(index[None], state, scale_table, shift_table)
    near = jnp.concatenate([modulated] + [send(modulated, first_axis(s)) for s in (1, -1, 2)], axis=0)
    half = near.shape[0] // 2
    before, after = send(near, second_axis(1)), send(near, second_axis(-1))
    low, high = send(before[:half], second_axis(1)), send(after[half:], second_axis(-1))

    place = core[None]
    weights = (qkv_weight, mine, theirs)
    near_q, near_kv = project(place, [near], *weights)
    side_q, side_kv = project(place, [before, after], *weights)
    last_q, last_kv = project(place, [low, high], *weights)
    kv = [near_kv, side_kv, last_kv]
    far = [send(value, to_partner) for value in kv]

    start = jnp.where(core == 0, state, send(state, to_later_core))
    start = jnp.where(group < 2, start, send(start, to_later_half))

    outs = (out_weight, out_mine, out_theirs)
    size = near.shape[0]
    last_low, last_high = attend(place, last_q, kv, far, *outs, [half, half])
    side_before, side_after = attend(place, side_q, kv, far, *outs, [size, size])
    (kept,) = attend(place, near_q, kv, far, *outs, [size])

    from_low, from_high = send(last_low, second_axis(1)), send(last_high, second_axis(-1))
    to_before, to_after = join(side_before, side_after, from_low, from_high, start)
    from_before, from_after = send(to_after, second_axis(1)), send(to_before, second_axis(-1))
    total, to_minus, to_plus, to_opposite = split(kept, from_before, from_after)
    for value, s in ((to_plus, 1), (to_minus, -1), (to_opposite, 2)):
        total = total + send(value, first_axis(s)).astype(F32)

    gates = lax.dynamic_slice_in_dim(gate_table, index, 1, 0)
    step = lax.dynamic_slice_in_dim(step_sizes, index, 1, 0)[0]
    drift = step * (gates * total)
    term = drift.astype(BF16)
    summed = drift
    for rule in (to_later_half, to_later_half_other_core, to_later_core):
        summed = summed + send(term, rule).astype(F32)
    return (start + summed)[None]


def solution(mesh):
    in_specs = (P("tm", "seq", None), P(None, None, "seq"), P("seq", None), P(), P(), P(), P(), P())
    out_specs = P("tm", "seq", None)
    return jax.shard_map(
        on_device, mesh=mesh, in_specs=in_specs, out_specs=out_specs, check_vma=False
    )
```

time: 184 us -> 152 us (0.83)
  waiting for transfers between devices: 83.1 us -> 57.9 us
  starting transfers between devices: 57.4 us -> 35.8 us
  Pallas kernels: 23.8 us -> 34.9 us
  local copies, waits for them, and re-layouts: 10.6 us -> 14.2 us
    ppermute x38 -> x26, waiting for transfers between devices: 83.1 us -> 57.9 us  [send(): return lax.ppermute(value, ('tm', 'seq'), moves(rule))]
    ppermute x38 -> x26, starting transfers between devices: 57.4 us -> 35.8 us  [send(): return lax.ppermute(value, ('tm', 'seq'), moves(rule))]
    pallas_call x1 -> x5, Pallas kernels: 9.39 us -> 17.3 us  [the longest x3 13.4 us: attend(): pl.pallas_call(functools.partial(attend_kernel, len(near), cuts), out_sha...]
    unnamed x42 -> x32, local copies, waits for them, and re-layouts: 1.37 us -> 7.12 us
    pallas_call x1 -> x3, Pallas kernels: 11.6 us -> 16.2 us  [project(): pl.pallas_call(functools.partial(project_kernel, len(pieces), 512), out_s...]
    slice x11 -> x2, local copies, waits for them, and re-layouts: 5.56 us -> 2.41 us  [the longest x1 1.28 us: on_device(): before[:half]]
    select_n x1, other arithmetic: 0.07 us -> 2.19 us  [on_device(): start = jnp.where(core == 0, state, send(state, to_later_core))]
  transfers between devices with their start and end apart: 38 -> 26, of which waited for: 18 -> 13; matrix products, arithmetic and copies ran while one was open for 6% -> 6% of each run, Pallas kernels for 13% -> 21%
where the time goes in v2:
time: 152 us; the launch traced here: 151 us
  waiting for transfers between devices  57.9 us (38%)
  starting transfers between devices  35.8 us (24%)
  Pallas kernels  34.9 us (23%)
  local copies, waits for them, and re-layouts  14.2 us (9%)
  other arithmetic  7.13 us (5%)
    ppermute x26, waiting for transfers between devices, send(): return lax.ppermute(value, ('tm', 'seq'), moves(rule))  57.9 us
    ppermute x26, starting transfers between devices, send(): return lax.ppermute(value, ('tm', 'seq'), moves(rule))  35.8 us
    pallas_call x3, Pallas kernels, project(): pl.pallas_call(functools.partial(project_kernel, len(pieces), 512), out_s...  16.2 us
    pallas_call x3, Pallas kernels, attend(): pl.pallas_call(functools.partial(attend_kernel, len(near), cuts), out_sha...  13.4 us
    unnamed x32, local copies, waits for them, and re-layouts  7.12 us
    dynamic_slice x2, local copies, waits for them, and re-layouts, swap_weights(): lax.dynamic_slice_in_dim(weight, core * half, half, axis)  3.96 us
  transfers between devices with their start and end apart: 26, of which 13 were waited for; matrix products, arithmetic and copies ran while one was open for 6% of the time, Pallas kernels for 21%

profile of v2, /device:TPU:17, one launch (start us, length us, event | category | flops | bytes accessed | tf_op | source)
XLA Modules:
  0.0 150.8 jit_solution(8787350885250310557)
XLA Ops:
  0.0 3.1 %constant_dynamic-slice_fusion.1 = bf16[3,2560,128]{2,1,0:T(8,128)(2,1)} fusion(bf16[3,5120,128]{2,1,0:T(8,128)(2,1)} %refs_3_.3, s32[]{:T(128)S(6)} %select_n.35), kind=kLoop, calls=%fused_computation.6 | loop fusion | bytes 3932164 | tf_op jit(solution)/shard_map/dynamic_slice | solution.py:242
  9.5 2.2 %collective-permute-start.3 = (bf16[32,5120]{1,0:T(8,128)(2,1)S(1)}, bf16[32,5120]{1,0:T(8,128)(2,1)S(1)}, u32[]{:S(2)}, u32[]{:S(2)}) collective-permute-start(bf16[32,5120]{1,0:T(8,128)(2,1)S(1)} %shard_map.82), channel_id=1, source_target_pairs={{0,24},{1,25},{2,26},{3,27},{4,28},{5,29},{6,30},{7,31},{8,0},{9,1... | collective-permute-start | bytes 983048 | tf_op jit(solution)/shard_map/ppermute | solution.py:38
  12.9 3.5 %collective-permute-done.2 = bf16[32,5120]{1,0:T(8,128)(2,1)S(1)} collective-permute-done((bf16[32,5120]{1,0:T(8,128)(2,1)S(1)}, bf16[32,5120]{1,0:T(8,128)(2,1)S(1)}, u32[]{:S(2)}, u32[]{:S(2)}) %collective-permute-start.2) | collective-permute-done | bytes 327712 | tf_op jit(solution)/shard_map/ppermute | solution.py:38
  16.4 2.9 %collective-permute-done.3 = bf16[32,5120]{1,0:T(8,128)(2,1)S(1)} collective-permute-done((bf16[32,5120]{1,0:T(8,128)(2,1)S(1)}, bf16[32,5120]{1,0:T(8,128)(2,1)S(1)}, u32[]{:S(2)}, u32[]{:S(2)}) %collective-permute-start.3) | collective-permute-done | bytes 327712 | tf_op jit(solution)/shard_map/ppermute | solution.py:38
  28.1 3.4 %collective-permute-start.6 = (bf16[3,2560,128]{2,1,0:T(8,128)(2,1)S(1)}, bf16[3,2560,128]{2,1,0:T(8,128)(2,1)}, u32[]{:S(2)}, u32[]{:S(2)}) collective-permute-start(bf16[3,2560,128]{2,1,0:T(8,128)(2,1)S(1)} %collective-permute-done.5.refs_3_.refs_4_), channel_id=1, source_target_pairs={{0,32},{1,33},{2,34},{3,35},{4,36},{5,37},{6,38},{7,39},{8,40},{9,... | collective-permute-start | bytes 5898248 | tf_op jit(solution)/shard_map/ppermute | solution.py:38
  31.5 4.4 %collective-permute-done.7.mine = bf16[128,2560]{1,0:T(8,128)(2,1)} collective-permute-done((bf16[128,2560]{1,0:T(8,128)(2,1)}, bf16[128,2560]{1,0:T(8,128)(2,1)}, u32[]{:S(2)}, u32[]{:S(2)}) %collective-permute-start.7) | collective-permute-done | bytes 655392 | tf_op jit(solution)/shard_map/ppermute | solution.py:38
  35.8 3.6 %collective-permute-start.8 = (bf16[128,2560]{1,0:T(8,128)(2,1)}, bf16[128,2560]{1,0:T(8,128)(2,1)}, u32[]{:S(2)}, u32[]{:S(2)}) collective-permute-start(bf16[128,2560]{1,0:T(8,128)(2,1)} %collective-permute-done.7.mine), channel_id=1, source_target_pairs={{0,32},{1,33},{2,34},{3,35},{4,36},{5,37},{6,38},{7,39},{8,40},{9,... | collective-permute-start | bytes 1966088 | tf_op jit(solution)/shard_map/ppermute | solution.py:38
  43.1 2.7 %collective-permute-start.12 = (bf16[64,5120]{1,0:T(8,128)(2,1)S(1)}, bf16[64,5120]{1,0:T(8,128)(2,1)S(1)}, u32[]{:S(2)}, u32[]{:S(2)}) collective-permute-start(bf16[64,5120]{1,0:T(8,128)(2,1)S(1)} %slice.9), channel_id=1, source_target_pairs={{0,3},{1,0},{2,1},{3,2},{4,7},{5,4},{6,5},{7,6},{8,11},{9,8},{10,9... | collective-permute-start | bytes 1966088 | tf_op jit(solution)/shard_map/ppermute | solution.py:38
  45.8 2.2 %broadcast_select_fusion = f32[32,5120]{1,0:T(8,128)} fusion(f32[32,5120]{1,0:T(8,128)} %collective-permute-done, pred[]{:T(512)S(6)} %eq.5, f32[1,32,5120]{2,1,0:T(8,128)} %param.8), kind=kLoop, calls=%fused_computation.3 | loop fusion | flops 163840 | bytes 1966081 | tf_op jit(solution)/shard_map/jit(_where)/select_n | solution.py:271
  49.3 6.3 %shard_map.84 = (bf16[256,256]{1,0:T(8,128)(2,1)S(1)}, bf16[256,512]{1,0:T(8,128)(2,1)S(1)}) custom-call(s32[1]{0:T(128)} %bitcast.4.refs_0_.core_ref, bf16[128,5120]{1,0:T(8,128)(2,1)} %collective-permute-done.9.refs_1_, bf16[128,5120]{1,0:T(8,128)(2,1)} %collective-permute-done.10.refs_2_, bf16[3,5120,128]{2,1,0:T(8,128)(2,1)S(1)} %copy-done.1, ...), custom_call_target="tpu_custom_call" | custom-call | tf_op jit(solution)/shard_map/pallas_call | solution.py:133
  56.4 4.4 %shard_map.85 = (bf16[128,256]{1,0:T(8,128)(2,1)S(1)}, bf16[128,512]{1,0:T(8,128)(2,1)S(1)}) custom-call(s32[1]{0:T(128)} %bitcast.4.refs_0_.core_ref, bf16[64,5120]{1,0:T(8,128)(2,1)S(1)} %collective-permute-done.11.refs_1_, bf16[64,5120]{1,0:T(8,128)(2,1)S(1)} %collective-permute-done.12.refs_2_, bf16[3,5120,128]{2,1,0:T(8,128)(2,1)S(1)} %copy-done.1, ...), custom_call_target="tpu_custom_call" | custom-call | tf_op jit(solution)/shard_map/pallas_call | solution.py:133
  61.6 5.5 %shard_map.83 = (bf16[128,256]{1,0:T(8,128)(2,1)S(1)}, bf16[128,512]{1,0:T(8,128)(2,1)}) custom-call(s32[1]{0:T(128)} %bitcast.4.refs_0_.core_ref, bf16[128,5120]{1,0:T(8,128)(2,1)} %pad_maximum_fusion.refs_1_, bf16[3,5120,128]{2,1,0:T(8,128)(2,1)S(1)} %copy-done.1, bf16[3,2560,128]{2,1,0:T(8,128)(2,1)S(1)} %collective-permute-done.5.refs_3_.refs_4_, ...), custom_call_target="tpu_custom_call" | custom-call | tf_op jit(solution)/shard_map/pallas_call | solution.py:133
  68.6 3.6 %collective-permute-done.13.refs_3_ = bf16[128,512]{1,0:T(8,128)(2,1)S(1)} collective-permute-done((bf16[128,512]{1,0:T(8,128)(2,1)}, bf16[128,512]{1,0:T(8,128)(2,1)S(1)}, u32[]{:S(2)}, u32[]{:S(2)}) %collective-permute-start.13) | collective-permute-done | bytes 131104 | tf_op jit(solution)/shard_map/ppermute | solution.py:38
  74.4 4.2 %shard_map.88 = (bf16[64,5120]{1,0:T(8,128)(2,1)S(1)}, bf16[64,5120]{1,0:T(8,128)(2,1)S(1)}) custom-call(s32[1]{0:T(128)} %bitcast.4.refs_0_.core_ref, bf16[128,256]{1,0:T(8,128)(2,1)S(1)} %copy-done.12, bf16[128,5120]{1,0:T(8,128)(2,1)S(1)} %copy-done.3, bf16[128,2560]{1,0:T(8,128)(2,1)} %collective-permute-done.7.mine, ...), custom_call_target="tpu_custom_call" | custom-call | tf_op jit(solution)/shard_map/pallas_call | solution.py:189
  78.7 2.7 %collective-permute-start.17 = (bf16[64,5120]{1,0:T(8,128)(2,1)S(1)}, bf16[64,5120]{1,0:T(8,128)(2,1)S(1)}, u32[]{:S(2)}, u32[]{:S(2)}) collective-permute-start(bf16[64,5120]{1,0:T(8,128)(2,1)S(1)} %get-tuple-element.30), channel_id=1, source_target_pairs={{0,3},{1,0},{2,1},{3,2},{4,7},{5,4},{6,5},{7,6},{8,11},{9,8},{10,9... | collective-permute-start | bytes 1966088 | tf_op jit(solution)/shard_map/ppermute | solution.py:38
  82.6 4.9 %shard_map.87 = (bf16[128,5120]{1,0:T(8,128)(2,1)S(1)}, bf16[128,5120]{1,0:T(8,128)(2,1)S(1)}) custom-call(s32[1]{0:T(128)} %bitcast.4.refs_0_.core_ref, bf16[256,256]{1,0:T(8,128)(2,1)S(1)} %copy-done.10, bf16[128,5120]{1,0:T(8,128)(2,1)S(1)} %copy-done.3, bf16[128,2560]{1,0:T(8,128)(2,1)} %collective-permute-done.7.mine, ...), custom_call_target="tpu_custom_call" | custom-call | tf_op jit(solution)/shard_map/pallas_call | solution.py:189
  91.4 2.7 %collective-permute-start.19 = (bf16[128,5120]{1,0:T(8,128)(2,1)}, bf16[128,5120]{1,0:T(8,128)(2,1)}, u32[]{:S(2)}, u32[]{:S(2)}) collective-permute-start(bf16[128,5120]{1,0:T(8,128)(2,1)} %get-tuple-element.32), channel_id=1, source_target_pairs={{0,3},{1,0},{2,1},{3,2},{4,7},{5,4},{6,5},{7,6},{8,11},{9,8},{10,9... | collective-permute-start | bytes 3932168 | tf_op jit(solution)/shard_map/ppermute | solution.py:38
  96.5 4.2 %shard_map.86.near = bf16[128,5120]{1,0:T(8,128)(2,1)S(1)} custom-call(s32[1]{0:T(128)} %bitcast.4.refs_0_.core_ref, bf16[128,256]{1,0:T(8,128)(2,1)S(1)} %copy-done.14, bf16[128,5120]{1,0:T(8,128)(2,1)S(1)} %copy-done.4, bf16[128,2560]{1,0:T(8,128)(2,1)} %collective-permute-done.7.mine, bf16[128,2560]{1,0:T(8,128)(2,1)} %collective-permute-done.8.theirs, ...), custom_call_target="tpu_custom_call" | custom-call | tf_op jit(solution)/shard_map/pallas_call | solution.py:189
  100.7 9.0 %collective-permute-done.18.one = bf16[128,5120]{1,0:T(8,128)(2,1)} collective-permute-done((bf16[128,5120]{1,0:T(8,128)(2,1)}, bf16[128,5120]{1,0:T(8,128)(2,1)}, u32[]{:S(2)}, u32[]{:S(2)}) %collective-permute-start.18) | collective-permute-done | bytes 1310752 | tf_op jit(solution)/shard_map/ppermute | solution.py:38
  112.0 2.7 %collective-permute-start.21 = (bf16[32,5120]{1,0:T(8,128)(2,1)S(1)}, bf16[32,5120]{1,0:T(8,128)(2,1)S(1)}, u32[]{:S(2)}, u32[]{:S(2)}) collective-permute-start(bf16[32,5120]{1,0:T(8,128)(2,1)S(1)} %get-tuple-element.35), channel_id=1, source_target_pairs={{0,24},{1,25},{2,26},{3,27},{4,28},{5,29},{6,30},{7,31},{8,0},{9,1... | collective-permute-start | bytes 983048 | tf_op jit(solution)/shard_map/ppermute | solution.py:38
  114.7 4.4 %collective-permute-done.20 = bf16[32,5120]{1,0:T(8,128)(2,1)S(1)} collective-permute-done((bf16[32,5120]{1,0:T(8,128)(2,1)S(1)}, bf16[32,5120]{1,0:T(8,128)(2,1)S(1)}, u32[]{:S(2)}, u32[]{:S(2)}) %collective-permute-start.20) | collective-permute-done | bytes 327712 | tf_op jit(solution)/shard_map/ppermute | solution.py:38
  119.1 3.1 %collective-permute-done.21 = bf16[32,5120]{1,0:T(8,128)(2,1)S(1)} collective-permute-done((bf16[32,5120]{1,0:T(8,128)(2,1)S(1)}, bf16[32,5120]{1,0:T(8,128)(2,1)S(1)}, u32[]{:S(2)}, u32[]{:S(2)}) %collective-permute-start.21) | collective-permute-done | bytes 327712 | tf_op jit(solution)/shard_map/ppermute | solution.py:38
  128.5 6.7 %collective-permute-done.23 = bf16[32,5120]{1,0:T(8,128)(2,1)S(1)} collective-permute-done((bf16[32,5120]{1,0:T(8,128)(2,1)S(1)}, bf16[32,5120]{1,0:T(8,128)(2,1)S(1)}, u32[]{:S(2)}, u32[]{:S(2)}) %collective-permute-start.23) | collective-permute-done | bytes 327712 | tf_op jit(solution)/shard_map/ppermute | solution.py:38
  135.2 13.8 %collective-permute-done.24 = bf16[32,5120]{1,0:T(8,128)(2,1)S(1)} collective-permute-done((bf16[32,5120]{1,0:T(8,128)(2,1)S(1)}, bf16[32,5120]{1,0:T(8,128)(2,1)S(1)}, u32[]{:S(2)}, u32[]{:S(2)}) %collective-permute-start.24) | collective-permute-done | bytes 327712 | tf_op jit(solution)/shard_map/ppermute | solution.py:38
  (80 shorter events, 44.0 us)
Async XLA Ops:
  3.1 25.0 %collective-permute-start.5 = (bf16[3,2560,128]{2,1,0:T(8,128)(2,1)}, bf16[3,2560,128]{2,1,0:T(8,128)(2,1)S(1)}, u32[]{:S(2)}, u32[]{:S(2)}) collective-permute-start(bf16[3,2560,128]{2,1,0:T(8,128)(2,1)} %constant_dynamic-slice_fusion.1), channel_id=1, source_target_pairs={{0,4},{1,5},{2,6},{3,7},{4,0},{5,1},{6,2},{7,3},{8,12},{9,13},{10,... | collective-permute-start | bytes 5898248 | tf_op jit(solution)/shard_map/ppermute | solution.py:38
  7.8 8.6 %collective-permute-start.2 = (bf16[32,5120]{1,0:T(8,128)(2,1)S(1)}, bf16[32,5120]{1,0:T(8,128)(2,1)S(1)}, u32[]{:S(2)}, u32[]{:S(2)}) collective-permute-start(bf16[32,5120]{1,0:T(8,128)(2,1)S(1)} %shard_map.82), channel_id=1, source_target_pairs={{0,8},{1,9},{2,10},{3,11},{4,12},{5,13},{6,14},{7,15},{8,16},{9,17... | collective-permute-start | bytes 983048 | tf_op jit(solution)/shard_map/ppermute | solution.py:38
  9.5 9.7 %collective-permute-start.3 = (bf16[32,5120]{1,0:T(8,128)(2,1)S(1)}, bf16[32,5120]{1,0:T(8,128)(2,1)S(1)}, u32[]{:S(2)}, u32[]{:S(2)}) collective-permute-start(bf16[32,5120]{1,0:T(8,128)(2,1)S(1)} %shard_map.82), channel_id=1, source_target_pairs={{0,24},{1,25},{2,26},{3,27},{4,28},{5,29},{6,30},{7,31},{8,0},{9,1... | collective-permute-start | bytes 983048 | tf_op jit(solution)/shard_map/ppermute | solution.py:38
  11.7 9.4 %collective-permute-start.4 = (bf16[32,5120]{1,0:T(8,128)(2,1)S(1)}, bf16[32,5120]{1,0:T(8,128)(2,1)S(1)}, u32[]{:S(2)}, u32[]{:S(2)}) collective-permute-start(bf16[32,5120]{1,0:T(8,128)(2,1)S(1)} %shard_map.82), channel_id=1, source_target_pairs={{0,16},{1,17},{2,18},{3,19},{4,20},{5,21},{6,22},{7,23},{8,24},{9,... | collective-permute-start | bytes 983048 | tf_op jit(solution)/shard_map/ppermute | solution.py:38
  22.2 18.3 %collective-permute-start.9 = (bf16[128,5120]{1,0:T(8,128)(2,1)}, bf16[128,5120]{1,0:T(8,128)(2,1)}, u32[]{:S(2)}, u32[]{:S(2)}) collective-permute-start(bf16[128,5120]{1,0:T(8,128)(2,1)} %pad_maximum_fusion.refs_1_), channel_id=1, source_target_pairs={{0,1},{1,2},{2,3},{3,0},{4,5},{5,6},{6,7},{7,4},{8,9},{9,10},{10,1... | collective-permute-start | bytes 3932168 | tf_op jit(solution)/shard_map/ppermute | solution.py:38
  23.1 18.8 %collective-permute-start.10 = (bf16[128,5120]{1,0:T(8,128)(2,1)}, bf16[128,5120]{1,0:T(8,128)(2,1)}, u32[]{:S(2)}, u32[]{:S(2)}) collective-permute-start(bf16[128,5120]{1,0:T(8,128)(2,1)} %pad_maximum_fusion.refs_1_), channel_id=1, source_target_pairs={{0,3},{1,0},{2,1},{3,2},{4,7},{5,4},{6,5},{7,6},{8,11},{9,8},{10,9... | collective-permute-start | bytes 3932168 | tf_op jit(solution)/shard_map/ppermute | solution.py:38
  25.8 10.0 %collective-permute-start.7 = (bf16[128,2560]{1,0:T(8,128)(2,1)}, bf16[128,2560]{1,0:T(8,128)(2,1)}, u32[]{:S(2)}, u32[]{:S(2)}) collective-permute-start(bf16[128,2560]{1,0:T(8,128)(2,1)} %constant_dynamic-slice_fusion), channel_id=1, source_target_pairs={{0,4},{1,5},{2,6},{3,7},{4,0},{5,1},{6,2},{7,3},{8,12},{9,13},{10,... | collective-permute-start | bytes 1966088 | tf_op jit(solution)/shard_map/ppermute | solution.py:38
  26.8 19.0 %collective-permute-start = (f32[32,5120]{1,0:T(8,128)}, f32[32,5120]{1,0:T(8,128)}, u32[]{:S(2)}, u32[]{:S(2)}) collective-permute-start(f32[32,5120]{1,0:T(8,128)} %bitcast.state), channel_id=1, source_target_pairs={{0,32},{1,33},{2,34},{3,35},{4,36},{5,37},{6,38},{7,39},{8,40},{9,... | collective-permute-start | bytes 1966088 | tf_op jit(solution)/shard_map/ppermute | solution.py:38
  28.1 21.1 %collective-permute-start.6 = (bf16[3,2560,128]{2,1,0:T(8,128)(2,1)S(1)}, bf16[3,2560,128]{2,1,0:T(8,128)(2,1)}, u32[]{:S(2)}, u32[]{:S(2)}) collective-permute-start(bf16[3,2560,128]{2,1,0:T(8,128)(2,1)S(1)} %collective-permute-done.5.refs_3_.refs_4_), channel_id=1, source_target_pairs={{0,32},{1,33},{2,34},{3,35},{4,36},{5,37},{6,38},{7,39},{8,40},{9,... | collective-permute-start | bytes 5898248 | tf_op jit(solution)/shard_map/ppermute | solution.py:38
  35.8 32.8 %collective-permute-start.8 = (bf16[128,2560]{1,0:T(8,128)(2,1)}, bf16[128,2560]{1,0:T(8,128)(2,1)}, u32[]{:S(2)}, u32[]{:S(2)}) collective-permute-start(bf16[128,2560]{1,0:T(8,128)(2,1)} %collective-permute-done.7.mine), channel_id=1, source_target_pairs={{0,32},{1,33},{2,34},{3,35},{4,36},{5,37},{6,38},{7,39},{8,40},{9,... | collective-permute-start | bytes 1966088 | tf_op jit(solution)/shard_map/ppermute | solution.py:38
  41.8 14.6 %collective-permute-start.11 = (bf16[64,5120]{1,0:T(8,128)(2,1)S(1)}, bf16[64,5120]{1,0:T(8,128)(2,1)S(1)}, u32[]{:S(2)}, u32[]{:S(2)}) collective-permute-start(bf16[64,5120]{1,0:T(8,128)(2,1)S(1)} %slice.8), channel_id=1, source_target_pairs={{0,1},{1,2},{2,3},{3,0},{4,5},{5,6},{6,7},{7,4},{8,9},{9,10},{10,1... | collective-permute-start | bytes 1966088 | tf_op jit(solution)/shard_map/ppermute | solution.py:38
  43.1 13.4 %collective-permute-start.12 = (bf16[64,5120]{1,0:T(8,128)(2,1)S(1)}, bf16[64,5120]{1,0:T(8,128)(2,1)S(1)}, u32[]{:S(2)}, u32[]{:S(2)}) collective-permute-start(bf16[64,5120]{1,0:T(8,128)(2,1)S(1)} %slice.9), channel_id=1, source_target_pairs={{0,3},{1,0},{2,1},{3,2},{4,7},{5,4},{6,5},{7,6},{8,11},{9,8},{10,9... | collective-permute-start | bytes 1966088 | tf_op jit(solution)/shard_map/ppermute | solution.py:38
  47.9 33.4 %collective-permute-start.1 = (f32[32,5120]{1,0:T(8,128)}, f32[32,5120]{1,0:T(8,128)}, u32[]{:S(2)}, u32[]{:S(2)}) collective-permute-start(f32[32,5120]{1,0:T(8,128)} %broadcast_select_fusion), channel_id=1, source_target_pairs={{0,64},{1,65},{2,66},{3,67},{4,68},{5,69},{6,70},{7,71},{8,72},{9,... | collective-permute-start | bytes 1966088 | tf_op jit(solution)/shard_map/ppermute | solution.py:38
  55.5 16.7 %collective-permute-start.14 = (bf16[256,512]{1,0:T(8,128)(2,1)S(1)}, bf16[256,512]{1,0:T(8,128)(2,1)}, u32[]{:S(2)}, u32[]{:S(2)}) collective-permute-start(bf16[256,512]{1,0:T(8,128)(2,1)S(1)} %get-tuple-element.23.refs_1_), channel_id=1, source_target_pairs={{0,4},{1,5},{2,6},{3,7},{4,0},{5,1},{6,2},{7,3},{8,12},{9,13},{10,... | collective-permute-start | bytes 786440 | tf_op jit(solution)/shard_map/ppermute | solution.py:38
  60.9 7.7 %collective-permute-start.15 = (bf16[128,512]{1,0:T(8,128)(2,1)S(1)}, bf16[128,512]{1,0:T(8,128)(2,1)}, u32[]{:S(2)}, u32[]{:S(2)}) collective-permute-start(bf16[128,512]{1,0:T(8,128)(2,1)S(1)} %get-tuple-element.24.refs_2_), channel_id=1, source_target_pairs={{0,4},{1,5},{2,6},{3,7},{4,0},{5,1},{6,2},{7,3},{8,12},{9,13},{10,... | collective-permute-start | bytes 393224 | tf_op jit(solution)/shard_map/ppermute | solution.py:38
  78.6 11.0 %collective-permute-start.16 = (bf16[64,5120]{1,0:T(8,128)(2,1)S(1)}, bf16[64,5120]{1,0:T(8,128)(2,1)S(1)}, u32[]{:S(2)}, u32[]{:S(2)}) collective-permute-start(bf16[64,5120]{1,0:T(8,128)(2,1)S(1)} %get-tuple-element.29), channel_id=1, source_target_pairs={{0,1},{1,2},{2,3},{3,0},{4,5},{5,6},{6,7},{7,4},{8,9},{9,10},{10,1... | collective-permute-start | bytes 1966088 | tf_op jit(solution)/shard_map/ppermute | solution.py:38
  78.7 10.9 %collective-permute-start.17 = (bf16[64,5120]{1,0:T(8,128)(2,1)S(1)}, bf16[64,5120]{1,0:T(8,128)(2,1)S(1)}, u32[]{:S(2)}, u32[]{:S(2)}) collective-permute-start(bf16[64,5120]{1,0:T(8,128)(2,1)S(1)} %get-tuple-element.30), channel_id=1, source_target_pairs={{0,3},{1,0},{2,1},{3,2},{4,7},{5,4},{6,5},{7,6},{8,11},{9,8},{10,9... | collective-permute-start | bytes 1966088 | tf_op jit(solution)/shard_map/ppermute | solution.py:38
  91.4 18.3 %collective-permute-start.18 = (bf16[128,5120]{1,0:T(8,128)(2,1)}, bf16[128,5120]{1,0:T(8,128)(2,1)}, u32[]{:S(2)}, u32[]{:S(2)}) collective-permute-start(bf16[128,5120]{1,0:T(8,128)(2,1)} %get-tuple-element.31), channel_id=1, source_target_pairs={{0,1},{1,2},{2,3},{3,0},{4,5},{5,6},{6,7},{7,4},{8,9},{9,10},{10,1... | collective-permute-start | bytes 3932168 | tf_op jit(solution)/shard_map/ppermute | solution.py:38
  91.4 18.3 %collective-permute-start.19 = (bf16[128,5120]{1,0:T(8,128)(2,1)}, bf16[128,5120]{1,0:T(8,128)(2,1)}, u32[]{:S(2)}, u32[]{:S(2)}) collective-permute-start(bf16[128,5120]{1,0:T(8,128)(2,1)} %get-tuple-element.32), channel_id=1, source_target_pairs={{0,3},{1,0},{2,1},{3,2},{4,7},{5,4},{6,5},{7,6},{8,11},{9,8},{10,9... | collective-permute-start | bytes 3932168 | tf_op jit(solution)/shard_map/ppermute | solution.py:38
  112.0 10.2 %collective-permute-start.21 = (bf16[32,5120]{1,0:T(8,128)(2,1)S(1)}, bf16[32,5120]{1,0:T(8,128)(2,1)S(1)}, u32[]{:S(2)}, u32[]{:S(2)}) collective-permute-start(bf16[32,5120]{1,0:T(8,128)(2,1)S(1)} %get-tuple-element.35), channel_id=1, source_target_pairs={{0,24},{1,25},{2,26},{3,27},{4,28},{5,29},{6,30},{7,31},{8,0},{9,1... | collective-permute-start | bytes 983048 | tf_op jit(solution)/shard_map/ppermute | solution.py:38
  114.6 9.2 %collective-permute-start.22 = (bf16[32,5120]{1,0:T(8,128)(2,1)S(1)}, bf16[32,5120]{1,0:T(8,128)(2,1)S(1)}, u32[]{:S(2)}, u32[]{:S(2)}) collective-permute-start(bf16[32,5120]{1,0:T(8,128)(2,1)S(1)} %get-tuple-element.36), channel_id=1, source_target_pairs={{0,16},{1,17},{2,18},{3,19},{4,20},{5,21},{6,22},{7,23},{8,24},{9,... | collective-permute-start | bytes 983048 | tf_op jit(solution)/shard_map/ppermute | solution.py:38
  124.6 10.6 %collective-permute-start.23 = (bf16[32,5120]{1,0:T(8,128)(2,1)S(1)}, bf16[32,5120]{1,0:T(8,128)(2,1)S(1)}, u32[]{:S(2)}, u32[]{:S(2)}) collective-permute-start(bf16[32,5120]{1,0:T(8,128)(2,1)S(1)} %fusion), channel_id=1, source_target_pairs={{0,64},{1,65},{2,66},{3,67},{4,68},{5,69},{6,70},{7,71},{8,72},{9,... | collective-permute-start | bytes 983048 | tf_op jit(solution)/shard_map/ppermute | solution.py:38
  125.9 23.1 %collective-permute-start.24 = (bf16[32,5120]{1,0:T(8,128)(2,1)S(1)}, bf16[32,5120]{1,0:T(8,128)(2,1)S(1)}, u32[]{:S(2)}, u32[]{:S(2)}) collective-permute-start(bf16[32,5120]{1,0:T(8,128)(2,1)S(1)} %fusion), channel_id=1, source_target_pairs={{0,96},{1,97},{2,98},{3,99},{4,100},{5,101},{6,102},{7,103},{8,104... | collective-permute-start | bytes 983048 | tf_op jit(solution)/shard_map/ppermute | solution.py:38
  127.2 21.8 %collective-permute-start.25 = (bf16[32,5120]{1,0:T(8,128)(2,1)S(1)}, bf16[32,5120]{1,0:T(8,128)(2,1)S(1)}, u32[]{:S(2)}, u32[]{:S(2)}) collective-permute-start(bf16[32,5120]{1,0:T(8,128)(2,1)S(1)} %fusion), channel_id=1, source_target_pairs={{0,32},{1,33},{2,34},{3,35},{4,36},{5,37},{6,38},{7,39},{8,40},{9,... | collective-permute-start | bytes 983048 | tf_op jit(solution)/shard_map/ppermute | solution.py:38
  (18 other events, 194.7 us)

commit v3 on v2

v3 whole, which is shorter than its diff:
```python
import functools
import math

import jax
import jax.numpy as jnp
from jax import lax
from jax.experimental import pallas as pl
from jax.experimental.pallas import tpu as pltpu
from jax.sharding import PartitionSpec as P

HDIM = 128
XS, YLS, ZS = 4, 2, 4
BF16, F32 = jnp.bfloat16, jnp.float32
VMEM = pl.BlockSpec(memory_space=pltpu.VMEM)
SMEM = pl.BlockSpec(memory_space=pltpu.SMEM)
ANY = pl.BlockSpec(memory_space=pl.ANY)
PARAMS = pltpu.CompilerParams(vmem_limit_bytes=24 * 1024 * 1024)


def moves(rule):
    pairs = []
    for yh in range(2):
        for core in range(2):
            for x in range(XS):
                for yl in range(YLS):
                    for z in range(ZS):
                        to = rule(yh, core, x, yl, z)
                        if to is not None:
                            pairs.append((flat(yh, core, x, yl, z), flat(*to)))
    return pairs


def flat(yh, core, x, yl, z):
    return (((yh * 2 + core) * XS + x) * YLS + yl) * ZS + z


def send(value, rule):
    return lax.ppermute(value, ("tm", "seq"), moves(rule))


def first_axis(step):
    return lambda yh, core, x, yl, z: (
        (yh, core, (x + step) % XS, yl, z) if core == 0 else (yh, core, x, yl, (z + step) % ZS)
    )


def second_axis(step):
    return lambda yh, core, x, yl, z: (
        (yh, core, x, yl, (z + step) % ZS) if core == 0 else (yh, core, (x + step) % XS, yl, z)
    )


def to_other_core(yh, core, x, yl, z):
    return (yh, 1 - core, x, yl, z)


def to_partner(yh, core, x, yl, z):
    return (yh, core, x, 1 - yl, z)


def to_both_sides(yh, core, x, yl, z):
    return (yh if core == 0 else 1 - yh, core, x, 1 - yl, z)


def to_later_half(yh, core, x, yl, z):
    return (1, core, x, yl, z) if yh == 0 else None


def to_later_half_other_core(yh, core, x, yl, z):
    return (1, 1 - core, x, yl, z) if yh == 0 else None


def to_later_core(yh, core, x, yl, z):
    return (yh, 1, x, yl, z) if core == 0 else None


def modulate_kernel(index, state, scale, shift, out):
    row = lax.rem(index[0], 8)
    value = state[...]
    mean = jnp.mean(value * value, axis=-1, keepdims=True)
    normed = value * lax.rsqrt(mean + 1e-06)
    out[...] = (normed * (1.0 + scale[pl.ds(row, 1), :]) + shift[pl.ds(row, 1), :]).astype(BF16)


def modulate(index, state, scale, shift):
    rows, width = state.shape
    table = pl.BlockSpec((8, width), lambda i, index: (lax.div(index[0], 8), 0))
    whole = pl.BlockSpec((rows, width), lambda i, index: (0, 0))
    return pl.pallas_call(
        modulate_kernel,
        grid_spec=pltpu.PrefetchScalarGridSpec(
            num_scalar_prefetch=1, grid=(1,), in_specs=[whole, table, table], out_specs=whole
        ),
        out_shape=jax.ShapeDtypeStruct(state.shape, BF16),
        compiler_params=PARAMS,
        cost_estimate=pl.CostEstimate(flops=1000000, bytes_accessed=2000000, transcendentals=0),
    )(index, state, scale, shift)


def halves(block, steps):
    return (
        lambda k, core: lax.rem(k + core[0] * steps, 2 * steps),
        lambda k, core: jnp.minimum(k, steps - 1),
        lambda k, core: jnp.maximum(k - steps, 0),
    )


def project_kernel(count, kinds, steps, rows, core, *refs):
    pieces, own = refs[:count], refs[count : count + kinds]
    mine, theirs = refs[count + kinds : count + kinds + 2]
    outs, total = refs[count + kinds + 2 : -1], refs[-1]
    k = pl.program_id(0)
    left = jnp.concatenate([piece[...] for piece in pieces], axis=0)

    def add(other):
        for kind in range(kinds):
            both = jnp.concatenate([own[kind][0], other[kind]], axis=-1)
            part = jnp.dot(left, both, preferred_element_type=F32)

            @pl.when(k == 0)
            def _():
                total[kind] = part

            @pl.when(k > 0)
            def _():
                total[kind] += part

    pl.when(k < steps)(lambda: add(mine))
    pl.when(k >= steps)(lambda: add(theirs))

    @pl.when(k == 2 * steps - 1)
    def _():
        at = 0
        for out, size in zip(outs, rows):
            for kind in range(kinds):
                out[:, kind * 2 * HDIM : (kind + 1) * 2 * HDIM] = total[
                    kind, at : at + size
                ].astype(BF16)
            at += size


def project(core, pieces, weight, kinds, mine, theirs, rows):
    tokens = sum(rows)
    wide = 2 * HDIM
    depth = weight.shape[1]
    steps = 2
    block = depth // (2 * steps)
    place, near, later = halves(block, steps)
    in_specs = [
        pl.BlockSpec((piece.shape[0], block), lambda k, core: (0, place(k, core)))
        for piece in pieces
    ]
    in_specs += [
        pl.BlockSpec((1, block, HDIM), lambda k, core, kind=kind: (kind, place(k, core), 0))
        for kind in kinds
    ]
    in_specs += [
        pl.BlockSpec((len(kinds), block, HDIM), lambda k, core, at=at: (0, at(k, core), 0))
        for at in (near, later)
    ]
    return pl.pallas_call(
        functools.partial(project_kernel, len(pieces), len(kinds), steps, rows),
        grid_spec=pltpu.PrefetchScalarGridSpec(
            num_scalar_prefetch=1,
            grid=(2 * steps,),
            in_specs=in_specs,
            out_specs=[
                pl.BlockSpec((size, len(kinds) * wide), lambda k, core: (0, 0)) for size in rows
            ],
            scratch_shapes=[pltpu.VMEM((len(kinds), tokens, wide), F32)],
        ),
        out_shape=[jax.ShapeDtypeStruct((size, len(kinds) * wide), BF16) for size in rows],
        compiler_params=PARAMS,
        cost_estimate=pl.CostEstimate(
            flops=2 * tokens * depth * wide * len(kinds), bytes_accessed=10000000, transcendentals=0
        ),
    )(core, *pieces, *[weight] * len(kinds), mine, theirs)


def attend_kernel(count, steps, cuts, core, queries, *refs):
    near, far, refs = refs[:count], refs[count : 2 * count], refs[2 * count :]
    own, mine, theirs, outs, attended = refs[0], refs[1], refs[2], refs[-1 - len(cuts) : -1], refs[-1]
    k = pl.program_id(0)

    @pl.when(k == 0)
    def _():
        scale = 1.0 / math.sqrt(HDIM)
        contract = (((1,), (1,)), ((), ()))
        for head in range(2):
            here = slice(head * HDIM, (head + 1) * HDIM)
            there = slice((1 - head) * HDIM, (2 - head) * HDIM)
            here_v = slice((2 + head) * HDIM, (3 + head) * HDIM)
            there_v = slice((3 - head) * HDIM, (4 - head) * HDIM)
            all_keys = jnp.concatenate(
                [r[:, here] for r in near] + [r[:, there] for r in far], axis=0
            )
            all_values = jnp.concatenate(
                [r[:, here_v] for r in near] + [r[:, there_v] for r in far], axis=0
            )
            scores = lax.dot_general(
                queries[:, here], all_keys, contract, preferred_element_type=F32
            )
            top = jnp.max(scores, axis=-1, keepdims=True)
            weights = jnp.exp((scores - top) * scale)
            total = jnp.sum(weights, axis=-1, keepdims=True)
            mixed = jnp.dot(weights.astype(BF16), all_values, preferred_element_type=F32)
            attended[:, here] = (mixed / total).astype(BF16)

    def out(other):
        both = jnp.concatenate([own[...], other[...]], axis=0)
        result = jnp.dot(attended[...], both, preferred_element_type=F32).astype(BF16)
        row = 0
        for out, size in zip(outs, cuts):
            out[...] = result[row : row + size]
            row += size

    pl.when(k < steps)(lambda: out(mine))
    pl.when(k >= steps)(lambda: out(theirs))


def attend(core, queries, near, far, own, mine, theirs, cuts, passed=None):
    width = own.shape[1]
    tokens = queries.shape[0]
    steps = 2
    block = width // (2 * steps)
    place, first, later = halves(block, steps)
    in_specs = [
        pl.BlockSpec(value.shape, lambda k, core: (0, 0)) for value in (queries, *near, *far)
    ]
    in_specs += [
        pl.BlockSpec((HDIM, block), lambda k, core, at=at: (0, at(k, core)))
        for at in (place, first, later)
    ]
    out_specs = [pl.BlockSpec((size, block), lambda k, core: (0, place(k, core))) for size in cuts]
    out_shape = [jax.ShapeDtypeStruct((size, width), BF16) for size in cuts]
    extra, aliases = [], {}
    if passed is not None:
        aliases = {1 + len(in_specs): 0}
        in_specs, out_specs = in_specs + [ANY], [ANY] + out_specs
        out_shape = [jax.ShapeDtypeStruct(passed.shape, passed.dtype)] + out_shape
        extra = [passed]
    return pl.pallas_call(
        functools.partial(attend_kernel, len(near), steps, cuts),
        grid_spec=pltpu.PrefetchScalarGridSpec(
            num_scalar_prefetch=1,
            grid=(2 * steps,),
            in_specs=in_specs,
            out_specs=out_specs,
            scratch_shapes=[pltpu.VMEM((tokens, 2 * HDIM), BF16)],
        ),
        out_shape=out_shape,
        input_output_aliases=aliases,
        compiler_params=PARAMS,
        cost_estimate=pl.CostEstimate(
            flops=4 * tokens * HDIM * (width + 2048), bytes_accessed=8000000, transcendentals=0
        ),
    )(core, queries, *near, *far, own, mine, theirs, *extra)


def join_kernel(after, before, low, high, to_after, to_before):
    to_after[...] = (after[...].astype(F32) + low[...].astype(F32)).astype(BF16)
    to_before[...] = (before[...].astype(F32) + high[...].astype(F32)).astype(BF16)


def join(after, before, low, high):
    return pl.pallas_call(
        join_kernel,
        out_shape=[jax.ShapeDtypeStruct(before.shape, BF16)] * 2,
        in_specs=[VMEM] * 4,
        out_specs=[VMEM] * 2,
        compiler_params=PARAMS,
    )(after, before, low, high)


def split_kernel(near_low, near_high, low_1, low_2, high_1, high_2, kept, to_minus, to_plus, to_opposite):
    size = kept.shape[0]

    def total(near, one, two, rows):
        return near[rows].astype(F32) + one[rows].astype(F32) + two[rows].astype(F32)

    kept[...] = total(near_low, low_1, low_2, slice(0, size))
    to_minus[...] = total(near_low, low_1, low_2, slice(size, 2 * size)).astype(BF16)
    to_plus[...] = total(near_high, high_1, high_2, slice(0, size)).astype(BF16)
    to_opposite[...] = total(near_high, high_1, high_2, slice(size, 2 * size)).astype(BF16)


def split(*parts):
    size, width = parts[0].shape[0] // 2, parts[0].shape[1]
    return pl.pallas_call(
        split_kernel,
        out_shape=[jax.ShapeDtypeStruct((size, width), F32)]
        + [jax.ShapeDtypeStruct((size, width), BF16)] * 3,
        in_specs=[VMEM] * 6,
        out_specs=[VMEM] * 4,
        compiler_params=PARAMS,
    )(*parts)


def swap_weights(core, weight, axis):
    half = weight.shape[axis] // 2
    mine = send(lax.dynamic_slice_in_dim(weight, core * half, half, axis), to_both_sides)
    return mine, send(mine, to_other_core)


def on_device(
    trajectory, qkv_weight, out_weight, shift_table, scale_table, gate_table, step_sizes, window_start
):
    group = lax.axis_index("tm")
    core = group % 2
    index = window_start[0] + group
    state = trajectory[0]
    rows = state.shape[0]
    kv_mine, kv_theirs = swap_weights(core, qkv_weight[1:], 1)
    q_mine, q_theirs = swap_weights(core, qkv_weight[:1], 1)
    out_mine, out_theirs = swap_weights(core, out_weight, 1)

    modulated = modulate(index[None], state, scale_table, shift_table)
    minus, plus, opposite = [send(modulated, first_axis(s)) for s in (1, -1, 2)]
    near_low = jnp.concatenate([modulated, minus], axis=0)
    before_low, after_low = send(near_low, second_axis(1)), send(near_low, second_axis(-1))
    near_high = jnp.concatenate([plus, opposite], axis=0)
    after_high, before_high = send(near_high, second_axis(-1)), send(near_high, second_axis(1))
    last_low, last_high = send(before_low, second_axis(1)), send(after_high, second_axis(-1))

    place = core[None]
    size = near_low.shape[0]
    near = [near_low, near_high]
    side = [before_low, before_high, after_low, after_high]
    last = [last_low, last_high]
    kv = [
        project(place, pieces, qkv_weight, (1, 2), kv_mine, kv_theirs, [size * len(pieces)])[0]
        for pieces in (near, side, last)
    ]
    far = [send(value, to_partner) for value in kv]
    near_q, side_q, last_q = project(
        place,
        near + side + last,
        qkv_weight,
        (0,),
        q_mine,
        q_theirs,
        [2 * size, 4 * size, 2 * size],
    )

    start = jnp.where(core == 0, state, send(state, to_later_core))

    outs = (out_weight, out_mine, out_theirs)
    start, last_low, last_high = attend(place, last_q, kv, far, *outs, [size] * 2, start)
    from_low, from_high = send(last_low, second_axis(1)), send(last_high, second_axis(-1))
    start = jnp.where(group < 2, start, send(start, to_later_half))
    before_low, before_high, after_low, after_high = attend(
        place, side_q, kv, far, *outs, [size] * 4
    )
    high_1, low_2 = send(after_high, second_axis(1)), send(before_low, second_axis(-1))
    near_low, near_high = attend(place, near_q, kv, far, *outs, [size] * 2)
    after_low, before_high = join(after_low, before_high, from_low, from_high)
    low_1, high_2 = send(after_low, second_axis(1)), send(before_high, second_axis(-1))
    total, to_minus, to_plus, to_opposite = split(near_low, near_high, low_1, low_2, high_1, high_2)
    for value, s in ((to_plus, 1), (to_minus, -1), (to_opposite, 2)):
        total = total + send(value, first_axis(s)).astype(F32)

    gates = lax.dynamic_slice_in_dim(gate_table, index, 1, 0)
    step = lax.dynamic_slice_in_dim(step_sizes, index, 1, 0)[0]
    drift = step * (gates * total)
    term = drift.astype(BF16)
    summed = drift
    for rule in (to_later_half, to_later_half_other_core, to_later_core):
        summed = summed + send(term, rule).astype(F32)
    return (start + summed)[None]


def solution(mesh):
    in_specs = (P("tm", "seq", None), P(None, None, "seq"), P("seq", None), P(), P(), P(), P(), P())
    out_specs = P("tm", "seq", None)
    return jax.shard_map(
        on_device, mesh=mesh, in_specs=in_specs, out_specs=out_specs, check_vma=False
    )
```

time: 152 us -> 160 us (1.053)
  local copies, waits for them, and re-layouts: 14.2 us -> 19.8 us
  starting transfers between devices: 35.8 us -> 40.8 us
  waiting for transfers between devices: 57.9 us -> 56.2 us
    unnamed x32 -> x63, local copies, waits for them, and re-layouts: 7.12 us -> 13.2 us
    ppermute x26 -> x32, starting transfers between devices: 35.8 us -> 40.8 us  [send(): return lax.ppermute(value, ('tm', 'seq'), moves(rule))]
    dynamic_slice x2 -> x3, local copies, waits for them, and re-layouts: 3.96 us -> 1.49 us  [swap_weights(): lax.dynamic_slice_in_dim(weight, core * half, half, axis)]
    slice x2 -> x3, local copies, waits for them, and re-layouts: 2.41 us -> 4.44 us  [the longest x1 3.37 us: on_device(): kv_mine, kv_theirs = swap_weights(core, qkv_weight[1:], 1)]
    ppermute x26 -> x32, waiting for transfers between devices: 57.9 us -> 56.2 us  [send(): return lax.ppermute(value, ('tm', 'seq'), moves(rule))]
    pallas_call x7 -> x8, Pallas kernels: 30.9 us -> 30.1 us  [the longest x4 19.6 us: project(): pl.pallas_call(functools.partial(project_kernel, len(pieces), len(kinds),...]
  transfers between devices with their start and end apart: 26 -> 32, of which waited for: 13 -> 14; matrix products, arithmetic and copies ran while one was open for 6% -> 6% of each run, Pallas kernels for 21% -> 17%
where the time goes in v3:
time: 160 us; the launch traced here: 159 us
  waiting for transfers between devices  56.2 us (35%)
  starting transfers between devices  40.8 us (25%)
  Pallas kernels  33.6 us (21%)
  local copies, waits for them, and re-layouts  19.8 us (12%)
  other arithmetic  7.13 us (4%)
    ppermute x32, waiting for transfers between devices, send(): return lax.ppermute(value, ('tm', 'seq'), moves(rule))  56.2 us
    ppermute x32, starting transfers between devices, send(): return lax.ppermute(value, ('tm', 'seq'), moves(rule))  40.8 us
    pallas_call x4, Pallas kernels, project(): pl.pallas_call(functools.partial(project_kernel, len(pieces), len(kinds),...  19.6 us
    unnamed x63, local copies, waits for them, and re-layouts  13.2 us
    pallas_call x3, Pallas kernels, attend(): pl.pallas_call(functools.partial(attend_kernel, len(near), steps, cuts),...  9.18 us
    slice x1, local copies, waits for them, and re-layouts, on_device(): kv_mine, kv_theirs = swap_weights(core, qkv_weight[1:], 1)  3.37 us
    broadcast_in_dim x1, other arithmetic, on_device(): return (start + summed)[None]  3.21 us
  transfers between devices with their start and end apart: 32, of which 14 were waited for; matrix products, arithmetic and copies ran while one was open for 6% of the time, Pallas kernels for 17%

profile of v3, /device:TPU:17, one launch (start us, length us, event | category | flops | bytes accessed | tf_op | source)
XLA Modules:
  0.0 158.6 jit_solution(13302896880602955425)
XLA Ops:
  4.6 3.8 %collective-permute-start.1 = (bf16[32,5120]{1,0:T(8,128)(2,1)S(1)}, bf16[32,5120]{1,0:T(8,128)(2,1)S(1)}, u32[]{:S(2)}, u32[]{:S(2)}) collective-permute-start(bf16[32,5120]{1,0:T(8,128)(2,1)S(1)} %shard_map.82), channel_id=1, source_target_pairs={{0,24},{1,25},{2,26},{3,27},{4,28},{5,29},{6,30},{7,31},{8,0},{9,1... | collective-permute-start | bytes 983048 | tf_op jit(solution)/shard_map/ppermute | solution.py:38
  9.2 3.4 %slice.7 = bf16[2,5120,128]{2,1,0:T(8,128)(2,1)} slice(bf16[3,5120,128]{2,1,0:T(8,128)(2,1)} %refs_3_.3), slice={[1:3], [0:5120], [0:128]} | slice | bytes 5242880 | tf_op jit(solution)/shard_map/slice | solution.py:313
  17.1 2.5 %collective-permute-start.6 = (bf16[64,5120]{1,0:T(8,128)(2,1)S(1)}, bf16[64,5120]{1,0:T(8,128)(2,1)}, u32[]{:S(2)}, u32[]{:S(2)}) collective-permute-start(bf16[64,5120]{1,0:T(8,128)(2,1)S(1)} %constant_dynamic-update-slice_fusion.refs_1_), channel_id=1, source_target_pairs={{0,3},{1,0},{2,1},{3,2},{4,7},{5,4},{6,5},{7,6},{8,11},{9,8},{10,9... | collective-permute-start | bytes 1966088 | tf_op jit(solution)/shard_map/ppermute | solution.py:38
  19.6 11.3 %collective-permute-done.11.refs_4_.refs_6_ = bf16[2,2560,128]{2,1,0:T(8,128)(2,1)} collective-permute-done((bf16[2,2560,128]{2,1,0:T(8,128)(2,1)S(1)}, bf16[2,2560,128]{2,1,0:T(8,128)(2,1)}, u32[]{:S(2)}, u32[]{:S(2)}) %collective-permute-start.11) | collective-permute-done | bytes 1310752 | tf_op jit(solution)/shard_map/ppermute | solution.py:38
  35.0 2.8 %collective-permute-done.9.refs_9_ = bf16[1,2560,128]{2,1,0:T(8,128)(2,1)S(1)} collective-permute-done((bf16[1,2560,128]{2,1,0:T(8,128)(2,1)S(1)}, bf16[1,2560,128]{2,1,0:T(8,128)(2,1)S(1)}, u32[]{:S(2)}, u32[]{:S(2)}) %collective-permute-start.9) | collective-permute-done | bytes 655392 | tf_op jit(solution)/shard_map/ppermute | solution.py:38
  39.0 5.9 %collective-permute-done.16.refs_7_ = bf16[128,2560]{1,0:T(8,128)(2,1)S(1)} collective-permute-done((bf16[128,2560]{1,0:T(8,128)(2,1)S(1)}, bf16[128,2560]{1,0:T(8,128)(2,1)S(1)}, u32[]{:S(2)}, u32[]{:S(2)}) %collective-permute-start.16) | collective-permute-done | bytes 655392 | tf_op jit(solution)/shard_map/ppermute | solution.py:38
  44.9 2.5 %collective-permute-start.5 = (bf16[64,5120]{1,0:T(8,128)(2,1)S(1)}, bf16[64,5120]{1,0:T(8,128)(2,1)}, u32[]{:S(2)}, u32[]{:S(2)}) collective-permute-start(bf16[64,5120]{1,0:T(8,128)(2,1)S(1)} %pad_maximum_fusion.refs_0_), channel_id=1, source_target_pairs={{0,3},{1,0},{2,1},{3,2},{4,7},{5,4},{6,5},{7,6},{8,11},{9,8},{10,9... | collective-permute-start | bytes 1966088 | tf_op jit(solution)/shard_map/ppermute | solution.py:38
  48.9 2.6 %collective-permute-done.4.refs_3_.refs_1_ = bf16[64,5120]{1,0:T(8,128)(2,1)S(1)} collective-permute-done((bf16[64,5120]{1,0:T(8,128)(2,1)S(1)}, bf16[64,5120]{1,0:T(8,128)(2,1)S(1)}, u32[]{:S(2)}, u32[]{:S(2)}) %collective-permute-start.4) | collective-permute-done | bytes 655392 | tf_op jit(solution)/shard_map/ppermute | solution.py:38
  54.9 3.5 %collective-permute-start.10 = (bf16[1,2560,128]{2,1,0:T(8,128)(2,1)}, bf16[1,2560,128]{2,1,0:T(8,128)(2,1)S(1)}, u32[]{:S(2)}, u32[]{:S(2)}) collective-permute-start(bf16[1,2560,128]{2,1,0:T(8,128)(2,1)} %copy-done.26), channel_id=1, source_target_pairs={{0,32},{1,33},{2,34},{3,35},{4,36},{5,37},{6,38},{7,39},{8,40},{9,... | collective-permute-start | bytes 1966088 | tf_op jit(solution)/shard_map/ppermute | solution.py:38
  61.7 6.0 %shard_map.85.refs_1_ = bf16[256,512]{1,0:T(8,128)(2,1)S(1)} custom-call(s32[1]{0:T(128)} %bitcast.core, bf16[64,5120]{1,0:T(8,128)(2,1)} %collective-permute-done.3.refs_2_.refs_0_, bf16[64,5120]{1,0:T(8,128)(2,1)S(1)} %copy-done.14, bf16[64,5120]{1,0:T(8,128)(2,1)} %collective-permute-done.5.refs_4_.refs_2_, ...), custom_call_target="tpu_custom_call" | custom-call | flops 1342177280 | bytes 10000000 | tf_op jit(solution)/shard_map/pallas_call | solution.py:161
  68.8 4.5 %shard_map.86.refs_2_ = bf16[128,512]{1,0:T(8,128)(2,1)S(1)} custom-call(s32[1]{0:T(128)} %bitcast.core, bf16[64,5120]{1,0:T(8,128)(2,1)} %collective-permute-done.7.refs_6_.refs_0_, bf16[64,5120]{1,0:T(8,128)(2,1)} %collective-permute-done.8.refs_7_.refs_1_, bf16[3,5120,128]{2,1,0:T(8,128)(2,1)S(1)} %copy-done.1, bf16[3,5120,128]{2,1,0:T(8,128)(2,1)S(1)} %copy-done.1, ...), custom_call_target="tpu_custom_call" | custom-call | flops 671088640 | bytes 10000000 | tf_op jit(solution)/shard_map/pallas_call | solution.py:161
  73.8 4.1 %shard_map.84.refs_0_ = bf16[128,512]{1,0:T(8,128)(2,1)S(1)} custom-call(s32[1]{0:T(128)} %bitcast.core, bf16[64,5120]{1,0:T(8,128)(2,1)S(1)} %pad_maximum_fusion.refs_0_, bf16[64,5120]{1,0:T(8,128)(2,1)S(1)} %copy-done.12, bf16[3,5120,128]{2,1,0:T(8,128)(2,1)S(1)} %copy-done.1, bf16[3,5120,128]{2,1,0:T(8,128)(2,1)S(1)} %copy-done.1, ...), custom_call_target="tpu_custom_call" | custom-call | flops 671088640 | bytes 10000000 | tf_op jit(solution)/shard_map/pallas_call | solution.py:161
  80.7 4.9 %shard_map.83 = (bf16[128,256]{1,0:T(8,128)(2,1)S(1)}, bf16[256,256]{1,0:T(8,128)(2,1)S(1)}, bf16[128,256]{1,0:T(8,128)(2,1)S(1)}) custom-call(s32[1]{0:T(128)} %bitcast.core, bf16[64,5120]{1,0:T(8,128)(2,1)S(1)} %pad_maximum_fusion.refs_0_, bf16[64,5120]{1,0:T(8,128)(2,1)S(1)} %copy-done.12, bf16[64,5120]{1,0:T(8,128)(2,1)} %collective-permute-done.3.refs_2_.refs_0_, ...), custom_call_target="tpu_custom_call" | custom-call | flops 1342177280 | bytes 10000000 | tf_op jit(solution)/shard_map/pallas_call | solution.py:161
  85.8 2.5 %shard_map.87 = (f32[32,5120]{1,0:T(8,128)S(1)}, bf16[64,5120]{1,0:T(8,128)(2,1)S(1)}, bf16[64,5120]{1,0:T(8,128)(2,1)S(1)}) custom-call(s32[1]{0:T(128)} %bitcast.core, bf16[128,256]{1,0:T(8,128)(2,1)S(1)} %get-tuple-element.23.queries, bf16[128,512]{1,0:T(8,128)(2,1)S(1)} %shard_map.84.refs_0_, ...), custom_call_target="tpu_custom_call", output_to_operand_aliasing={{0}: (11, {})} | custom-call | flops 469762048 | bytes 8000000 | tf_op jit(solution)/shard_map/pallas_call | solution.py:242
  91.1 4.2 %shard_map.89 = (bf16[64,5120]{1,0:T(8,128)(2,1)}, bf16[64,5120]{1,0:T(8,128)(2,1)S(1)}, bf16[64,5120]{1,0:T(8,128)(2,1)S(1)}, bf16[64,5120]{1,0:T(8,128)(2,1)}) custom-call(s32[1]{0:T(128)} %bitcast.core, bf16[256,256]{1,0:T(8,128)(2,1)S(1)} %get-tuple-element.28.queries, bf16[128,512]{1,0:T(8,128)(2,1)S(1)} %shard_map.84.refs_0_, ...), custom_call_target="tpu_custom_call" | custom-call | flops 939524096 | bytes 8000000 | tf_op jit(solution)/shard_map/pallas_call | solution.py:242
  96.7 2.6 %collective-permute-done.20.low = bf16[64,5120]{1,0:T(8,128)(2,1)S(1)} collective-permute-done((bf16[64,5120]{1,0:T(8,128)(2,1)S(1)}, bf16[64,5120]{1,0:T(8,128)(2,1)S(1)}, u32[]{:S(2)}, u32[]{:S(2)}) %collective-permute-start.20) | collective-permute-done | bytes 655392 | tf_op jit(solution)/shard_map/ppermute | solution.py:38
  101.0 2.6 %collective-permute-start.25 = (bf16[64,5120]{1,0:T(8,128)(2,1)}, bf16[64,5120]{1,0:T(8,128)(2,1)}, u32[]{:S(2)}, u32[]{:S(2)}) collective-permute-start(bf16[64,5120]{1,0:T(8,128)(2,1)} %get-tuple-element.36), channel_id=1, source_target_pairs={{0,3},{1,0},{2,1},{3,2},{4,7},{5,4},{6,5},{7,6},{8,11},{9,8},{10,9... | collective-permute-start | bytes 1966088 | tf_op jit(solution)/shard_map/ppermute | solution.py:38
  109.8 2.5 %shard_map.88 = (bf16[64,5120]{1,0:T(8,128)(2,1)S(1)}, bf16[64,5120]{1,0:T(8,128)(2,1)S(1)}) custom-call(s32[1]{0:T(128)} %bitcast.core, bf16[128,256]{1,0:T(8,128)(2,1)S(1)} %copy-done.29, bf16[128,512]{1,0:T(8,128)(2,1)S(1)} %copy-done.19, bf16[256,512]{1,0:T(8,128)(2,1)S(1)} %shard_map.85.refs_1_, bf16[128,512]{1,0:T(8,128)(2,1)S(1)} %shard_map.86.refs_2_, ...), custom_call_target="tpu_custom_call" | custom-call | flops 469762048 | bytes 8000000 | tf_op jit(solution)/shard_map/pallas_call | solution.py:242
  117.3 3.0 %collective-permute-start.27 = (bf16[32,5120]{1,0:T(8,128)(2,1)S(1)}, bf16[32,5120]{1,0:T(8,128)(2,1)S(1)}, u32[]{:S(2)}, u32[]{:S(2)}) collective-permute-start(bf16[32,5120]{1,0:T(8,128)(2,1)S(1)} %get-tuple-element.39), channel_id=1, source_target_pairs={{0,24},{1,25},{2,26},{3,27},{4,28},{5,29},{6,30},{7,31},{8,0},{9,1... | collective-permute-start | bytes 983048 | tf_op jit(solution)/shard_map/ppermute | solution.py:38
  124.7 3.1 %collective-permute-done.27 = bf16[32,5120]{1,0:T(8,128)(2,1)S(1)} collective-permute-done((bf16[32,5120]{1,0:T(8,128)(2,1)S(1)}, bf16[32,5120]{1,0:T(8,128)(2,1)S(1)}, u32[]{:S(2)}, u32[]{:S(2)}) %collective-permute-start.27) | collective-permute-done | bytes 327712 | tf_op jit(solution)/shard_map/ppermute | solution.py:38
  135.1 2.5 %collective-permute-done.19 = f32[32,5120]{1,0:T(8,128)} collective-permute-done((f32[32,5120]{1,0:T(8,128)S(1)}, f32[32,5120]{1,0:T(8,128)}, u32[]{:S(2)}, u32[]{:S(2)}) %collective-permute-start.19) | collective-permute-done | bytes 655392 | tf_op jit(solution)/shard_map/ppermute | solution.py:38
  137.6 7.0 %collective-permute-done.29 = bf16[32,5120]{1,0:T(8,128)(2,1)} collective-permute-done((bf16[32,5120]{1,0:T(8,128)(2,1)}, bf16[32,5120]{1,0:T(8,128)(2,1)}, u32[]{:S(2)}, u32[]{:S(2)}) %collective-permute-start.29) | collective-permute-done | bytes 327712 | tf_op jit(solution)/shard_map/ppermute | solution.py:38
  144.6 10.8 %collective-permute-done.30 = bf16[32,5120]{1,0:T(8,128)(2,1)} collective-permute-done((bf16[32,5120]{1,0:T(8,128)(2,1)}, bf16[32,5120]{1,0:T(8,128)(2,1)}, u32[]{:S(2)}, u32[]{:S(2)}) %collective-permute-start.30) | collective-permute-done | bytes 327712 | tf_op jit(solution)/shard_map/ppermute | solution.py:38
  155.4 3.2 %add_bitcast_fusion = f32[1,32,5120]{2,1,0:T(8,128)} fusion(bf16[32,5120]{1,0:T(8,128)(2,1)} %collective-permute-done.31, bf16[32,5120]{1,0:T(8,128)(2,1)} %collective-permute-done.30, bf16[32,5120]{1,0:T(8,128)(2,1)} %collective-permute-done.29, f32[32,5120]{1,0:T(8,128)S(1)} %copy-done.5, f32[32,5120]{1,0:T(8,128)} %collective-permute-done.19, pred[]{:T(512)S(6)} %lt.18, ...), kind=kLoop, calls=%fused_computation.1 | loop fusion | flops 2621440 | bytes 4608005 | tf_op jit(solution)/shard_map/broadcast_in_dim | solution.py:369
  (126 shorter events, 55.5 us)
Async XLA Ops:
  4.6 12.0 %collective-permute-start.1 = (bf16[32,5120]{1,0:T(8,128)(2,1)S(1)}, bf16[32,5120]{1,0:T(8,128)(2,1)S(1)}, u32[]{:S(2)}, u32[]{:S(2)}) collective-permute-start(bf16[32,5120]{1,0:T(8,128)(2,1)S(1)} %shard_map.82), channel_id=1, source_target_pairs={{0,24},{1,25},{2,26},{3,27},{4,28},{5,29},{6,30},{7,31},{8,0},{9,1... | collective-permute-start | bytes 983048 | tf_op jit(solution)/shard_map/ppermute | solution.py:38
  8.5 23.9 %collective-permute-start = (bf16[32,5120]{1,0:T(8,128)(2,1)S(1)}, bf16[32,5120]{1,0:T(8,128)(2,1)}, u32[]{:S(2)}, u32[]{:S(2)}) collective-permute-start(bf16[32,5120]{1,0:T(8,128)(2,1)S(1)} %shard_map.82), channel_id=1, source_target_pairs={{0,8},{1,9},{2,10},{3,11},{4,12},{5,13},{6,14},{7,15},{8,16},{9,17... | collective-permute-start | bytes 983048 | tf_op jit(solution)/shard_map/ppermute | solution.py:38
  13.9 16.9 %collective-permute-start.11 = (bf16[2,2560,128]{2,1,0:T(8,128)(2,1)S(1)}, bf16[2,2560,128]{2,1,0:T(8,128)(2,1)}, u32[]{:S(2)}, u32[]{:S(2)}) collective-permute-start(bf16[2,2560,128]{2,1,0:T(8,128)(2,1)S(1)} %constant_dynamic-slice_fusion.2), channel_id=1, source_target_pairs={{0,4},{1,5},{2,6},{3,7},{4,0},{5,1},{6,2},{7,3},{8,12},{9,13},{10,... | collective-permute-start | bytes 3932168 | tf_op jit(solution)/shard_map/ppermute | solution.py:38
  15.3 22.5 %collective-permute-start.9 = (bf16[1,2560,128]{2,1,0:T(8,128)(2,1)S(1)}, bf16[1,2560,128]{2,1,0:T(8,128)(2,1)S(1)}, u32[]{:S(2)}, u32[]{:S(2)}) collective-permute-start(bf16[1,2560,128]{2,1,0:T(8,128)(2,1)S(1)} %constant_dynamic-slice_fusion.3), channel_id=1, source_target_pairs={{0,4},{1,5},{2,6},{3,7},{4,0},{5,1},{6,2},{7,3},{8,12},{9,13},{10,... | collective-permute-start | bytes 1966088 | tf_op jit(solution)/shard_map/ppermute | solution.py:38
  16.6 28.3 %collective-permute-start.16 = (bf16[128,2560]{1,0:T(8,128)(2,1)S(1)}, bf16[128,2560]{1,0:T(8,128)(2,1)S(1)}, u32[]{:S(2)}, u32[]{:S(2)}) collective-permute-start(bf16[128,2560]{1,0:T(8,128)(2,1)S(1)} %constant_dynamic-slice_fusion.1), channel_id=1, source_target_pairs={{0,4},{1,5},{2,6},{3,7},{4,0},{5,1},{6,2},{7,3},{8,12},{9,13},{10,... | collective-permute-start | bytes 1966088 | tf_op jit(solution)/shard_map/ppermute | solution.py:38
  17.1 30.3 %collective-permute-start.6 = (bf16[64,5120]{1,0:T(8,128)(2,1)S(1)}, bf16[64,5120]{1,0:T(8,128)(2,1)}, u32[]{:S(2)}, u32[]{:S(2)}) collective-permute-start(bf16[64,5120]{1,0:T(8,128)(2,1)S(1)} %constant_dynamic-update-slice_fusion.refs_1_), channel_id=1, source_target_pairs={{0,3},{1,0},{2,1},{3,2},{4,7},{5,4},{6,5},{7,6},{8,11},{9,8},{10,9... | collective-permute-start | bytes 1966088 | tf_op jit(solution)/shard_map/ppermute | solution.py:38
  30.9 27.6 %collective-permute-start.12 = (bf16[2,2560,128]{2,1,0:T(8,128)(2,1)}, bf16[2,2560,128]{2,1,0:T(8,128)(2,1)S(1)}, u32[]{:S(2)}, u32[]{:S(2)}) collective-permute-start(bf16[2,2560,128]{2,1,0:T(8,128)(2,1)} %collective-permute-done.11.refs_4_.refs_6_), channel_id=1, source_target_pairs={{0,32},{1,33},{2,34},{3,35},{4,36},{5,37},{6,38},{7,39},{8,40},{9,... | collective-permute-start | bytes 3932168 | tf_op jit(solution)/shard_map/ppermute | solution.py:38
  33.4 14.4 %collective-permute-start.3 = (bf16[64,5120]{1,0:T(8,128)(2,1)S(1)}, bf16[64,5120]{1,0:T(8,128)(2,1)}, u32[]{:S(2)}, u32[]{:S(2)}) collective-permute-start(bf16[64,5120]{1,0:T(8,128)(2,1)S(1)} %pad_maximum_fusion.refs_0_), channel_id=1, source_target_pairs={{0,1},{1,2},{2,3},{3,0},{4,5},{5,6},{6,7},{7,4},{8,9},{9,10},{10,1... | collective-permute-start | bytes 1966088 | tf_op jit(solution)/shard_map/ppermute | solution.py:38
  37.8 13.7 %collective-permute-start.4 = (bf16[64,5120]{1,0:T(8,128)(2,1)S(1)}, bf16[64,5120]{1,0:T(8,128)(2,1)S(1)}, u32[]{:S(2)}, u32[]{:S(2)}) collective-permute-start(bf16[64,5120]{1,0:T(8,128)(2,1)S(1)} %constant_dynamic-update-slice_fusion.refs_1_), channel_id=1, source_target_pairs={{0,1},{1,2},{2,3},{3,0},{4,5},{5,6},{6,7},{7,4},{8,9},{9,10},{10,1... | collective-permute-start | bytes 1966088 | tf_op jit(solution)/shard_map/ppermute | solution.py:38
  47.4 20.3 %collective-permute-start.8 = (bf16[64,5120]{1,0:T(8,128)(2,1)}, bf16[64,5120]{1,0:T(8,128)(2,1)}, u32[]{:S(2)}, u32[]{:S(2)}) collective-permute-start(bf16[64,5120]{1,0:T(8,128)(2,1)} %collective-permute-done.6.refs_5_.refs_3_), channel_id=1, source_target_pairs={{0,3},{1,0},{2,1},{3,2},{4,7},{5,4},{6,5},{7,6},{8,11},{9,8},{10,9... | collective-permute-start | bytes 1966088 | tf_op jit(solution)/shard_map/ppermute | solution.py:38
  47.9 20.9 %collective-permute-start.7 = (bf16[64,5120]{1,0:T(8,128)(2,1)}, bf16[64,5120]{1,0:T(8,128)(2,1)}, u32[]{:S(2)}, u32[]{:S(2)}) collective-permute-start(bf16[64,5120]{1,0:T(8,128)(2,1)} %collective-permute-done.3.refs_2_.refs_0_), channel_id=1, source_target_pairs={{0,1},{1,2},{2,3},{3,0},{4,5},{5,6},{6,7},{7,4},{8,9},{9,10},{10,1... | collective-permute-start | bytes 1966088 | tf_op jit(solution)/shard_map/ppermute | solution.py:38
  52.3 25.7 %collective-permute-start.18 = (f32[32,5120]{1,0:T(8,128)}, f32[32,5120]{1,0:T(8,128)}, u32[]{:S(2)}, u32[]{:S(2)}) collective-permute-start(f32[32,5120]{1,0:T(8,128)} %bitcast.3.state), channel_id=1, source_target_pairs={{0,32},{1,33},{2,34},{3,35},{4,36},{5,37},{6,38},{7,39},{8,40},{9,... | collective-permute-start | bytes 1966088 | tf_op jit(solution)/shard_map/ppermute | solution.py:38
  54.9 25.8 %collective-permute-start.10 = (bf16[1,2560,128]{2,1,0:T(8,128)(2,1)}, bf16[1,2560,128]{2,1,0:T(8,128)(2,1)S(1)}, u32[]{:S(2)}, u32[]{:S(2)}) collective-permute-start(bf16[1,2560,128]{2,1,0:T(8,128)(2,1)} %copy-done.26), channel_id=1, source_target_pairs={{0,32},{1,33},{2,34},{3,35},{4,36},{5,37},{6,38},{7,39},{8,40},{9,... | collective-permute-start | bytes 1966088 | tf_op jit(solution)/shard_map/ppermute | solution.py:38
  58.5 27.2 %collective-permute-start.17 = (bf16[128,2560]{1,0:T(8,128)(2,1)}, bf16[128,2560]{1,0:T(8,128)(2,1)S(1)}, u32[]{:S(2)}, u32[]{:S(2)}) collective-permute-start(bf16[128,2560]{1,0:T(8,128)(2,1)} %copy-done.6), channel_id=1, source_target_pairs={{0,32},{1,33},{2,34},{3,35},{4,36},{5,37},{6,38},{7,39},{8,40},{9,... | collective-permute-start | bytes 1966088 | tf_op jit(solution)/shard_map/ppermute | solution.py:38
  67.7 18.0 %collective-permute-start.14 = (bf16[256,512]{1,0:T(8,128)(2,1)S(1)}, bf16[256,512]{1,0:T(8,128)(2,1)S(1)}, u32[]{:S(2)}, u32[]{:S(2)}) collective-permute-start(bf16[256,512]{1,0:T(8,128)(2,1)S(1)} %shard_map.85.refs_1_), channel_id=1, source_target_pairs={{0,4},{1,5},{2,6},{3,7},{4,0},{5,1},{6,2},{7,3},{8,12},{9,13},{10,... | collective-permute-start | bytes 786440 | tf_op jit(solution)/shard_map/ppermute | solution.py:38
  73.3 12.4 %collective-permute-start.15 = (bf16[128,512]{1,0:T(8,128)(2,1)S(1)}, bf16[128,512]{1,0:T(8,128)(2,1)S(1)}, u32[]{:S(2)}, u32[]{:S(2)}) collective-permute-start(bf16[128,512]{1,0:T(8,128)(2,1)S(1)} %shard_map.86.refs_2_), channel_id=1, source_target_pairs={{0,4},{1,5},{2,6},{3,7},{4,0},{5,1},{6,2},{7,3},{8,12},{9,13},{10,... | collective-permute-start | bytes 393224 | tf_op jit(solution)/shard_map/ppermute | solution.py:38
  95.3 17.1 %collective-permute-start.23 = (bf16[64,5120]{1,0:T(8,128)(2,1)}, bf16[64,5120]{1,0:T(8,128)(2,1)}, u32[]{:S(2)}, u32[]{:S(2)}) collective-permute-start(bf16[64,5120]{1,0:T(8,128)(2,1)} %get-tuple-element.34), channel_id=1, source_target_pairs={{0,3},{1,0},{2,1},{3,2},{4,7},{5,4},{6,5},{7,6},{8,11},{9,8},{10,9... | collective-permute-start | bytes 1966088 | tf_op jit(solution)/shard_map/ppermute | solution.py:38
  96.1 16.2 %collective-permute-start.24 = (bf16[64,5120]{1,0:T(8,128)(2,1)}, bf16[64,5120]{1,0:T(8,128)(2,1)}, u32[]{:S(2)}, u32[]{:S(2)}) collective-permute-start(bf16[64,5120]{1,0:T(8,128)(2,1)} %get-tuple-element.35), channel_id=1, source_target_pairs={{0,1},{1,2},{2,3},{3,0},{4,5},{5,6},{6,7},{7,4},{8,9},{9,10},{10,1... | collective-permute-start | bytes 1966088 | tf_op jit(solution)/shard_map/ppermute | solution.py:38
  101.0 13.4 %collective-permute-start.22 = (bf16[64,5120]{1,0:T(8,128)(2,1)}, bf16[64,5120]{1,0:T(8,128)(2,1)}, u32[]{:S(2)}, u32[]{:S(2)}) collective-permute-start(bf16[64,5120]{1,0:T(8,128)(2,1)} %get-tuple-element.33), channel_id=1, source_target_pairs={{0,1},{1,2},{2,3},{3,0},{4,5},{5,6},{6,7},{7,4},{8,9},{9,10},{10,1... | collective-permute-start | bytes 1966088 | tf_op jit(solution)/shard_map/ppermute | solution.py:38
  101.0 13.4 %collective-permute-start.25 = (bf16[64,5120]{1,0:T(8,128)(2,1)}, bf16[64,5120]{1,0:T(8,128)(2,1)}, u32[]{:S(2)}, u32[]{:S(2)}) collective-permute-start(bf16[64,5120]{1,0:T(8,128)(2,1)} %get-tuple-element.36), channel_id=1, source_target_pairs={{0,3},{1,0},{2,1},{3,2},{4,7},{5,4},{6,5},{7,6},{8,11},{9,8},{10,9... | collective-permute-start | bytes 1966088 | tf_op jit(solution)/shard_map/ppermute | solution.py:38
  121.4 16.2 %collective-permute-start.19 = (f32[32,5120]{1,0:T(8,128)S(1)}, f32[32,5120]{1,0:T(8,128)}, u32[]{:S(2)}, u32[]{:S(2)}) collective-permute-start(f32[32,5120]{1,0:T(8,128)S(1)} %copy-done.5), channel_id=1, source_target_pairs={{0,64},{1,65},{2,66},{3,67},{4,68},{5,69},{6,70},{7,71},{8,72},{9,... | collective-permute-start | bytes 1966088 | tf_op jit(solution)/shard_map/ppermute | solution.py:38
  131.2 13.4 %collective-permute-start.29 = (bf16[32,5120]{1,0:T(8,128)(2,1)}, bf16[32,5120]{1,0:T(8,128)(2,1)}, u32[]{:S(2)}, u32[]{:S(2)}) collective-permute-start(bf16[32,5120]{1,0:T(8,128)(2,1)} %fusion), channel_id=1, source_target_pairs={{0,64},{1,65},{2,66},{3,67},{4,68},{5,69},{6,70},{7,71},{8,72},{9,... | collective-permute-start | bytes 983048 | tf_op jit(solution)/shard_map/ppermute | solution.py:38
  132.5 22.9 %collective-permute-start.30 = (bf16[32,5120]{1,0:T(8,128)(2,1)}, bf16[32,5120]{1,0:T(8,128)(2,1)}, u32[]{:S(2)}, u32[]{:S(2)}) collective-permute-start(bf16[32,5120]{1,0:T(8,128)(2,1)} %fusion), channel_id=1, source_target_pairs={{0,96},{1,97},{2,98},{3,99},{4,100},{5,101},{6,102},{7,103},{8,104... | collective-permute-start | bytes 983048 | tf_op jit(solution)/shard_map/ppermute | solution.py:38
  133.8 21.7 %collective-permute-start.31 = (bf16[32,5120]{1,0:T(8,128)(2,1)}, bf16[32,5120]{1,0:T(8,128)(2,1)}, u32[]{:S(2)}, u32[]{:S(2)}) collective-permute-start(bf16[32,5120]{1,0:T(8,128)(2,1)} %fusion), channel_id=1, source_target_pairs={{0,32},{1,33},{2,34},{3,35},{4,36},{5,37},{6,38},{7,39},{8,40},{9,... | collective-permute-start | bytes 983048 | tf_op jit(solution)/shard_map/ppermute | solution.py:38
  (40 other events, 341.0 us)

commit v4 on v2

v4 whole, which is shorter than its diff:
```python
import functools
import math

import jax
import jax.numpy as jnp
from jax import lax
from jax.experimental import pallas as pl
from jax.experimental.pallas import tpu as pltpu
from jax.sharding import PartitionSpec as P

HDIM = 128
XS, YLS, ZS = 4, 2, 4
BF16, F32 = jnp.bfloat16, jnp.float32
VMEM = pl.BlockSpec(memory_space=pltpu.VMEM)
SMEM = pl.BlockSpec(memory_space=pltpu.SMEM)
ANY = pl.BlockSpec(memory_space=pl.ANY)
PARAMS = pltpu.CompilerParams(vmem_limit_bytes=20 * 1024 * 1024)
WIDE = pltpu.CompilerParams(vmem_limit_bytes=60 * 1024 * 1024)


def moves(rule):
    pairs = []
    for yh in range(2):
        for core in range(2):
            for x in range(XS):
                for yl in range(YLS):
                    for z in range(ZS):
                        to = rule(yh, core, x, yl, z)
                        if to is not None:
                            pairs.append((flat(yh, core, x, yl, z), flat(*to)))
    return pairs


def flat(yh, core, x, yl, z):
    return (((yh * 2 + core) * XS + x) * YLS + yl) * ZS + z


def send(value, rule):
    return lax.ppermute(value, ("tm", "seq"), moves(rule))


def first_axis(step):
    return lambda yh, core, x, yl, z: (
        (yh, core, (x + step) % XS, yl, z) if core == 0 else (yh, core, x, yl, (z + step) % ZS)
    )


def second_axis(step):
    return lambda yh, core, x, yl, z: (
        (yh, core, x, yl, (z + step) % ZS) if core == 0 else (yh, core, (x + step) % XS, yl, z)
    )


def to_other_core(yh, core, x, yl, z):
    return (yh, 1 - core, x, yl, z)


def to_partner(yh, core, x, yl, z):
    return (yh, core, x, 1 - yl, z)


def to_both_sides(yh, core, x, yl, z):
    return (yh if core == 0 else 1 - yh, core, x, 1 - yl, z)


def to_later_half(yh, core, x, yl, z):
    return (1, core, x, yl, z) if yh == 0 else None


def from_first(yh_to, core_to):
    return lambda yh, core, x, yl, z: (yh_to, core_to, x, yl, z) if yh == 0 and core == 0 else None


def modulate_kernel(index, state, scale, shift, gate, out, gates):
    row = pl.ds(lax.rem(index[0], 8), 1)
    value = state[...]
    mean = jnp.mean(value * value, axis=-1, keepdims=True)
    normed = value * lax.rsqrt(mean + 1e-06)
    out[...] = (normed * (1.0 + scale[row, :]) + shift[row, :]).astype(BF16)
    gates[...] = gate[row, :]


def modulate(index, state, scale, shift, gate):
    rows, width = state.shape
    table = pl.BlockSpec((8, width), lambda i, index: (lax.div(index[0], 8), 0))
    whole = pl.BlockSpec((rows, width), lambda i, index: (0, 0))
    return pl.pallas_call(
        modulate_kernel,
        grid_spec=pltpu.PrefetchScalarGridSpec(
            num_scalar_prefetch=1,
            grid=(1,),
            in_specs=[whole, table, table, table],
            out_specs=[whole, pl.BlockSpec((1, width), lambda i, index: (0, 0))],
        ),
        out_shape=[
            jax.ShapeDtypeStruct(state.shape, BF16),
            jax.ShapeDtypeStruct((1, width), F32),
        ],
        compiler_params=WIDE,
        cost_estimate=pl.CostEstimate(flops=1000000, bytes_accessed=2000000, transcendentals=0),
    )(index, state, scale, shift, gate)


def pack_kernel(core, qkv, out, half):
    del core
    half[:3] = qkv[...]
    for block in range(out.shape[1] // HDIM):
        here = slice(block * HDIM, (block + 1) * HDIM)
        half[3, here, :] = out[:, here]


def pack(core, qkv_weight, out_weight):
    half = qkv_weight.shape[1] // 2
    return pl.pallas_call(
        pack_kernel,
        grid_spec=pltpu.PrefetchScalarGridSpec(
            num_scalar_prefetch=1,
            grid=(1,),
            in_specs=[
                pl.BlockSpec((3, half, HDIM), lambda i, core: (0, core[0], 0)),
                pl.BlockSpec((HDIM, half), lambda i, core: (0, core[0])),
            ],
            out_specs=pl.BlockSpec((4, half, HDIM), lambda i, core: (0, 0, 0)),
        ),
        out_shape=jax.ShapeDtypeStruct((4, half, HDIM), BF16),
        compiler_params=WIDE,
        cost_estimate=pl.CostEstimate(flops=0, bytes_accessed=4000000, transcendentals=0),
    )(core, qkv_weight, out_weight)


def stack_kernel(one, two, out):
    size = one.shape[0]
    out[:size] = one[...]
    out[size:] = two[...]


def stack(one, two):
    return pl.pallas_call(
        stack_kernel,
        out_shape=jax.ShapeDtypeStruct((2 * one.shape[0], one.shape[1]), one.dtype),
        in_specs=[VMEM] * 2,
        out_specs=VMEM,
        compiler_params=PARAMS,
    )(one, two)


def sides(core, mine, theirs, width, step, one):
    half = width // 2
    first = core[0] * half

    def side(weight, start):
        def body(block, carry):
            at = pl.multiple_of(block * step, step)
            one(weight, at, pl.multiple_of(start + at, 128))
            return carry

        lax.fori_loop(0, half // step, body, 0, unroll=True)

    side(mine, first)
    side(theirs, half - first)


def project_kernel(count, rows, core, *refs):
    pieces, (own, mine, theirs) = refs[:count], refs[count : count + 3]
    both_kv, queries, total = refs[count + 3], refs[count + 4 : -1], refs[-1]
    step, wide = 512, 2 * HDIM
    total[...] = jnp.zeros_like(total)

    def one(weight, at, column):
        left = jnp.concatenate([piece[:, pl.ds(column, step)] for piece in pieces], axis=0)
        for kind in range(3):
            both = jnp.concatenate(
                [own[kind, pl.ds(column, step), :], weight[kind, pl.ds(at, step), :]], axis=-1
            )
            total[kind] += jnp.dot(left, both, preferred_element_type=F32)

    sides(core, mine, theirs, own.shape[1], step, one)
    both_kv[:, :wide] = total[1].astype(BF16)
    both_kv[:, wide:] = total[2].astype(BF16)
    at = 0
    for out, size in zip(queries, rows):
        out[...] = total[0, at : at + size].astype(BF16)
        at += size


def project(core, pieces, weight, mine, theirs, rows):
    wide = 2 * HDIM
    tokens, depth = sum(rows), weight.shape[1]
    return pl.pallas_call(
        functools.partial(project_kernel, len(pieces), rows),
        out_shape=[jax.ShapeDtypeStruct((tokens, 2 * wide), BF16)]
        + [jax.ShapeDtypeStruct((size, wide), BF16) for size in rows],
        in_specs=[SMEM] + [VMEM] * (len(pieces) + 3),
        out_specs=[VMEM] * (1 + len(rows)),
        scratch_shapes=[pltpu.VMEM((3, tokens, wide), F32)],
        compiler_params=PARAMS,
        cost_estimate=pl.CostEstimate(
            flops=6 * tokens * depth * wide, bytes_accessed=1000000, transcendentals=0
        ),
    )(core, *pieces, weight, mine, theirs)


def attend_kernel(count, cuts, core, queries, own, mine, theirs, *refs):
    near, far = refs[:count], refs[count : 2 * count]
    outs, attended = refs[2 * count : -1], refs[-1]
    scale = 1.0 / math.sqrt(HDIM)
    contract = (((1,), (1,)), ((), ()))
    for head in range(2):
        here = slice(head * HDIM, (head + 1) * HDIM)
        there = slice((1 - head) * HDIM, (2 - head) * HDIM)
        here_v = slice((2 + head) * HDIM, (3 + head) * HDIM)
        there_v = slice((3 - head) * HDIM, (4 - head) * HDIM)
        all_keys = jnp.concatenate([r[:, here] for r in near] + [r[:, there] for r in far], axis=0)
        all_values = jnp.concatenate(
            [r[:, here_v] for r in near] + [r[:, there_v] for r in far], axis=0
        )
        scores = lax.dot_general(queries[:, here], all_keys, contract, preferred_element_type=F32)
        top = jnp.max(scores, axis=-1, keepdims=True)
        weights = jnp.exp((scores - top) * scale)
        total = jnp.sum(weights, axis=-1, keepdims=True)
        mixed = jnp.dot(weights.astype(BF16), all_values, preferred_element_type=F32)
        attended[:, here] = (mixed / total).astype(BF16)
    step = 512

    def one(weight, at, column):
        blocks = [
            weight[3, pl.ds(pl.multiple_of(at + i, HDIM), HDIM), :] for i in range(0, step, HDIM)
        ]
        both = jnp.concatenate(
            [own[:, pl.ds(column, step)], jnp.concatenate(blocks, axis=1)], axis=0
        )
        result = jnp.dot(attended[...], both, preferred_element_type=F32).astype(BF16)
        row = 0
        for out, size in zip(outs, cuts):
            out[:, pl.ds(column, step)] = result[row : row + size]
            row += size

    sides(core, mine, theirs, own.shape[1], step, one)


def attend(core, queries, near, far, own, mine, theirs, cuts):
    width = own.shape[1]
    tokens = queries.shape[0]
    return pl.pallas_call(
        functools.partial(attend_kernel, len(near), cuts),
        out_shape=[jax.ShapeDtypeStruct((size, width), BF16) for size in cuts],
        in_specs=[SMEM] + [VMEM] * (4 + 2 * len(near)),
        out_specs=[VMEM] * len(cuts),
        scratch_shapes=[pltpu.VMEM((tokens, 2 * HDIM), BF16)],
        compiler_params=PARAMS,
        cost_estimate=pl.CostEstimate(
            flops=4 * tokens * HDIM * (width + 2048), bytes_accessed=1000000, transcendentals=0
        ),
    )(core, queries, own, mine, theirs, *near, *far)


def join_kernel(after, before, low, high, to_after, to_before):
    to_after[...] = (after[...].astype(F32) + low[...].astype(F32)).astype(BF16)
    to_before[...] = (before[...].astype(F32) + high[...].astype(F32)).astype(BF16)


def join(after, before, low, high):
    return pl.pallas_call(
        join_kernel,
        out_shape=[jax.ShapeDtypeStruct(before.shape, BF16)] * 2,
        in_specs=[VMEM] * 4,
        out_specs=[VMEM] * 2,
        compiler_params=PARAMS,
    )(after, before, low, high)


def split_kernel(*refs):
    near_low, near_high, low_1, low_2, high_1, high_2 = refs[:6]
    kept, to_minus, to_plus, to_opposite = refs[-4:]
    size = kept.shape[0]

    def total(near, one, two, rows):
        return near[rows].astype(F32) + one[rows].astype(F32) + two[rows].astype(F32)

    kept[...] = total(near_low, low_1, low_2, slice(0, size))
    to_minus[...] = total(near_low, low_1, low_2, slice(size, 2 * size)).astype(BF16)
    to_plus[...] = total(near_high, high_1, high_2, slice(0, size)).astype(BF16)
    to_opposite[...] = total(near_high, high_1, high_2, slice(size, 2 * size)).astype(BF16)


def split(parts, until):
    size, width = parts[0].shape[0] // 2, parts[0].shape[1]
    return pl.pallas_call(
        split_kernel,
        out_shape=[jax.ShapeDtypeStruct((size, width), F32)]
        + [jax.ShapeDtypeStruct((size, width), BF16)] * 3,
        in_specs=[VMEM] * 6 + [ANY] * len(until),
        out_specs=[VMEM] * 4,
        compiler_params=PARAMS,
    )(*parts, *until)


def drift_kernel(index, steps, total, one, two, three, gates, drift, term):
    moved = total[...] + one[...].astype(F32) + two[...].astype(F32) + three[...].astype(F32)
    result = steps[index[0]] * (gates[...] * moved)
    drift[...] = result
    term[...] = result.astype(BF16)


def drifts(index, steps, total, arrived, gates):
    return pl.pallas_call(
        drift_kernel,
        out_shape=[
            jax.ShapeDtypeStruct(total.shape, F32),
            jax.ShapeDtypeStruct(total.shape, BF16),
        ],
        in_specs=[SMEM] * 2 + [VMEM] * 5,
        out_specs=[VMEM] * 2,
        compiler_params=PARAMS,
    )(index, steps, total, *arrived, gates)


def both_kernel(drift, beside, term):
    term[...] = (drift[...] + beside[...].astype(F32)).astype(BF16)


def both_cores(drift, beside):
    return pl.pallas_call(
        both_kernel,
        out_shape=jax.ShapeDtypeStruct(drift.shape, BF16),
        in_specs=[VMEM] * 2,
        out_specs=VMEM,
        compiler_params=PARAMS,
    )(drift, beside)


def finish_kernel(place, start, one, two, three, drift, beside, earlier, out):
    first = jnp.where(place[0] == 0, start[...], one[...] + two[...] + three[...])
    on_second = jnp.where(lax.rem(place[0], 2) == 1, beside[...].astype(F32), 0.0)
    out[...] = first + (drift[...] + on_second + earlier[...].astype(F32))


def finish(place, *parts):
    return pl.pallas_call(
        finish_kernel,
        out_shape=jax.ShapeDtypeStruct(parts[0].shape, F32),
        in_specs=[SMEM] + [VMEM] * 7,
        out_specs=VMEM,
        compiler_params=PARAMS,
    )(place, *parts)


def hold_kernel(value, *refs):
    del value, refs


def hold(value, *until):
    return pl.pallas_call(
        hold_kernel,
        out_shape=jax.ShapeDtypeStruct(value.shape, value.dtype),
        in_specs=[ANY] * (1 + len(until)),
        out_specs=ANY,
        input_output_aliases={0: 0},
        compiler_params=PARAMS,
    )(value, *until)


def on_device(
    trajectory, qkv_weight, out_weight, shift_table, scale_table, gate_table, step_sizes, window_start
):
    group = lax.axis_index("tm")
    core = group & 1
    place, core, index = group[None], core[None], window_start + group
    state = trajectory[0]
    mine = send(pack(core, qkv_weight, out_weight), to_both_sides)
    modulated, gates = modulate(index, state, scale_table, shift_table, gate_table)
    minus, plus, opposite = [send(modulated, first_axis(s)) for s in (1, -1, 2)]
    near_low = stack(modulated, minus)
    before_low, after_low = send(near_low, second_axis(1)), send(near_low, second_axis(-1))
    near_high = stack(plus, opposite)
    after_high, before_high = send(near_high, second_axis(-1)), send(near_high, second_axis(1))
    last_low, last_high = send(before_low, second_axis(1)), send(after_high, second_axis(-1))

    size = near_low.shape[0]
    near = [near_low, near_high]
    side = [before_low, before_high, after_low, after_high]
    last = [last_low, last_high]
    mine = hold(mine, *side)
    weights = (qkv_weight, mine, send(mine, to_other_core))
    first_kv, near_q, side_q = project(core, near + side, *weights, [2 * size, 4 * size])
    last_kv, last_q = project(core, last, *weights, [2 * size])
    kv = [first_kv, last_kv]
    far = [send(value, to_partner) for value in kv]

    outs = (out_weight, *weights[1:])
    last_low, last_high = attend(core, last_q, kv, far, *outs, [size] * 2)
    from_low, from_high = send(last_low, second_axis(1)), send(last_high, second_axis(-1))
    before_low, before_high, after_low, after_high = attend(
        core, side_q, kv, far, *outs, [size] * 4
    )
    high_1, low_2 = send(after_high, second_axis(1)), send(before_low, second_axis(-1))
    near_low, near_high = attend(core, near_q, kv, far, *outs, [size] * 2)
    after_low, before_high = join(after_low, before_high, from_low, from_high)
    low_1, high_2 = send(after_low, second_axis(1)), send(before_high, second_axis(-1))
    starts = [send(state, from_first(*to)) for to in ((0, 1), (1, 0), (1, 1))]
    total, to_minus, to_plus, to_opposite = split(
        [near_low, near_high, low_1, low_2, high_1, high_2], starts
    )
    arrived = [
        send(value, first_axis(s)) for value, s in ((to_plus, 1), (to_minus, -1), (to_opposite, 2))
    ]
    drift, term = drifts(index, step_sizes, total, arrived, gates)
    beside = send(term, to_other_core)
    earlier = send(both_cores(drift, beside), to_later_half)
    return finish(place, state, *starts, drift, beside, earlier)[None]


def solution(mesh):
    in_specs = (P("tm", "seq", None), P(None, None, "seq"), P("seq", None), P(), P(), P(), P(), P())
    out_specs = P("tm", "seq", None)
    return jax.shard_map(
        on_device, mesh=mesh, in_specs=in_specs, out_specs=out_specs, check_vma=False
    )
```

time: 152 us -> 128 us (0.84)
  Pallas kernels: 34.9 us -> 17.4 us
  waiting for transfers between devices: 57.9 us -> 72.3 us
  local copies, waits for them, and re-layouts: 14.2 us -> 1 us
  other arithmetic: 7.13 us -> 0 us
    ppermute x26 -> x27, waiting for transfers between devices: 57.9 us -> 72.3 us  [send(): return lax.ppermute(value, ('tm', 'seq'), moves(rule))]
    pallas_call x3, Pallas kernels: 13.4 us -> 4.6 us  [attend(): pl.pallas_call(functools.partial(attend_kernel, len(near), cuts), out_sha...]
    unnamed x32 -> x12, local copies, waits for them, and re-layouts: 7.12 us -> 1 us
    pallas_call x4 -> x10, Pallas kernels: 17.5 us -> 12 us  [the longest x2 4.43 us: project(): pl.pallas_call(functools.partial(project_kernel, len(pieces), rows), out_...]
    dynamic_slice x4 -> x0, local copies, waits for them, and re-layouts: 4.63 us -> none  [the longest x2 3.96 us: swap_weights(): lax.dynamic_slice_in_dim(weight, core * half, half, axis)]
    select_n x2 -> x0, other arithmetic: 3.35 us -> none  [the longest x1 2.19 us: on_device(): start = jnp.where(core == 0, state, send(state, to_later_core))]
    slice x2 -> x0, local copies, waits for them, and re-layouts: 2.41 us -> none  [the longest x1 1.28 us: on_device(): before[:half]]
    broadcast_in_dim x1 -> x0, other arithmetic: 1.81 us -> none  [on_device(): return (start + summed)[None]]
  transfers between devices with their start and end apart: 26 -> 27, of which waited for: 13 -> 16; matrix products, arithmetic and copies ran while one was open for 6% -> 0% of each run, Pallas kernels for 21% -> 8%
where the time goes in v4:
time: 128 us
  waiting for transfers between devices  72.3 us (56%)
  starting transfers between devices  36.1 us (28%)
  Pallas kernels  17.4 us (14%)
    ppermute x27, waiting for transfers between devices, send(): return lax.ppermute(value, ('tm', 'seq'), moves(rule))  72.3 us
    ppermute x27, starting transfers between devices, send(): return lax.ppermute(value, ('tm', 'seq'), moves(rule))  36.1 us
    pallas_call x3, Pallas kernels, attend(): pl.pallas_call(functools.partial(attend_kernel, len(near), cuts), out_sha...  4.6 us
    pallas_call x2, Pallas kernels, project(): pl.pallas_call(functools.partial(project_kernel, len(pieces), rows), out_...  4.43 us
    pallas_call x1, Pallas kernels, pack(): pl.pallas_call(pack_kernel, grid_spec=pltpu.PrefetchScalarGridSpec(num_sc...  3.4 us
  transfers between devices with their start and end apart: 27, of which 16 were waited for; matrix products, arithmetic and copies ran while one was open for 0% of the time, Pallas kernels for 8%

profile of v4, /device:TPU:17, one launch (start us, length us, event | category | flops | bytes accessed | tf_op | source)
XLA Modules:
  0.0 127.5 jit_solution(10117647134143611394)
XLA Ops:
  0.0 3.4 %shard_map.85 = bf16[4,2560,128]{2,1,0:T(8,128)(2,1)} custom-call(s32[1]{0:T(128)} %bitcast.2.core, bf16[3,5120,128]{2,1,0:T(8,128)(2,1)} %refs_2_.1, bf16[128,5120]{1,0:T(8,128)(2,1)} %own.5), custom_call_target="tpu_custom_call" | custom-call | bytes 4000000 | tf_op jit(solution)/shard_map/pallas_call | solution.py:114
  4.2 2.3 %shard_map.82 = (bf16[32,5120]{1,0:T(8,128)(2,1)}, f32[1,5120]{1,0:T(1,128)}) custom-call(s32[1]{0:T(128)S(6)} %add.4.index, f32[32,5120]{1,0:T(8,128)} %bitcast.4, f32[50,5120]{1,0:T(8,128)} %scale.1, f32[50,5120]{1,0:T(8,128)} %shift.1, f32[50,5120]{1,0:T(8,128)} %gate.1), custom_call_target="tpu_custom_call" | custom-call | flops 1000000 | bytes 2000000 | tf_op jit(solution)/shard_map/pallas_call | solution.py:87
  6.5 3.8 %collective-permute-start.4 = (bf16[32,5120]{1,0:T(8,128)(2,1)}, bf16[32,5120]{1,0:T(8,128)(2,1)S(1)}, u32[]{:S(2)}, u32[]{:S(2)}) collective-permute-start(bf16[32,5120]{1,0:T(8,128)(2,1)} %get-tuple-element.28.one), channel_id=1, source_target_pairs={{0,24},{1,25},{2,26},{3,27},{4,28},{5,29},{6,30},{7,31},{8,0},{9,1... | collective-permute-start | bytes 983048 | tf_op jit(solution)/shard_map/ppermute | solution.py:39
  10.9 7.1 %collective-permute-done.4.one = bf16[32,5120]{1,0:T(8,128)(2,1)S(1)} collective-permute-done((bf16[32,5120]{1,0:T(8,128)(2,1)}, bf16[32,5120]{1,0:T(8,128)(2,1)S(1)}, u32[]{:S(2)}, u32[]{:S(2)}) %collective-permute-start.4) | collective-permute-done | bytes 327712 | tf_op jit(solution)/shard_map/ppermute | solution.py:39
  18.3 2.5 %collective-permute-start.9 = (bf16[64,5120]{1,0:T(8,128)(2,1)S(1)}, bf16[64,5120]{1,0:T(8,128)(2,1)S(1)}, u32[]{:S(2)}, u32[]{:S(2)}) collective-permute-start(bf16[64,5120]{1,0:T(8,128)(2,1)S(1)} %shard_map.84.refs_1_), channel_id=1, source_target_pairs={{0,3},{1,0},{2,1},{3,2},{4,7},{5,4},{6,5},{7,6},{8,11},{9,8},{10,9... | collective-permute-start | bytes 1966088 | tf_op jit(solution)/shard_map/ppermute | solution.py:39
  26.1 2.3 %collective-permute-done.9.refs_3_.refs_5_ = bf16[64,5120]{1,0:T(8,128)(2,1)S(1)} collective-permute-done((bf16[64,5120]{1,0:T(8,128)(2,1)S(1)}, bf16[64,5120]{1,0:T(8,128)(2,1)S(1)}, u32[]{:S(2)}, u32[]{:S(2)}) %collective-permute-start.9) | collective-permute-done | bytes 655392 | tf_op jit(solution)/shard_map/ppermute | solution.py:39
  28.3 5.1 %collective-permute-done.6.refs_0_.refs_2_ = bf16[64,5120]{1,0:T(8,128)(2,1)S(1)} collective-permute-done((bf16[64,5120]{1,0:T(8,128)(2,1)S(1)}, bf16[64,5120]{1,0:T(8,128)(2,1)S(1)}, u32[]{:S(2)}, u32[]{:S(2)}) %collective-permute-start.6) | collective-permute-done | bytes 655392 | tf_op jit(solution)/shard_map/ppermute | solution.py:39
  33.4 7.0 %collective-permute-done.7.refs_1_.refs_3_ = bf16[64,5120]{1,0:T(8,128)(2,1)S(1)} collective-permute-done((bf16[64,5120]{1,0:T(8,128)(2,1)S(1)}, bf16[64,5120]{1,0:T(8,128)(2,1)S(1)}, u32[]{:S(2)}, u32[]{:S(2)}) %collective-permute-start.7) | collective-permute-done | bytes 655392 | tf_op jit(solution)/shard_map/ppermute | solution.py:39
  40.5 3.7 %collective-permute-start.11 = (bf16[4,2560,128]{2,1,0:T(8,128)(2,1)S(1)}, bf16[4,2560,128]{2,1,0:T(8,128)(2,1)S(1)}, u32[]{:S(2)}, u32[]{:S(2)}) collective-permute-start(bf16[4,2560,128]{2,1,0:T(8,128)(2,1)S(1)} %shard_map.86.refs_7_.refs_3_.mine), channel_id=1, source_target_pairs={{0,32},{1,33},{2,34},{3,35},{4,36},{5,37},{6,38},{7,39},{8,40},{9,... | collective-permute-start | bytes 7864328 | tf_op jit(solution)/shard_map/ppermute | solution.py:39
  44.1 2.8 %collective-permute-start.13 = (bf16[64,5120]{1,0:T(8,128)(2,1)S(1)}, bf16[64,5120]{1,0:T(8,128)(2,1)S(1)}, u32[]{:S(2)}, u32[]{:S(2)}) collective-permute-start(bf16[64,5120]{1,0:T(8,128)(2,1)S(1)} %collective-permute-done.9.refs_3_.refs_5_), channel_id=1, source_target_pairs={{0,3},{1,0},{2,1},{3,2},{4,7},{5,4},{6,5},{7,6},{8,11},{9,8},{10,9... | collective-permute-start | bytes 1966088 | tf_op jit(solution)/shard_map/ppermute | solution.py:39
  46.9 1.8 %collective-permute-done.11.refs_8_.refs_4_.theirs = bf16[4,2560,128]{2,1,0:T(8,128)(2,1)S(1)} collective-permute-done((bf16[4,2560,128]{2,1,0:T(8,128)(2,1)S(1)}, bf16[4,2560,128]{2,1,0:T(8,128)(2,1)S(1)}, u32[]{:S(2)}, u32[]{:S(2)}) %collective-permute-start.11) | collective-permute-done | bytes 2621472 | tf_op jit(solution)/shard_map/ppermute | solution.py:39
  48.7 3.2 %shard_map.87 = (bf16[384,512]{1,0:T(8,128)(2,1)S(1)}, bf16[128,256]{1,0:T(8,128)(2,1)S(1)}, bf16[256,256]{1,0:T(8,128)(2,1)S(1)}) custom-call(s32[1]{0:T(128)} %bitcast.2.core, bf16[64,5120]{1,0:T(8,128)(2,1)S(1)} %shard_map.83.refs_0_, bf16[64,5120]{1,0:T(8,128)(2,1)S(1)} %shard_map.84.refs_1_, ...), custom_call_target="tpu_custom_call" | custom-call | flops 3019898880 | bytes 1000000 | tf_op jit(solution)/shard_map/pallas_call | solution.py:189
  52.5 2.0 %collective-permute-done.13.refs_1_ = bf16[64,5120]{1,0:T(8,128)(2,1)S(1)} collective-permute-done((bf16[64,5120]{1,0:T(8,128)(2,1)S(1)}, bf16[64,5120]{1,0:T(8,128)(2,1)S(1)}, u32[]{:S(2)}, u32[]{:S(2)}) %collective-permute-start.13) | collective-permute-done | bytes 655392 | tf_op jit(solution)/shard_map/ppermute | solution.py:39
  54.4 3.2 %collective-permute-done.12.refs_0_ = bf16[64,5120]{1,0:T(8,128)(2,1)S(1)} collective-permute-done((bf16[64,5120]{1,0:T(8,128)(2,1)S(1)}, bf16[64,5120]{1,0:T(8,128)(2,1)S(1)}, u32[]{:S(2)}, u32[]{:S(2)}) %collective-permute-start.12) | collective-permute-done | bytes 655392 | tf_op jit(solution)/shard_map/ppermute | solution.py:39
  59.4 5.7 %collective-permute-done.15.refs_3_ = bf16[128,512]{1,0:T(8,128)(2,1)S(1)} collective-permute-done((bf16[128,512]{1,0:T(8,128)(2,1)S(1)}, bf16[128,512]{1,0:T(8,128)(2,1)S(1)}, u32[]{:S(2)}, u32[]{:S(2)}) %collective-permute-start.15) | collective-permute-done | bytes 131104 | tf_op jit(solution)/shard_map/ppermute | solution.py:39
  72.3 1.9 %shard_map.90 = (bf16[64,5120]{1,0:T(8,128)(2,1)S(1)}, bf16[64,5120]{1,0:T(8,128)(2,1)S(1)}, bf16[64,5120]{1,0:T(8,128)(2,1)S(1)}, bf16[64,5120]{1,0:T(8,128)(2,1)S(1)}) custom-call(s32[1]{0:T(128)} %bitcast.2.core, bf16[256,256]{1,0:T(8,128)(2,1)S(1)} %get-tuple-element.34.queries, bf16[128,5120]{1,0:T(8,128)(2,1)S(1)} %copy-done.1, ...), custom_call_target="tpu_custom_call" | custom-call | flops 939524096 | bytes 1000000 | tf_op jit(solution)/shard_map/pallas_call | solution.py:244
  74.3 3.4 %collective-permute-done.16.low = bf16[64,5120]{1,0:T(8,128)(2,1)S(1)} collective-permute-done((bf16[64,5120]{1,0:T(8,128)(2,1)S(1)}, bf16[64,5120]{1,0:T(8,128)(2,1)S(1)}, u32[]{:S(2)}, u32[]{:S(2)}) %collective-permute-start.16) | collective-permute-done | bytes 655392 | tf_op jit(solution)/shard_map/ppermute | solution.py:39
  80.3 1.9 %collective-permute-start.21 = (bf16[64,5120]{1,0:T(8,128)(2,1)S(1)}, bf16[64,5120]{1,0:T(8,128)(2,1)S(1)}, u32[]{:S(2)}, u32[]{:S(2)}) collective-permute-start(bf16[64,5120]{1,0:T(8,128)(2,1)S(1)} %get-tuple-element.43), channel_id=1, source_target_pairs={{0,3},{1,0},{2,1},{3,2},{4,7},{5,4},{6,5},{7,6},{8,11},{9,8},{10,9... | collective-permute-start | bytes 1966088 | tf_op jit(solution)/shard_map/ppermute | solution.py:39
  83.6 8.7 %collective-permute-done.2.refs_8_.three = f32[32,5120]{1,0:T(8,128)S(1)} collective-permute-done((f32[32,5120]{1,0:T(8,128)S(1)}, f32[32,5120]{1,0:T(8,128)S(1)}, u32[]{:S(2)}, u32[]{:S(2)}) %collective-permute-start.2) | collective-permute-done | bytes 655392 | tf_op jit(solution)/shard_map/ppermute | solution.py:39
  92.3 4.7 %collective-permute-done.18.refs_2_ = bf16[64,5120]{1,0:T(8,128)(2,1)S(1)} collective-permute-done((bf16[64,5120]{1,0:T(8,128)(2,1)S(1)}, bf16[64,5120]{1,0:T(8,128)(2,1)S(1)}, u32[]{:S(2)}, u32[]{:S(2)}) %collective-permute-start.18) | collective-permute-done | bytes 655392 | tf_op jit(solution)/shard_map/ppermute | solution.py:39
  97.6 2.7 %collective-permute-start.23 = (bf16[32,5120]{1,0:T(8,128)(2,1)S(1)}, bf16[32,5120]{1,0:T(8,128)(2,1)S(1)}, u32[]{:S(2)}, u32[]{:S(2)}) collective-permute-start(bf16[32,5120]{1,0:T(8,128)(2,1)S(1)} %get-tuple-element.46), channel_id=1, source_target_pairs={{0,24},{1,25},{2,26},{3,27},{4,28},{5,29},{6,30},{7,31},{8,0},{9,1... | collective-permute-start | bytes 983048 | tf_op jit(solution)/shard_map/ppermute | solution.py:39
  100.3 8.3 %collective-permute-done.22.one = bf16[32,5120]{1,0:T(8,128)(2,1)S(1)} collective-permute-done((bf16[32,5120]{1,0:T(8,128)(2,1)S(1)}, bf16[32,5120]{1,0:T(8,128)(2,1)S(1)}, u32[]{:S(2)}, u32[]{:S(2)}) %collective-permute-start.22) | collective-permute-done | bytes 327712 | tf_op jit(solution)/shard_map/ppermute | solution.py:39
  109.3 3.5 %collective-permute-start.25 = (bf16[32,5120]{1,0:T(8,128)(2,1)S(1)}, bf16[32,5120]{1,0:T(8,128)(2,1)S(1)}, u32[]{:S(2)}, u32[]{:S(2)}) collective-permute-start(bf16[32,5120]{1,0:T(8,128)(2,1)S(1)} %get-tuple-element.50), channel_id=1, source_target_pairs={{0,32},{1,33},{2,34},{3,35},{4,36},{5,37},{6,38},{7,39},{8,40},{9,... | collective-permute-start | bytes 983048 | tf_op jit(solution)/shard_map/ppermute | solution.py:39
  115.5 11.0 %collective-permute-done.26.earlier = bf16[32,5120]{1,0:T(8,128)(2,1)S(1)} collective-permute-done((bf16[32,5120]{1,0:T(8,128)(2,1)S(1)}, bf16[32,5120]{1,0:T(8,128)(2,1)S(1)}, u32[]{:S(2)}, u32[]{:S(2)}) %collective-permute-start.26) | collective-permute-done | bytes 327712 | tf_op jit(solution)/shard_map/ppermute | solution.py:39
  (57 shorter events, 24.7 us)
Async XLA Ops:
  3.4 37.1 %collective-permute-start.10 = (bf16[4,2560,128]{2,1,0:T(8,128)(2,1)}, bf16[4,2560,128]{2,1,0:T(8,128)(2,1)S(1)}, u32[]{:S(2)}, u32[]{:S(2)}) collective-permute-start(bf16[4,2560,128]{2,1,0:T(8,128)(2,1)} %shard_map.85), channel_id=1, source_target_pairs={{0,4},{1,5},{2,6},{3,7},{4,0},{5,1},{6,2},{7,3},{8,12},{9,13},{10,... | collective-permute-start | bytes 7864328 | tf_op jit(solution)/shard_map/ppermute | solution.py:39
  6.5 11.6 %collective-permute-start.4 = (bf16[32,5120]{1,0:T(8,128)(2,1)}, bf16[32,5120]{1,0:T(8,128)(2,1)S(1)}, u32[]{:S(2)}, u32[]{:S(2)}) collective-permute-start(bf16[32,5120]{1,0:T(8,128)(2,1)} %get-tuple-element.28.one), channel_id=1, source_target_pairs={{0,24},{1,25},{2,26},{3,27},{4,28},{5,29},{6,30},{7,31},{8,0},{9,1... | collective-permute-start | bytes 983048 | tf_op jit(solution)/shard_map/ppermute | solution.py:39
  10.2 11.2 %collective-permute-start.3 = (bf16[32,5120]{1,0:T(8,128)(2,1)}, bf16[32,5120]{1,0:T(8,128)(2,1)S(1)}, u32[]{:S(2)}, u32[]{:S(2)}) collective-permute-start(bf16[32,5120]{1,0:T(8,128)(2,1)} %get-tuple-element.28.one), channel_id=1, source_target_pairs={{0,8},{1,9},{2,10},{3,11},{4,12},{5,13},{6,14},{7,15},{8,16},{9,17... | collective-permute-start | bytes 983048 | tf_op jit(solution)/shard_map/ppermute | solution.py:39
  18.3 10.1 %collective-permute-start.9 = (bf16[64,5120]{1,0:T(8,128)(2,1)S(1)}, bf16[64,5120]{1,0:T(8,128)(2,1)S(1)}, u32[]{:S(2)}, u32[]{:S(2)}) collective-permute-start(bf16[64,5120]{1,0:T(8,128)(2,1)S(1)} %shard_map.84.refs_1_), channel_id=1, source_target_pairs={{0,3},{1,0},{2,1},{3,2},{4,7},{5,4},{6,5},{7,6},{8,11},{9,8},{10,9... | collective-permute-start | bytes 1966088 | tf_op jit(solution)/shard_map/ppermute | solution.py:39
  22.4 11.0 %collective-permute-start.6 = (bf16[64,5120]{1,0:T(8,128)(2,1)S(1)}, bf16[64,5120]{1,0:T(8,128)(2,1)S(1)}, u32[]{:S(2)}, u32[]{:S(2)}) collective-permute-start(bf16[64,5120]{1,0:T(8,128)(2,1)S(1)} %shard_map.83.refs_0_), channel_id=1, source_target_pairs={{0,1},{1,2},{2,3},{3,0},{4,5},{5,6},{6,7},{7,4},{8,9},{9,10},{10,1... | collective-permute-start | bytes 1966088 | tf_op jit(solution)/shard_map/ppermute | solution.py:39
  23.4 17.0 %collective-permute-start.7 = (bf16[64,5120]{1,0:T(8,128)(2,1)S(1)}, bf16[64,5120]{1,0:T(8,128)(2,1)S(1)}, u32[]{:S(2)}, u32[]{:S(2)}) collective-permute-start(bf16[64,5120]{1,0:T(8,128)(2,1)S(1)} %shard_map.84.refs_1_), channel_id=1, source_target_pairs={{0,1},{1,2},{2,3},{3,0},{4,5},{5,6},{6,7},{7,4},{8,9},{9,10},{10,1... | collective-permute-start | bytes 1966088 | tf_op jit(solution)/shard_map/ppermute | solution.py:39
  24.6 15.8 %collective-permute-start.8 = (bf16[64,5120]{1,0:T(8,128)(2,1)S(1)}, bf16[64,5120]{1,0:T(8,128)(2,1)S(1)}, u32[]{:S(2)}, u32[]{:S(2)}) collective-permute-start(bf16[64,5120]{1,0:T(8,128)(2,1)S(1)} %shard_map.83.refs_0_), channel_id=1, source_target_pairs={{0,3},{1,0},{2,1},{3,2},{4,7},{5,4},{6,5},{7,6},{8,11},{9,8},{10,9... | collective-permute-start | bytes 1966088 | tf_op jit(solution)/shard_map/ppermute | solution.py:39
  40.5 8.2 %collective-permute-start.11 = (bf16[4,2560,128]{2,1,0:T(8,128)(2,1)S(1)}, bf16[4,2560,128]{2,1,0:T(8,128)(2,1)S(1)}, u32[]{:S(2)}, u32[]{:S(2)}) collective-permute-start(bf16[4,2560,128]{2,1,0:T(8,128)(2,1)S(1)} %shard_map.86.refs_7_.refs_3_.mine), channel_id=1, source_target_pairs={{0,32},{1,33},{2,34},{3,35},{4,36},{5,37},{6,38},{7,39},{8,40},{9,... | collective-permute-start | bytes 7864328 | tf_op jit(solution)/shard_map/ppermute | solution.py:39
  44.1 10.3 %collective-permute-start.13 = (bf16[64,5120]{1,0:T(8,128)(2,1)S(1)}, bf16[64,5120]{1,0:T(8,128)(2,1)S(1)}, u32[]{:S(2)}, u32[]{:S(2)}) collective-permute-start(bf16[64,5120]{1,0:T(8,128)(2,1)S(1)} %collective-permute-done.9.refs_3_.refs_5_), channel_id=1, source_target_pairs={{0,3},{1,0},{2,1},{3,2},{4,7},{5,4},{6,5},{7,6},{8,11},{9,8},{10,9... | collective-permute-start | bytes 1966088 | tf_op jit(solution)/shard_map/ppermute | solution.py:39
  46.9 10.7 %collective-permute-start.12 = (bf16[64,5120]{1,0:T(8,128)(2,1)S(1)}, bf16[64,5120]{1,0:T(8,128)(2,1)S(1)}, u32[]{:S(2)}, u32[]{:S(2)}) collective-permute-start(bf16[64,5120]{1,0:T(8,128)(2,1)S(1)} %collective-permute-done.6.refs_0_.refs_2_), channel_id=1, source_target_pairs={{0,1},{1,2},{2,3},{3,0},{4,5},{5,6},{6,7},{7,4},{8,9},{9,10},{10,1... | collective-permute-start | bytes 1966088 | tf_op jit(solution)/shard_map/ppermute | solution.py:39
  51.9 13.2 %collective-permute-start.14 = (bf16[384,512]{1,0:T(8,128)(2,1)S(1)}, bf16[384,512]{1,0:T(8,128)(2,1)S(1)}, u32[]{:S(2)}, u32[]{:S(2)}) collective-permute-start(bf16[384,512]{1,0:T(8,128)(2,1)S(1)} %get-tuple-element.30.refs_0_), channel_id=1, source_target_pairs={{0,4},{1,5},{2,6},{3,7},{4,0},{5,1},{6,2},{7,3},{8,12},{9,13},{10,... | collective-permute-start | bytes 1179656 | tf_op jit(solution)/shard_map/ppermute | solution.py:39
  66.5 11.1 %collective-permute-start.16 = (bf16[64,5120]{1,0:T(8,128)(2,1)S(1)}, bf16[64,5120]{1,0:T(8,128)(2,1)S(1)}, u32[]{:S(2)}, u32[]{:S(2)}) collective-permute-start(bf16[64,5120]{1,0:T(8,128)(2,1)S(1)} %get-tuple-element.38), channel_id=1, source_target_pairs={{0,1},{1,2},{2,3},{3,0},{4,5},{5,6},{6,7},{7,4},{8,9},{9,10},{10,1... | collective-permute-start | bytes 1966088 | tf_op jit(solution)/shard_map/ppermute | solution.py:39
  67.8 11.3 %collective-permute-start.17 = (bf16[64,5120]{1,0:T(8,128)(2,1)S(1)}, bf16[64,5120]{1,0:T(8,128)(2,1)S(1)}, u32[]{:S(2)}, u32[]{:S(2)}) collective-permute-start(bf16[64,5120]{1,0:T(8,128)(2,1)S(1)} %get-tuple-element.39), channel_id=1, source_target_pairs={{0,3},{1,0},{2,1},{3,2},{4,7},{5,4},{6,5},{7,6},{8,11},{9,8},{10,9... | collective-permute-start | bytes 1966088 | tf_op jit(solution)/shard_map/ppermute | solution.py:39
  69.4 10.0 %collective-permute-start = (f32[32,5120]{1,0:T(8,128)S(1)}, f32[32,5120]{1,0:T(8,128)S(1)}, u32[]{:S(2)}, u32[]{:S(2)}) collective-permute-start(f32[32,5120]{1,0:T(8,128)S(1)} %bitcast.5), channel_id=1, source_target_pairs={{0,32},{1,33},{2,34},{3,35},{4,36},{5,37},{6,38},{7,39},{8,40},{9,... | collective-permute-start | bytes 1966088 | tf_op jit(solution)/shard_map/ppermute | solution.py:39
  70.1 10.2 %collective-permute-start.1 = (f32[32,5120]{1,0:T(8,128)S(1)}, f32[32,5120]{1,0:T(8,128)S(1)}, u32[]{:S(2)}, u32[]{:S(2)}) collective-permute-start(f32[32,5120]{1,0:T(8,128)S(1)} %bitcast.6), channel_id=1, source_target_pairs={{0,64},{1,65},{2,66},{3,67},{4,68},{5,69},{6,70},{7,71},{8,72},{9,... | collective-permute-start | bytes 1966088 | tf_op jit(solution)/shard_map/ppermute | solution.py:39
  70.8 21.5 %collective-permute-start.2 = (f32[32,5120]{1,0:T(8,128)S(1)}, f32[32,5120]{1,0:T(8,128)S(1)}, u32[]{:S(2)}, u32[]{:S(2)}) collective-permute-start(f32[32,5120]{1,0:T(8,128)S(1)} %bitcast.7), channel_id=1, source_target_pairs={{0,96},{1,97},{2,98},{3,99},{4,100},{5,101},{6,102},{7,103},{8,104... | collective-permute-start | bytes 1966088 | tf_op jit(solution)/shard_map/ppermute | solution.py:39
  77.6 14.7 %collective-permute-start.19 = (bf16[64,5120]{1,0:T(8,128)(2,1)S(1)}, bf16[64,5120]{1,0:T(8,128)(2,1)S(1)}, u32[]{:S(2)}, u32[]{:S(2)}) collective-permute-start(bf16[64,5120]{1,0:T(8,128)(2,1)S(1)} %get-tuple-element.41), channel_id=1, source_target_pairs={{0,3},{1,0},{2,1},{3,2},{4,7},{5,4},{6,5},{7,6},{8,11},{9,8},{10,9... | collective-permute-start | bytes 1966088 | tf_op jit(solution)/shard_map/ppermute | solution.py:39
  79.1 13.3 %collective-permute-start.20 = (bf16[64,5120]{1,0:T(8,128)(2,1)S(1)}, bf16[64,5120]{1,0:T(8,128)(2,1)S(1)}, u32[]{:S(2)}, u32[]{:S(2)}) collective-permute-start(bf16[64,5120]{1,0:T(8,128)(2,1)S(1)} %get-tuple-element.42), channel_id=1, source_target_pairs={{0,1},{1,2},{2,3},{3,0},{4,5},{5,6},{6,7},{7,4},{8,9},{9,10},{10,1... | collective-permute-start | bytes 1966088 | tf_op jit(solution)/shard_map/ppermute | solution.py:39
  79.4 17.6 %collective-permute-start.18 = (bf16[64,5120]{1,0:T(8,128)(2,1)S(1)}, bf16[64,5120]{1,0:T(8,128)(2,1)S(1)}, u32[]{:S(2)}, u32[]{:S(2)}) collective-permute-start(bf16[64,5120]{1,0:T(8,128)(2,1)S(1)} %get-tuple-element.40), channel_id=1, source_target_pairs={{0,1},{1,2},{2,3},{3,0},{4,5},{5,6},{6,7},{7,4},{8,9},{9,10},{10,1... | collective-permute-start | bytes 1966088 | tf_op jit(solution)/shard_map/ppermute | solution.py:39
  80.3 16.7 %collective-permute-start.21 = (bf16[64,5120]{1,0:T(8,128)(2,1)S(1)}, bf16[64,5120]{1,0:T(8,128)(2,1)S(1)}, u32[]{:S(2)}, u32[]{:S(2)}) collective-permute-start(bf16[64,5120]{1,0:T(8,128)(2,1)S(1)} %get-tuple-element.43), channel_id=1, source_target_pairs={{0,3},{1,0},{2,1},{3,2},{4,7},{5,4},{6,5},{7,6},{8,11},{9,8},{10,9... | collective-permute-start | bytes 1966088 | tf_op jit(solution)/shard_map/ppermute | solution.py:39
  97.5 11.0 %collective-permute-start.22 = (bf16[32,5120]{1,0:T(8,128)(2,1)S(1)}, bf16[32,5120]{1,0:T(8,128)(2,1)S(1)}, u32[]{:S(2)}, u32[]{:S(2)}) collective-permute-start(bf16[32,5120]{1,0:T(8,128)(2,1)S(1)} %get-tuple-element.45), channel_id=1, source_target_pairs={{0,8},{1,9},{2,10},{3,11},{4,12},{5,13},{6,14},{7,15},{8,16},{9,17... | collective-permute-start | bytes 983048 | tf_op jit(solution)/shard_map/ppermute | solution.py:39
  97.6 10.9 %collective-permute-start.23 = (bf16[32,5120]{1,0:T(8,128)(2,1)S(1)}, bf16[32,5120]{1,0:T(8,128)(2,1)S(1)}, u32[]{:S(2)}, u32[]{:S(2)}) collective-permute-start(bf16[32,5120]{1,0:T(8,128)(2,1)S(1)} %get-tuple-element.46), channel_id=1, source_target_pairs={{0,24},{1,25},{2,26},{3,27},{4,28},{5,29},{6,30},{7,31},{8,0},{9,1... | collective-permute-start | bytes 983048 | tf_op jit(solution)/shard_map/ppermute | solution.py:39
  100.3 8.3 %collective-permute-start.24 = (bf16[32,5120]{1,0:T(8,128)(2,1)S(1)}, bf16[32,5120]{1,0:T(8,128)(2,1)S(1)}, u32[]{:S(2)}, u32[]{:S(2)}) collective-permute-start(bf16[32,5120]{1,0:T(8,128)(2,1)S(1)} %get-tuple-element.47), channel_id=1, source_target_pairs={{0,16},{1,17},{2,18},{3,19},{4,20},{5,21},{6,22},{7,23},{8,24},{9,... | collective-permute-start | bytes 983048 | tf_op jit(solution)/shard_map/ppermute | solution.py:39
  114.2 12.3 %collective-permute-start.26 = (bf16[32,5120]{1,0:T(8,128)(2,1)S(1)}, bf16[32,5120]{1,0:T(8,128)(2,1)S(1)}, u32[]{:S(2)}, u32[]{:S(2)}) collective-permute-start(bf16[32,5120]{1,0:T(8,128)(2,1)S(1)} %shard_map.95), channel_id=1, source_target_pairs={{0,64},{1,65},{2,66},{3,67},{4,68},{5,69},{6,70},{7,71},{8,72},{9,... | collective-permute-start | bytes 983048 | tf_op jit(solution)/shard_map/ppermute | solution.py:39
  (9 other events, 86.8 us)

commit v5 on v4

--- a/solution.py
+++ b/solution.py
@@ -67,8 +67,8 @@
     return (1, core, x, yl, z) if yh == 0 else None
 
 
-def from_first(yh_to, core_to):
-    return lambda yh, core, x, yl, z: (yh_to, core_to, x, yl, z) if yh == 0 and core == 0 else None
+def to_later_core(yh, core, x, yl, z):
+    return (0, 1, x, yl, z) if yh == 0 and core == 0 else None
 
 
 def modulate_kernel(index, state, scale, shift, gate, out, gates):
@@ -101,31 +101,41 @@
     )(index, state, scale, shift, gate)
 
 
-def pack_kernel(core, qkv, out, half):
-    del core
-    half[:3] = qkv[...]
-    for block in range(out.shape[1] // HDIM):
-        here = slice(block * HDIM, (block + 1) * HDIM)
-        half[3, here, :] = out[:, here]
-
-
-def pack(core, qkv_weight, out_weight):
+def pack_kernel(kinds, core, qkv, output, until, packed, sem):
+    half = packed.shape[1]
+    first = pl.multiple_of(core[0] * half, half)
+    copies = []
+    for place, kind in enumerate(kinds):
+        if kind < 3:
+            rows = qkv.at[kind, pl.ds(first, half), :]
+            copies.append(pltpu.make_async_copy(rows, packed.at[place], sem))
+        else:
+            for at in range(0, half, HDIM):
+                block = output.at[:, pl.ds(pl.multiple_of(first + at, HDIM), HDIM)]
+                copies.append(
+                    pltpu.make_async_copy(block, packed.at[place, pl.ds(at, HDIM), :], sem)
+                )
+    for copy in copies:
+        copy.start()
+    for copy in copies:
+        copy.wait()
+
+
+def pack(kinds, core, qkv_weight, out_weight, until):
     half = qkv_weight.shape[1] // 2
     return pl.pallas_call(
-        pack_kernel,
+        functools.partial(pack_kernel, kinds),
         grid_spec=pltpu.PrefetchScalarGridSpec(
             num_scalar_prefetch=1,
             grid=(1,),
-            in_specs=[
-                pl.BlockSpec((3, half, HDIM), lambda i, core: (0, core[0], 0)),
-                pl.BlockSpec((HDIM, half), lambda i, core: (0, core[0])),
-            ],
-            out_specs=pl.BlockSpec((4, half, HDIM), lambda i, core: (0, 0, 0)),
+            in_specs=[ANY] * 3,
+            out_specs=pl.BlockSpec((len(kinds), half, HDIM), lambda i, core: (0, 0, 0)),
+            scratch_shapes=[pltpu.SemaphoreType.DMA],
         ),
-        out_shape=jax.ShapeDtypeStruct((4, half, HDIM), BF16),
-        compiler_params=WIDE,
+        out_shape=jax.ShapeDtypeStruct((len(kinds), half, HDIM), BF16),
+        compiler_params=PARAMS,
         cost_estimate=pl.CostEstimate(flops=0, bytes_accessed=4000000, transcendentals=0),
-    )(core, qkv_weight, out_weight)
+    )(core, qkv_weight, out_weight, until)
 
 
 def stack_kernel(one, two, out):
@@ -160,42 +170,40 @@
     side(theirs, half - first)
 
 
-def project_kernel(count, rows, core, *refs):
+def project_kernel(count, kinds, rows, core, *refs):
     pieces, (own, mine, theirs) = refs[:count], refs[count : count + 3]
-    both_kv, queries, total = refs[count + 3], refs[count + 4 : -1], refs[-1]
+    outs, total = refs[count + 3 : -1], refs[-1]
     step, wide = 512, 2 * HDIM
     total[...] = jnp.zeros_like(total)
 
     def one(weight, at, column):
         left = jnp.concatenate([piece[:, pl.ds(column, step)] for piece in pieces], axis=0)
-        for kind in range(3):
+        for place, kind in enumerate(kinds):
             both = jnp.concatenate(
-                [own[kind, pl.ds(column, step), :], weight[kind, pl.ds(at, step), :]], axis=-1
+                [own[kind, pl.ds(column, step), :], weight[place, pl.ds(at, step), :]], axis=-1
             )
-            total[kind] += jnp.dot(left, both, preferred_element_type=F32)
+            total[place] += jnp.dot(left, both, preferred_element_type=F32)
 
     sides(core, mine, theirs, own.shape[1], step, one)
-    both_kv[:, :wide] = total[1].astype(BF16)
-    both_kv[:, wide:] = total[2].astype(BF16)
     at = 0
-    for out, size in zip(queries, rows):
-        out[...] = total[0, at : at + size].astype(BF16)
+    for out, size in zip(outs, rows):
+        for place in range(len(kinds)):
+            out[:, place * wide : (place + 1) * wide] = total[place, at : at + size].astype(BF16)
         at += size
 
 
-def project(core, pieces, weight, mine, theirs, rows):
+def project(core, kinds, pieces, weight, mine, theirs, rows):
     wide = 2 * HDIM
     tokens, depth = sum(rows), weight.shape[1]
     return pl.pallas_call(
-        functools.partial(project_kernel, len(pieces), rows),
-        out_shape=[jax.ShapeDtypeStruct((tokens, 2 * wide), BF16)]
-        + [jax.ShapeDtypeStruct((size, wide), BF16) for size in rows],
+        functools.partial(project_kernel, len(pieces), kinds, rows),
+        out_shape=[jax.ShapeDtypeStruct((size, len(kinds) * wide), BF16) for size in rows],
         in_specs=[SMEM] + [VMEM] * (len(pieces) + 3),
-        out_specs=[VMEM] * (1 + len(rows)),
-        scratch_shapes=[pltpu.VMEM((3, tokens, wide), F32)],
+        out_specs=[VMEM] * len(rows),
+        scratch_shapes=[pltpu.VMEM((len(kinds), tokens, wide), F32)],
         compiler_params=PARAMS,
         cost_estimate=pl.CostEstimate(
-            flops=6 * tokens * depth * wide, bytes_accessed=1000000, transcendentals=0
+            flops=2 * len(kinds) * tokens * depth * wide, bytes_accessed=1000000, transcendentals=0
         ),
     )(core, *pieces, weight, mine, theirs)
 
@@ -224,7 +232,7 @@
 
     def one(weight, at, column):
         blocks = [
-            weight[3, pl.ds(pl.multiple_of(at + i, HDIM), HDIM), :] for i in range(0, step, HDIM)
+            weight[1, pl.ds(pl.multiple_of(at + i, HDIM), HDIM), :] for i in range(0, step, HDIM)
         ]
         both = jnp.concatenate(
             [own[:, pl.ds(column, step)], jnp.concatenate(blocks, axis=1)], axis=0
@@ -283,63 +291,95 @@
     to_opposite[...] = total(near_high, high_1, high_2, slice(size, 2 * size)).astype(BF16)
 
 
-def split(parts, until):
+def split(*parts):
     size, width = parts[0].shape[0] // 2, parts[0].shape[1]
     return pl.pallas_call(
         split_kernel,
         out_shape=[jax.ShapeDtypeStruct((size, width), F32)]
         + [jax.ShapeDtypeStruct((size, width), BF16)] * 3,
-        in_specs=[VMEM] * 6 + [ANY] * len(until),
+        in_specs=[VMEM] * 6,
         out_specs=[VMEM] * 4,
         compiler_params=PARAMS,
-    )(*parts, *until)
-
-
-def drift_kernel(index, steps, total, one, two, three, gates, drift, term):
+    )(*parts)
+
+
+def drift_kernel(index, steps, total, one, two, three, gates, *refs):
+    drift, term = refs[-2:]
     moved = total[...] + one[...].astype(F32) + two[...].astype(F32) + three[...].astype(F32)
     result = steps[index[0]] * (gates[...] * moved)
     drift[...] = result
     term[...] = result.astype(BF16)
 
 
-def drifts(index, steps, total, arrived, gates):
+def drifts(index, steps, total, arrived, gates, *until):
     return pl.pallas_call(
         drift_kernel,
         out_shape=[
             jax.ShapeDtypeStruct(total.shape, F32),
             jax.ShapeDtypeStruct(total.shape, BF16),
         ],
-        in_specs=[SMEM] * 2 + [VMEM] * 5,
+        in_specs=[SMEM] * 2 + [VMEM] * 5 + [ANY] * len(until),
         out_specs=[VMEM] * 2,
         compiler_params=PARAMS,
-    )(index, steps, total, *arrived, gates)
-
-
-def both_kernel(drift, beside, term):
-    term[...] = (drift[...] + beside[...].astype(F32)).astype(BF16)
-
-
-def both_cores(drift, beside):
+    )(index, steps, total, *arrived, gates, *until)
+
+
+def own_rows(place, half):
+    return pl.ds(pl.multiple_of(lax.rem(place[0], 2) * half, half), half)
+
+
+def start_kernel(place, state, received, until, out):
+    rows = own_rows(place, out.shape[0])
+    out[...] = jnp.where(place[0] == 0, state[rows, :], received[rows, :])
+
+
+def start_half(place, state, received, until):
+    return pl.pallas_call(
+        start_kernel,
+        out_shape=jax.ShapeDtypeStruct((state.shape[0] // 2, state.shape[1]), F32),
+        in_specs=[SMEM] + [VMEM] * 2 + [ANY],
+        out_specs=VMEM,
+        compiler_params=PARAMS,
+    )(place, state, received, until)
+
+
+def both_kernel(place, drift, beside, out):
+    rows = own_rows(place, out.shape[0])
+    out[...] = (drift[rows, :] + beside[rows, :].astype(F32)).astype(BF16)
+
+
+def both_half(place, drift, beside):
     return pl.pallas_call(
         both_kernel,
-        out_shape=jax.ShapeDtypeStruct(drift.shape, BF16),
-        in_specs=[VMEM] * 2,
+        out_shape=jax.ShapeDtypeStruct((drift.shape[0] // 2, drift.shape[1]), BF16),
+        in_specs=[SMEM] + [VMEM] * 2,
         out_specs=VMEM,
         compiler_params=PARAMS,
-    )(drift, beside)
-
-
-def finish_kernel(place, start, one, two, three, drift, beside, earlier, out):
-    first = jnp.where(place[0] == 0, start[...], one[...] + two[...] + three[...])
-    on_second = jnp.where(lax.rem(place[0], 2) == 1, beside[...].astype(F32), 0.0)
-    out[...] = first + (drift[...] + on_second + earlier[...].astype(F32))
+    )(place, drift, beside)
+
+
+def finish_kernel(place, state, near_start, own_start, far_start, drift, beside, own_sum, far_sum, out):
+    half = own_sum.shape[0]
+    second = lax.rem(place[0], 2)
+    summed = drift[...] + jnp.where(second == 1, beside[...].astype(F32), 0.0)
+
+    @pl.when(place[0] < 2)
+    def _():
+        out[...] = jnp.where(place[0] == 0, state[...], near_start[...]) + summed
+
+    @pl.when(place[0] >= 2)
+    def _():
+        for which, start, earlier in ((0, own_start, own_sum), (1, far_start, far_sum)):
+            rows = pl.ds(pl.multiple_of(lax.rem(second + which, 2) * half, half), half)
+            out[rows, :] = start[...] + earlier[...].astype(F32)
+        out[...] += summed
 
 
 def finish(place, *parts):
     return pl.pallas_call(
         finish_kernel,
         out_shape=jax.ShapeDtypeStruct(parts[0].shape, F32),
-        in_specs=[SMEM] + [VMEM] * 7,
+        in_specs=[SMEM] + [VMEM] * 8,
         out_specs=VMEM,
         compiler_params=PARAMS,
     )(place, *parts)
@@ -367,28 +407,42 @@
     core = group & 1
     place, core, index = group[None], core[None], window_start + group
     state = trajectory[0]
-    mine = send(pack(core, qkv_weight, out_weight), to_both_sides)
     modulated, gates = modulate(index, state, scale_table, shift_table, gate_table)
+    near_start = send(state, to_later_core)
     minus, plus, opposite = [send(modulated, first_axis(s)) for s in (1, -1, 2)]
     near_low = stack(modulated, minus)
     before_low, after_low = send(near_low, second_axis(1)), send(near_low, second_axis(-1))
     near_high = stack(plus, opposite)
     after_high, before_high = send(near_high, second_axis(-1)), send(near_high, second_axis(1))
-    last_low, last_high = send(before_low, second_axis(1)), send(after_high, second_axis(-1))
+    kv_mine = send(pack((1, 2), core, qkv_weight, out_weight, modulated), to_both_sides)
+    qo_mine = send(pack((0, 3), core, qkv_weight, out_weight, modulated), to_both_sides)
+    last_low = send(hold(before_low, before_high, after_low), second_axis(1))
+    last_high = send(hold(after_high, before_high, after_low), second_axis(-1))
 
     size = near_low.shape[0]
     near = [near_low, near_high]
     side = [before_low, before_high, after_low, after_high]
     last = [last_low, last_high]
-    mine = hold(mine, *side)
-    weights = (qkv_weight, mine, send(mine, to_other_core))
-    first_kv, near_q, side_q = project(core, near + side, *weights, [2 * size, 4 * size])
-    last_kv, last_q = project(core, last, *weights, [2 * size])
+    kv_mine = hold(kv_mine, near_low, near_high)
+    kv_weights = (qkv_weight, kv_mine, send(kv_mine, to_other_core))
+    qo_theirs = send(qo_mine, to_other_core)
+    (first_kv,) = project(core, (1, 2), near + side, *kv_weights, [6 * size])
+    (last_kv,) = project(core, (1, 2), last, *kv_weights, [2 * size])
     kv = [first_kv, last_kv]
     far = [send(value, to_partner) for value in kv]
-
-    outs = (out_weight, *weights[1:])
+    near_q, side_q, last_q = project(
+        core,
+        (0,),
+        near + side + last,
+        qkv_weight,
+        qo_mine,
+        qo_theirs,
+        [2 * size, 4 * size, 2 * size],
+    )
+
+    outs = (out_weight, qo_mine, qo_theirs)
     last_low, last_high = attend(core, last_q, kv, far, *outs, [size] * 2)
+    own_start = send(start_half(place, state, near_start, last_low), to_later_half)
     from_low, from_high = send(last_low, second_axis(1)), send(last_high, second_axis(-1))
     before_low, before_high, after_low, after_high = attend(
         core, side_q, kv, far, *outs, [size] * 4
@@ -397,17 +451,20 @@
     near_low, near_high = attend(core, near_q, kv, far, *outs, [size] * 2)
     after_low, before_high = join(after_low, before_high, from_low, from_high)
     low_1, high_2 = send(after_low, second_axis(1)), send(before_high, second_axis(-1))
-    starts = [send(state, from_first(*to)) for to in ((0, 1), (1, 0), (1, 1))]
     total, to_minus, to_plus, to_opposite = split(
-        [near_low, near_high, low_1, low_2, high_1, high_2], starts
+        near_low, near_high, low_1, low_2, high_1, high_2
     )
     arrived = [
         send(value, first_axis(s)) for value, s in ((to_plus, 1), (to_minus, -1), (to_opposite, 2))
     ]
-    drift, term = drifts(index, step_sizes, total, arrived, gates)
+    far_start = send(own_start, to_other_core)
+    drift, term = drifts(index, step_sizes, total, arrived, gates, far_start)
     beside = send(term, to_other_core)
-    earlier = send(both_cores(drift, beside), to_later_half)
-    return finish(place, state, *starts, drift, beside, earlier)[None]
+    own_sum = send(both_half(place, drift, beside), to_later_half)
+    far_sum = send(own_sum, to_other_core)
+    return finish(
+        place, state, near_start, own_start, far_start, drift, beside, own_sum, far_sum
+    )[None]
 
 
 def solution(mesh):

time: 128 us -> 118 us (0.922)
  waiting for transfers between devices: 72.3 us -> 55.8 us
  starting transfers between devices: 36.1 us -> 43.1 us
    ppermute x27 -> x30, waiting for transfers between devices: 72.3 us -> 55.8 us  [send(): return lax.ppermute(value, ('tm', 'seq'), moves(rule))]
    ppermute x27 -> x30, starting transfers between devices: 36.1 us -> 43.1 us  [send(): return lax.ppermute(value, ('tm', 'seq'), moves(rule))]
    pallas_call x4 -> x7, Pallas kernels: 7.89 us -> 5.58 us  [the longest x3 4.68 us: project(): pl.pallas_call(functools.partial(project_kernel, len(pieces), kinds, rows...]
  transfers between devices with their start and end apart: 27 -> 30, of which waited for: 16 -> 17; matrix products, arithmetic and copies ran while one was open for 0% -> 0% of each run, Pallas kernels for 8% -> 9%
where the time goes in v5:
time: 118 us
  waiting for transfers between devices  55.8 us (47%)
  starting transfers between devices  43.1 us (37%)
  Pallas kernels  16.3 us (14%)
  local copies, waits for them, and re-layouts  1.51 us (1%)
    ppermute x30, waiting for transfers between devices, send(): return lax.ppermute(value, ('tm', 'seq'), moves(rule))  55.8 us
    ppermute x30, starting transfers between devices, send(): return lax.ppermute(value, ('tm', 'seq'), moves(rule))  43.1 us
    pallas_call x3, Pallas kernels, project(): pl.pallas_call(functools.partial(project_kernel, len(pieces), kinds, rows...  4.68 us
    pallas_call x3, Pallas kernels, attend(): pl.pallas_call(functools.partial(attend_kernel, len(near), cuts), out_sha...  4.65 us
    pallas_call x1, Pallas kernels, modulate(): pl.pallas_call(modulate_kernel, grid_spec=pltpu.PrefetchScalarGridSpec(nu...  2.39 us
  transfers between devices with their start and end apart: 30, of which 17 were waited for; matrix products, arithmetic and copies ran while one was open for 0% of the time, Pallas kernels for 9%

profile of v5, /device:TPU:17, one launch (start us, length us, event | category | flops | bytes accessed | tf_op | source)
XLA Modules:
  0.0 117.7 jit_solution(1647334656100033814)
XLA Ops:
  0.7 2.4 %shard_map.82 = (bf16[32,5120]{1,0:T(8,128)(2,1)}, f32[1,5120]{1,0:T(1,128)}) custom-call(s32[1]{0:T(128)S(6)} %add.4.index, f32[32,5120]{1,0:T(8,128)} %bitcast.4, f32[50,5120]{1,0:T(8,128)} %scale.1, f32[50,5120]{1,0:T(8,128)} %shift.1, f32[50,5120]{1,0:T(8,128)} %gate.1), custom_call_target="tpu_custom_call" | custom-call | flops 1000000 | bytes 2000000 | tf_op jit(solution)/shard_map/pallas_call | solution.py:87
  6.9 3.8 %collective-permute-start.2 = (bf16[32,5120]{1,0:T(8,128)(2,1)}, bf16[32,5120]{1,0:T(8,128)(2,1)S(1)}, u32[]{:S(2)}, u32[]{:S(2)}) collective-permute-start(bf16[32,5120]{1,0:T(8,128)(2,1)} %get-tuple-element.26.one.until), channel_id=1, source_target_pairs={{0,24},{1,25},{2,26},{3,27},{4,28},{5,29},{6,30},{7,31},{8,0},{9,1... | collective-permute-start | bytes 983048 | tf_op jit(solution)/shard_map/ppermute | solution.py:39
  11.4 7.1 %collective-permute-done.2.one = bf16[32,5120]{1,0:T(8,128)(2,1)S(1)} collective-permute-done((bf16[32,5120]{1,0:T(8,128)(2,1)}, bf16[32,5120]{1,0:T(8,128)(2,1)S(1)}, u32[]{:S(2)}, u32[]{:S(2)}) %collective-permute-start.2) | collective-permute-done | bytes 327712 | tf_op jit(solution)/shard_map/ppermute | solution.py:39
  18.7 2.4 %collective-permute-start.7 = (bf16[64,5120]{1,0:T(8,128)(2,1)S(1)}, bf16[64,5120]{1,0:T(8,128)(2,1)S(1)}, u32[]{:S(2)}, u32[]{:S(2)}) collective-permute-start(bf16[64,5120]{1,0:T(8,128)(2,1)S(1)} %shard_map.84.refs_1_), channel_id=1, source_target_pairs={{0,3},{1,0},{2,1},{3,2},{4,7},{5,4},{6,5},{7,6},{8,11},{9,8},{10,9... | collective-permute-start | bytes 1966088 | tf_op jit(solution)/shard_map/ppermute | solution.py:39
  22.9 2.2 %collective-permute-start.13 = (bf16[2,2560,128]{2,1,0:T(8,128)(2,1)S(1)}, bf16[2,2560,128]{2,1,0:T(8,128)(2,1)S(1)}, u32[]{:S(2)}, u32[]{:S(2)}) collective-permute-start(bf16[2,2560,128]{2,1,0:T(8,128)(2,1)S(1)} %shard_map.90.refs_7_.refs_3_), channel_id=1, source_target_pairs={{0,32},{1,33},{2,34},{3,35},{4,36},{5,37},{6,38},{7,39},{8,40},{9,... | collective-permute-start | bytes 3932168 | tf_op jit(solution)/shard_map/ppermute | solution.py:39
  26.4 1.6 %collective-permute-start.6 = (bf16[64,5120]{1,0:T(8,128)(2,1)S(1)}, bf16[64,5120]{1,0:T(8,128)(2,1)S(1)}, u32[]{:S(2)}, u32[]{:S(2)}) collective-permute-start(bf16[64,5120]{1,0:T(8,128)(2,1)S(1)} %shard_map.83.refs_0_), channel_id=1, source_target_pairs={{0,3},{1,0},{2,1},{3,2},{4,7},{5,4},{6,5},{7,6},{8,11},{9,8},{10,9... | collective-permute-start | bytes 1966088 | tf_op jit(solution)/shard_map/ppermute | solution.py:39
  29.6 6.2 %collective-permute-done.10.refs_9_.mine = bf16[2,2560,128]{2,1,0:T(8,128)(2,1)S(1)} collective-permute-done((bf16[2,2560,128]{2,1,0:T(8,128)(2,1)S(1)}, bf16[2,2560,128]{2,1,0:T(8,128)(2,1)S(1)}, u32[]{:S(2)}, u32[]{:S(2)}) %collective-permute-start.10) | collective-permute-done | bytes 1310752 | tf_op jit(solution)/shard_map/ppermute | solution.py:39
  35.8 1.5 %collective-permute-start.11 = (bf16[2,2560,128]{2,1,0:T(8,128)(2,1)S(1)}, bf16[2,2560,128]{2,1,0:T(8,128)(2,1)S(1)}, u32[]{:S(2)}, u32[]{:S(2)}) collective-permute-start(bf16[2,2560,128]{2,1,0:T(8,128)(2,1)S(1)} %collective-permute-done.10.refs_9_.mine), channel_id=1, source_target_pairs={{0,32},{1,33},{2,34},{3,35},{4,36},{5,37},{6,38},{7,39},{8,40},{9,... | collective-permute-start | bytes 3932168 | tf_op jit(solution)/shard_map/ppermute | solution.py:39
  37.4 2.5 %collective-permute-start.9 = (bf16[64,5120]{1,0:T(8,128)(2,1)S(1)}, bf16[64,5120]{1,0:T(8,128)(2,1)S(1)}, u32[]{:S(2)}, u32[]{:S(2)}) collective-permute-start(bf16[64,5120]{1,0:T(8,128)(2,1)S(1)} %shard_map.86), channel_id=1, source_target_pairs={{0,3},{1,0},{2,1},{3,2},{4,7},{5,4},{6,5},{7,6},{8,11},{9,8},{10,9... | collective-permute-start | bytes 1966088 | tf_op jit(solution)/shard_map/ppermute | solution.py:39
  39.9 3.3 %collective-permute-done.4.refs_2_ = bf16[64,5120]{1,0:T(8,128)(2,1)S(1)} collective-permute-done((bf16[64,5120]{1,0:T(8,128)(2,1)S(1)}, bf16[64,5120]{1,0:T(8,128)(2,1)S(1)}, u32[]{:S(2)}, u32[]{:S(2)}) %collective-permute-start.4) | collective-permute-done | bytes 655392 | tf_op jit(solution)/shard_map/ppermute | solution.py:39
  43.4 2.3 %shard_map.91.refs_0_ = bf16[384,512]{1,0:T(8,128)(2,1)S(1)} custom-call(s32[1]{0:T(128)} %bitcast.2.core, bf16[64,5120]{1,0:T(8,128)(2,1)S(1)} %shard_map.83.refs_0_, bf16[64,5120]{1,0:T(8,128)(2,1)S(1)} %shard_map.84.refs_1_, bf16[64,5120]{1,0:T(8,128)(2,1)S(1)} %collective-permute-done.4.refs_2_, ...), custom_call_target="tpu_custom_call" | custom-call | flops 2013265920 | bytes 1000000 | tf_op jit(solution)/shard_map/pallas_call | solution.py:198
  47.4 6.9 %collective-permute-done.8.refs_6_.refs_0_ = bf16[64,5120]{1,0:T(8,128)(2,1)S(1)} collective-permute-done((bf16[64,5120]{1,0:T(8,128)(2,1)S(1)}, bf16[64,5120]{1,0:T(8,128)(2,1)S(1)}, u32[]{:S(2)}, u32[]{:S(2)}) %collective-permute-start.8) | collective-permute-done | bytes 655392 | tf_op jit(solution)/shard_map/ppermute | solution.py:39
  56.3 1.5 %shard_map.88 = (bf16[128,256]{1,0:T(8,128)(2,1)S(1)}, bf16[256,256]{1,0:T(8,128)(2,1)S(1)}, bf16[128,256]{1,0:T(8,128)(2,1)S(1)}) custom-call(s32[1]{0:T(128)} %bitcast.2.core, bf16[64,5120]{1,0:T(8,128)(2,1)S(1)} %shard_map.83.refs_0_, bf16[64,5120]{1,0:T(8,128)(2,1)S(1)} %shard_map.84.refs_1_, bf16[64,5120]{1,0:T(8,128)(2,1)S(1)} %collective-permute-done.4.refs_2_, ...), custom_call_target="tpu_custom_call" | custom-call | flops 1342177280 | bytes 1000000 | tf_op jit(solution)/shard_map/pallas_call | solution.py:198
  60.5 2.7 %collective-permute-start.19 = (bf16[64,5120]{1,0:T(8,128)(2,1)S(1)}, bf16[64,5120]{1,0:T(8,128)(2,1)S(1)}, u32[]{:S(2)}, u32[]{:S(2)}) collective-permute-start(bf16[64,5120]{1,0:T(8,128)(2,1)S(1)} %get-tuple-element.35), channel_id=1, source_target_pairs={{0,3},{1,0},{2,1},{3,2},{4,7},{5,4},{6,5},{7,6},{8,11},{9,8},{10,9... | collective-permute-start | bytes 1966088 | tf_op jit(solution)/shard_map/ppermute | solution.py:39
  64.1 2.0 %shard_map.96 = (bf16[64,5120]{1,0:T(8,128)(2,1)S(1)}, bf16[64,5120]{1,0:T(8,128)(2,1)S(1)}, bf16[64,5120]{1,0:T(8,128)(2,1)S(1)}, bf16[64,5120]{1,0:T(8,128)(2,1)S(1)}) custom-call(s32[1]{0:T(128)} %bitcast.2.core, bf16[256,256]{1,0:T(8,128)(2,1)S(1)} %get-tuple-element.32.queries, bf16[128,5120]{1,0:T(8,128)(2,1)S(1)} %copy-done.2, ...), custom_call_target="tpu_custom_call" | custom-call | flops 939524096 | bytes 1000000 | tf_op jit(solution)/shard_map/pallas_call | solution.py:252
  67.6 3.9 %collective-permute-done.18.low = bf16[64,5120]{1,0:T(8,128)(2,1)S(1)} collective-permute-done((bf16[64,5120]{1,0:T(8,128)(2,1)S(1)}, bf16[64,5120]{1,0:T(8,128)(2,1)S(1)}, u32[]{:S(2)}, u32[]{:S(2)}) %collective-permute-start.18) | collective-permute-done | bytes 655392 | tf_op jit(solution)/shard_map/ppermute | solution.py:39
  71.9 2.7 %collective-permute-start.23 = (bf16[64,5120]{1,0:T(8,128)(2,1)S(1)}, bf16[64,5120]{1,0:T(8,128)(2,1)S(1)}, u32[]{:S(2)}, u32[]{:S(2)}) collective-permute-start(bf16[64,5120]{1,0:T(8,128)(2,1)S(1)} %get-tuple-element.39), channel_id=1, source_target_pairs={{0,3},{1,0},{2,1},{3,2},{4,7},{5,4},{6,5},{7,6},{8,11},{9,8},{10,9... | collective-permute-start | bytes 1966088 | tf_op jit(solution)/shard_map/ppermute | solution.py:39
  77.3 7.0 %collective-permute-done.16.own_start = f32[16,5120]{1,0:T(8,128)S(1)} collective-permute-done((f32[16,5120]{1,0:T(8,128)S(1)}, f32[16,5120]{1,0:T(8,128)S(1)}, u32[]{:S(2)}, u32[]{:S(2)}) %collective-permute-start.16) | collective-permute-done | bytes 327712 | tf_op jit(solution)/shard_map/ppermute | solution.py:39
  84.3 5.4 %collective-permute-start.17 = (f32[16,5120]{1,0:T(8,128)S(1)}, f32[16,5120]{1,0:T(8,128)S(1)}, u32[]{:S(2)}, u32[]{:S(2)}) collective-permute-start(f32[16,5120]{1,0:T(8,128)S(1)} %collective-permute-done.16.own_start), channel_id=1, source_target_pairs={{0,32},{1,33},{2,34},{3,35},{4,36},{5,37},{6,38},{7,39},{8,40},{9,... | collective-permute-start | bytes 983048 | tf_op jit(solution)/shard_map/ppermute | solution.py:39
  90.2 2.7 %collective-permute-start.25 = (bf16[32,5120]{1,0:T(8,128)(2,1)S(1)}, bf16[32,5120]{1,0:T(8,128)(2,1)S(1)}, u32[]{:S(2)}, u32[]{:S(2)}) collective-permute-start(bf16[32,5120]{1,0:T(8,128)(2,1)S(1)} %get-tuple-element.42), channel_id=1, source_target_pairs={{0,24},{1,25},{2,26},{3,27},{4,28},{5,29},{6,30},{7,31},{8,0},{9,1... | collective-permute-start | bytes 983048 | tf_op jit(solution)/shard_map/ppermute | solution.py:39
  93.4 4.3 %collective-permute-done.24.one = bf16[32,5120]{1,0:T(8,128)(2,1)S(1)} collective-permute-done((bf16[32,5120]{1,0:T(8,128)(2,1)S(1)}, bf16[32,5120]{1,0:T(8,128)(2,1)S(1)}, u32[]{:S(2)}, u32[]{:S(2)}) %collective-permute-start.24) | collective-permute-done | bytes 327712 | tf_op jit(solution)/shard_map/ppermute | solution.py:39
  97.6 2.8 %collective-permute-done.25.two = bf16[32,5120]{1,0:T(8,128)(2,1)S(1)} collective-permute-done((bf16[32,5120]{1,0:T(8,128)(2,1)S(1)}, bf16[32,5120]{1,0:T(8,128)(2,1)S(1)}, u32[]{:S(2)}, u32[]{:S(2)}) %collective-permute-start.25) | collective-permute-done | bytes 327712 | tf_op jit(solution)/shard_map/ppermute | solution.py:39
  102.2 2.0 %collective-permute-start.27 = (bf16[32,5120]{1,0:T(8,128)(2,1)S(1)}, bf16[32,5120]{1,0:T(8,128)(2,1)S(1)}, u32[]{:S(2)}, u32[]{:S(2)}) collective-permute-start(bf16[32,5120]{1,0:T(8,128)(2,1)S(1)} %get-tuple-element.46), channel_id=1, source_target_pairs={{0,32},{1,33},{2,34},{3,35},{4,36},{5,37},{6,38},{7,39},{8,40},{9,... | collective-permute-start | bytes 983048 | tf_op jit(solution)/shard_map/ppermute | solution.py:39
  106.8 7.5 %collective-permute-done.28.own_sum = bf16[16,5120]{1,0:T(8,128)(2,1)S(1)} collective-permute-done((bf16[16,5120]{1,0:T(8,128)(2,1)S(1)}, bf16[16,5120]{1,0:T(8,128)(2,1)S(1)}, u32[]{:S(2)}, u32[]{:S(2)}) %collective-permute-start.28) | collective-permute-done | bytes 163872 | tf_op jit(solution)/shard_map/ppermute | solution.py:39
  (70 shorter events, 30.3 us)
Async XLA Ops:
  4.9 18.0 %collective-permute-start.12 = (bf16[2,2560,128]{2,1,0:T(8,128)(2,1)S(1)}, bf16[2,2560,128]{2,1,0:T(8,128)(2,1)S(1)}, u32[]{:S(2)}, u32[]{:S(2)}) collective-permute-start(bf16[2,2560,128]{2,1,0:T(8,128)(2,1)S(1)} %shard_map.89), channel_id=1, source_target_pairs={{0,4},{1,5},{2,6},{3,7},{4,0},{5,1},{6,2},{7,3},{8,12},{9,13},{10,... | collective-permute-start | bytes 3932168 | tf_op jit(solution)/shard_map/ppermute | solution.py:39
  5.6 30.2 %collective-permute-start.10 = (bf16[2,2560,128]{2,1,0:T(8,128)(2,1)S(1)}, bf16[2,2560,128]{2,1,0:T(8,128)(2,1)S(1)}, u32[]{:S(2)}, u32[]{:S(2)}) collective-permute-start(bf16[2,2560,128]{2,1,0:T(8,128)(2,1)S(1)} %shard_map.87), channel_id=1, source_target_pairs={{0,4},{1,5},{2,6},{3,7},{4,0},{5,1},{6,2},{7,3},{8,12},{9,13},{10,... | collective-permute-start | bytes 3932168 | tf_op jit(solution)/shard_map/ppermute | solution.py:39
  6.9 11.6 %collective-permute-start.2 = (bf16[32,5120]{1,0:T(8,128)(2,1)}, bf16[32,5120]{1,0:T(8,128)(2,1)S(1)}, u32[]{:S(2)}, u32[]{:S(2)}) collective-permute-start(bf16[32,5120]{1,0:T(8,128)(2,1)} %get-tuple-element.26.one.until), channel_id=1, source_target_pairs={{0,24},{1,25},{2,26},{3,27},{4,28},{5,29},{6,30},{7,31},{8,0},{9,1... | collective-permute-start | bytes 983048 | tf_op jit(solution)/shard_map/ppermute | solution.py:39
  10.7 11.2 %collective-permute-start.1 = (bf16[32,5120]{1,0:T(8,128)(2,1)}, bf16[32,5120]{1,0:T(8,128)(2,1)S(1)}, u32[]{:S(2)}, u32[]{:S(2)}) collective-permute-start(bf16[32,5120]{1,0:T(8,128)(2,1)} %get-tuple-element.26.one.until), channel_id=1, source_target_pairs={{0,8},{1,9},{2,10},{3,11},{4,12},{5,13},{6,14},{7,15},{8,16},{9,17... | collective-permute-start | bytes 983048 | tf_op jit(solution)/shard_map/ppermute | solution.py:39
  18.7 10.0 %collective-permute-start.7 = (bf16[64,5120]{1,0:T(8,128)(2,1)S(1)}, bf16[64,5120]{1,0:T(8,128)(2,1)S(1)}, u32[]{:S(2)}, u32[]{:S(2)}) collective-permute-start(bf16[64,5120]{1,0:T(8,128)(2,1)S(1)} %shard_map.84.refs_1_), channel_id=1, source_target_pairs={{0,3},{1,0},{2,1},{3,2},{4,7},{5,4},{6,5},{7,6},{8,11},{9,8},{10,9... | collective-permute-start | bytes 1966088 | tf_op jit(solution)/shard_map/ppermute | solution.py:39
  22.9 20.5 %collective-permute-start.13 = (bf16[2,2560,128]{2,1,0:T(8,128)(2,1)S(1)}, bf16[2,2560,128]{2,1,0:T(8,128)(2,1)S(1)}, u32[]{:S(2)}, u32[]{:S(2)}) collective-permute-start(bf16[2,2560,128]{2,1,0:T(8,128)(2,1)S(1)} %shard_map.90.refs_7_.refs_3_), channel_id=1, source_target_pairs={{0,32},{1,33},{2,34},{3,35},{4,36},{5,37},{6,38},{7,39},{8,40},{9,... | collective-permute-start | bytes 3932168 | tf_op jit(solution)/shard_map/ppermute | solution.py:39
  25.1 12.2 %collective-permute-start.5 = (bf16[64,5120]{1,0:T(8,128)(2,1)S(1)}, bf16[64,5120]{1,0:T(8,128)(2,1)S(1)}, u32[]{:S(2)}, u32[]{:S(2)}) collective-permute-start(bf16[64,5120]{1,0:T(8,128)(2,1)S(1)} %shard_map.84.refs_1_), channel_id=1, source_target_pairs={{0,1},{1,2},{2,3},{3,0},{4,5},{5,6},{6,7},{7,4},{8,9},{9,10},{10,1... | collective-permute-start | bytes 1966088 | tf_op jit(solution)/shard_map/ppermute | solution.py:39
  26.4 11.0 %collective-permute-start.6 = (bf16[64,5120]{1,0:T(8,128)(2,1)S(1)}, bf16[64,5120]{1,0:T(8,128)(2,1)S(1)}, u32[]{:S(2)}, u32[]{:S(2)}) collective-permute-start(bf16[64,5120]{1,0:T(8,128)(2,1)S(1)} %shard_map.83.refs_0_), channel_id=1, source_target_pairs={{0,3},{1,0},{2,1},{3,2},{4,7},{5,4},{6,5},{7,6},{8,11},{9,8},{10,9... | collective-permute-start | bytes 1966088 | tf_op jit(solution)/shard_map/ppermute | solution.py:39
  28.7 14.6 %collective-permute-start.4 = (bf16[64,5120]{1,0:T(8,128)(2,1)S(1)}, bf16[64,5120]{1,0:T(8,128)(2,1)S(1)}, u32[]{:S(2)}, u32[]{:S(2)}) collective-permute-start(bf16[64,5120]{1,0:T(8,128)(2,1)S(1)} %shard_map.83.refs_0_), channel_id=1, source_target_pairs={{0,1},{1,2},{2,3},{3,0},{4,5},{5,6},{6,7},{7,4},{8,9},{9,10},{10,1... | collective-permute-start | bytes 1966088 | tf_op jit(solution)/shard_map/ppermute | solution.py:39
  35.8 20.5 %collective-permute-start.11 = (bf16[2,2560,128]{2,1,0:T(8,128)(2,1)S(1)}, bf16[2,2560,128]{2,1,0:T(8,128)(2,1)S(1)}, u32[]{:S(2)}, u32[]{:S(2)}) collective-permute-start(bf16[2,2560,128]{2,1,0:T(8,128)(2,1)S(1)} %collective-permute-done.10.refs_9_.mine), channel_id=1, source_target_pairs={{0,32},{1,33},{2,34},{3,35},{4,36},{5,37},{6,38},{7,39},{8,40},{9,... | collective-permute-start | bytes 3932168 | tf_op jit(solution)/shard_map/ppermute | solution.py:39
  37.4 10.1 %collective-permute-start.9 = (bf16[64,5120]{1,0:T(8,128)(2,1)S(1)}, bf16[64,5120]{1,0:T(8,128)(2,1)S(1)}, u32[]{:S(2)}, u32[]{:S(2)}) collective-permute-start(bf16[64,5120]{1,0:T(8,128)(2,1)S(1)} %shard_map.86), channel_id=1, source_target_pairs={{0,3},{1,0},{2,1},{3,2},{4,7},{5,4},{6,5},{7,6},{8,11},{9,8},{10,9... | collective-permute-start | bytes 1966088 | tf_op jit(solution)/shard_map/ppermute | solution.py:39
  43.3 11.0 %collective-permute-start.8 = (bf16[64,5120]{1,0:T(8,128)(2,1)S(1)}, bf16[64,5120]{1,0:T(8,128)(2,1)S(1)}, u32[]{:S(2)}, u32[]{:S(2)}) collective-permute-start(bf16[64,5120]{1,0:T(8,128)(2,1)S(1)} %shard_map.85), channel_id=1, source_target_pairs={{0,1},{1,2},{2,3},{3,0},{4,5},{5,6},{6,7},{7,4},{8,9},{9,10},{10,1... | collective-permute-start | bytes 1966088 | tf_op jit(solution)/shard_map/ppermute | solution.py:39
  45.7 13.4 %collective-permute-start.14 = (bf16[384,512]{1,0:T(8,128)(2,1)S(1)}, bf16[384,512]{1,0:T(8,128)(2,1)S(1)}, u32[]{:S(2)}, u32[]{:S(2)}) collective-permute-start(bf16[384,512]{1,0:T(8,128)(2,1)S(1)} %shard_map.91.refs_0_), channel_id=1, source_target_pairs={{0,4},{1,5},{2,6},{3,7},{4,0},{5,1},{6,2},{7,3},{8,12},{9,13},{10,... | collective-permute-start | bytes 1179656 | tf_op jit(solution)/shard_map/ppermute | solution.py:39
  60.5 11.0 %collective-permute-start.18 = (bf16[64,5120]{1,0:T(8,128)(2,1)S(1)}, bf16[64,5120]{1,0:T(8,128)(2,1)S(1)}, u32[]{:S(2)}, u32[]{:S(2)}) collective-permute-start(bf16[64,5120]{1,0:T(8,128)(2,1)S(1)} %get-tuple-element.28.until), channel_id=1, source_target_pairs={{0,1},{1,2},{2,3},{3,0},{4,5},{5,6},{6,7},{7,4},{8,9},{9,10},{10,1... | collective-permute-start | bytes 1966088 | tf_op jit(solution)/shard_map/ppermute | solution.py:39
  60.5 10.9 %collective-permute-start.19 = (bf16[64,5120]{1,0:T(8,128)(2,1)S(1)}, bf16[64,5120]{1,0:T(8,128)(2,1)S(1)}, u32[]{:S(2)}, u32[]{:S(2)}) collective-permute-start(bf16[64,5120]{1,0:T(8,128)(2,1)S(1)} %get-tuple-element.35), channel_id=1, source_target_pairs={{0,3},{1,0},{2,1},{3,2},{4,7},{5,4},{6,5},{7,6},{8,11},{9,8},{10,9... | collective-permute-start | bytes 1966088 | tf_op jit(solution)/shard_map/ppermute | solution.py:39
  63.2 11.4 %collective-permute-start = (f32[32,5120]{1,0:T(8,128)S(1)}, f32[32,5120]{1,0:T(8,128)S(1)}, u32[]{:S(2)}, u32[]{:S(2)}) collective-permute-start(f32[32,5120]{1,0:T(8,128)S(1)} %bitcast.5), channel_id=1, source_target_pairs={{0,32},{1,33},{2,34},{3,35},{4,36},{5,37},{6,38},{7,39},{8,40},{9,... | collective-permute-start | bytes 1966088 | tf_op jit(solution)/shard_map/ppermute | solution.py:39
  66.0 23.6 %collective-permute-start.21 = (bf16[64,5120]{1,0:T(8,128)(2,1)S(1)}, bf16[64,5120]{1,0:T(8,128)(2,1)S(1)}, u32[]{:S(2)}, u32[]{:S(2)}) collective-permute-start(bf16[64,5120]{1,0:T(8,128)(2,1)S(1)} %get-tuple-element.37), channel_id=1, source_target_pairs={{0,3},{1,0},{2,1},{3,2},{4,7},{5,4},{6,5},{7,6},{8,11},{9,8},{10,9... | collective-permute-start | bytes 1966088 | tf_op jit(solution)/shard_map/ppermute | solution.py:39
  66.6 23.1 %collective-permute-start.22 = (bf16[64,5120]{1,0:T(8,128)(2,1)S(1)}, bf16[64,5120]{1,0:T(8,128)(2,1)S(1)}, u32[]{:S(2)}, u32[]{:S(2)}) collective-permute-start(bf16[64,5120]{1,0:T(8,128)(2,1)S(1)} %get-tuple-element.38), channel_id=1, source_target_pairs={{0,1},{1,2},{2,3},{3,0},{4,5},{5,6},{6,7},{7,4},{8,9},{9,10},{10,1... | collective-permute-start | bytes 1966088 | tf_op jit(solution)/shard_map/ppermute | solution.py:39
  71.8 17.9 %collective-permute-start.20 = (bf16[64,5120]{1,0:T(8,128)(2,1)S(1)}, bf16[64,5120]{1,0:T(8,128)(2,1)S(1)}, u32[]{:S(2)}, u32[]{:S(2)}) collective-permute-start(bf16[64,5120]{1,0:T(8,128)(2,1)S(1)} %get-tuple-element.36), channel_id=1, source_target_pairs={{0,1},{1,2},{2,3},{3,0},{4,5},{5,6},{6,7},{7,4},{8,9},{9,10},{10,1... | collective-permute-start | bytes 1966088 | tf_op jit(solution)/shard_map/ppermute | solution.py:39
  71.9 17.8 %collective-permute-start.23 = (bf16[64,5120]{1,0:T(8,128)(2,1)S(1)}, bf16[64,5120]{1,0:T(8,128)(2,1)S(1)}, u32[]{:S(2)}, u32[]{:S(2)}) collective-permute-start(bf16[64,5120]{1,0:T(8,128)(2,1)S(1)} %get-tuple-element.39), channel_id=1, source_target_pairs={{0,3},{1,0},{2,1},{3,2},{4,7},{5,4},{6,5},{7,6},{8,11},{9,8},{10,9... | collective-permute-start | bytes 1966088 | tf_op jit(solution)/shard_map/ppermute | solution.py:39
  74.6 9.6 %collective-permute-start.16 = (f32[16,5120]{1,0:T(8,128)S(1)}, f32[16,5120]{1,0:T(8,128)S(1)}, u32[]{:S(2)}, u32[]{:S(2)}) collective-permute-start(f32[16,5120]{1,0:T(8,128)S(1)} %shard_map.94), channel_id=1, source_target_pairs={{0,64},{1,65},{2,66},{3,67},{4,68},{5,69},{6,70},{7,71},{8,72},{9,... | collective-permute-start | bytes 983048 | tf_op jit(solution)/shard_map/ppermute | solution.py:39
  84.3 9.1 %collective-permute-start.17 = (f32[16,5120]{1,0:T(8,128)S(1)}, f32[16,5120]{1,0:T(8,128)S(1)}, u32[]{:S(2)}, u32[]{:S(2)}) collective-permute-start(f32[16,5120]{1,0:T(8,128)S(1)} %collective-permute-done.16.own_start), channel_id=1, source_target_pairs={{0,32},{1,33},{2,34},{3,35},{4,36},{5,37},{6,38},{7,39},{8,40},{9,... | collective-permute-start | bytes 983048 | tf_op jit(solution)/shard_map/ppermute | solution.py:39
  90.2 10.2 %collective-permute-start.25 = (bf16[32,5120]{1,0:T(8,128)(2,1)S(1)}, bf16[32,5120]{1,0:T(8,128)(2,1)S(1)}, u32[]{:S(2)}, u32[]{:S(2)}) collective-permute-start(bf16[32,5120]{1,0:T(8,128)(2,1)S(1)} %get-tuple-element.42), channel_id=1, source_target_pairs={{0,24},{1,25},{2,26},{3,27},{4,28},{5,29},{6,30},{7,31},{8,0},{9,1... | collective-permute-start | bytes 983048 | tf_op jit(solution)/shard_map/ppermute | solution.py:39
  105.5 8.8 %collective-permute-start.28 = (bf16[16,5120]{1,0:T(8,128)(2,1)S(1)}, bf16[16,5120]{1,0:T(8,128)(2,1)S(1)}, u32[]{:S(2)}, u32[]{:S(2)}) collective-permute-start(bf16[16,5120]{1,0:T(8,128)(2,1)S(1)} %shard_map.100), channel_id=1, source_target_pairs={{0,64},{1,65},{2,66},{3,67},{4,68},{5,69},{6,70},{7,71},{8,72},{9,... | collective-permute-start | bytes 491528 | tf_op jit(solution)/shard_map/ppermute | solution.py:39
  (12 other events, 68.9 us)

commit v6 on v5

--- a/solution.py
+++ b/solution.py
@@ -101,7 +101,8 @@
     )(index, state, scale, shift, gate)
 
 
-def pack_kernel(kinds, core, qkv, output, until, packed, sem):
+def pack_kernel(kinds, core, qkv, *refs):
+    packed, sem = refs[-2:]
     half = packed.shape[1]
     first = pl.multiple_of(core[0] * half, half)
     copies = []
@@ -111,7 +112,7 @@
             copies.append(pltpu.make_async_copy(rows, packed.at[place], sem))
         else:
             for at in range(0, half, HDIM):
-                block = output.at[:, pl.ds(pl.multiple_of(first + at, HDIM), HDIM)]
+                block = refs[0].at[:, pl.ds(pl.multiple_of(first + at, HDIM), HDIM)]
                 copies.append(
                     pltpu.make_async_copy(block, packed.at[place, pl.ds(at, HDIM), :], sem)
                 )
@@ -121,37 +122,57 @@
         copy.wait()
 
 
-def pack(kinds, core, qkv_weight, out_weight, until):
+def pack(kinds, core, qkv_weight, *more):
     half = qkv_weight.shape[1] // 2
     return pl.pallas_call(
         functools.partial(pack_kernel, kinds),
         grid_spec=pltpu.PrefetchScalarGridSpec(
             num_scalar_prefetch=1,
             grid=(1,),
-            in_specs=[ANY] * 3,
+            in_specs=[ANY] * (1 + len(more)),
             out_specs=pl.BlockSpec((len(kinds), half, HDIM), lambda i, core: (0, 0, 0)),
             scratch_shapes=[pltpu.SemaphoreType.DMA],
         ),
         out_shape=jax.ShapeDtypeStruct((len(kinds), half, HDIM), BF16),
         compiler_params=PARAMS,
         cost_estimate=pl.CostEstimate(flops=0, bytes_accessed=4000000, transcendentals=0),
-    )(core, qkv_weight, out_weight, until)
-
-
-def stack_kernel(one, two, out):
-    size = one.shape[0]
-    out[:size] = one[...]
-    out[size:] = two[...]
-
-
-def stack(one, two):
+    )(core, qkv_weight, *more)
+
+
+def stack_kernel(*refs):
+    out, at = refs[-1], 0
+    for piece in refs[:-1]:
+        out[at : at + piece.shape[0]] = piece[...]
+        at += piece.shape[0]
+
+
+def stack(*pieces):
     return pl.pallas_call(
         stack_kernel,
-        out_shape=jax.ShapeDtypeStruct((2 * one.shape[0], one.shape[1]), one.dtype),
-        in_specs=[VMEM] * 2,
+        out_shape=jax.ShapeDtypeStruct(
+            (sum(piece.shape[0] for piece in pieces), pieces[0].shape[1]), BF16
+        ),
+        in_specs=[VMEM] * len(pieces),
         out_specs=VMEM,
         compiler_params=PARAMS,
-    )(one, two)
+    )(*pieces)
+
+
+def halves_kernel(one, two, *refs):
+    low, high = refs[-2:]
+    half = low.shape[0]
+    low[...] = one[:half]
+    high[...] = two[half:]
+
+
+def first_and_second_half(one, two, *until):
+    return pl.pallas_call(
+        halves_kernel,
+        out_shape=[jax.ShapeDtypeStruct((one.shape[0] // 2, one.shape[1]), BF16)] * 2,
+        in_specs=[VMEM] * 2 + [ANY] * len(until),
+        out_specs=[VMEM] * 2,
+        compiler_params=PARAMS,
+    )(one, two, *until)
 
 
 def sides(core, mine, theirs, width, step, one):
@@ -410,30 +431,25 @@
     modulated, gates = modulate(index, state, scale_table, shift_table, gate_table)
     near_start = send(state, to_later_core)
     minus, plus, opposite = [send(modulated, first_axis(s)) for s in (1, -1, 2)]
-    near_low = stack(modulated, minus)
-    before_low, after_low = send(near_low, second_axis(1)), send(near_low, second_axis(-1))
-    near_high = stack(plus, opposite)
-    after_high, before_high = send(near_high, second_axis(-1)), send(near_high, second_axis(1))
-    kv_mine = send(pack((1, 2), core, qkv_weight, out_weight, modulated), to_both_sides)
-    qo_mine = send(pack((0, 3), core, qkv_weight, out_weight, modulated), to_both_sides)
-    last_low = send(hold(before_low, before_high, after_low), second_axis(1))
-    last_high = send(hold(after_high, before_high, after_low), second_axis(-1))
-
-    size = near_low.shape[0]
-    near = [near_low, near_high]
-    side = [before_low, before_high, after_low, after_high]
-    last = [last_low, last_high]
-    kv_mine = hold(kv_mine, near_low, near_high)
+    near = stack(modulated, minus, plus, opposite)
+    before, after = send(near, second_axis(1)), send(near, second_axis(-1))
+    kv_mine = send(pack((1, 2), core, qkv_weight, modulated), to_both_sides)
+    qo_mine = send(pack((0, 3), core, qkv_weight, out_weight, minus, plus, opposite), to_both_sides)
+    before_half, after_half = first_and_second_half(before, after, near_start)
+    last = [send(before_half, second_axis(1)), send(after_half, second_axis(-1))]
+
+    size = before_half.shape[0]
+    kv_mine = hold(kv_mine, near)
     kv_weights = (qkv_weight, kv_mine, send(kv_mine, to_other_core))
     qo_theirs = send(qo_mine, to_other_core)
-    (first_kv,) = project(core, (1, 2), near + side, *kv_weights, [6 * size])
+    (first_kv,) = project(core, (1, 2), [near, before, after], *kv_weights, [6 * size])
     (last_kv,) = project(core, (1, 2), last, *kv_weights, [2 * size])
     kv = [first_kv, last_kv]
     far = [send(value, to_partner) for value in kv]
     near_q, side_q, last_q = project(
         core,
         (0,),
-        near + side + last,
+        [near, before, after, *last],
         qkv_weight,
         qo_mine,
         qo_theirs,

time: 118 us -> 114 us (0.966)
  waiting for transfers between devices: 55.8 us -> 54.2 us
    ppermute x30 -> x28, waiting for transfers between devices: 55.8 us -> 54.2 us  [send(): return lax.ppermute(value, ('tm', 'seq'), moves(rule))]
    ppermute x30 -> x28, starting transfers between devices: 43.1 us -> 42.3 us  [send(): return lax.ppermute(value, ('tm', 'seq'), moves(rule))]
  transfers between devices with their start and end apart: 30 -> 28, of which waited for: 17 -> 13; matrix products, arithmetic and copies ran while one was open for 0% -> 0% of each run, Pallas kernels for 9% -> 8%
where the time goes in v6:
time: 114 us
  waiting for transfers between devices  54.2 us (48%)
  starting transfers between devices  42.3 us (37%)
  Pallas kernels  15.4 us (14%)
    ppermute x28, waiting for transfers between devices, send(): return lax.ppermute(value, ('tm', 'seq'), moves(rule))  54.2 us
    ppermute x28, starting transfers between devices, send(): return lax.ppermute(value, ('tm', 'seq'), moves(rule))  42.3 us
    pallas_call x3, Pallas kernels, project(): pl.pallas_call(functools.partial(project_kernel, len(pieces), kinds, rows...  4.66 us
    pallas_call x3, Pallas kernels, attend(): pl.pallas_call(functools.partial(attend_kernel, len(near), cuts), out_sha...  4.64 us
    pallas_call x1, Pallas kernels, modulate(): pl.pallas_call(modulate_kernel, grid_spec=pltpu.PrefetchScalarGridSpec(nu...  2.39 us
  transfers between devices with their start and end apart: 28, of which 13 were waited for; matrix products, arithmetic and copies ran while one was open for 0% of the time, Pallas kernels for 8%

profile of v6, /device:TPU:17, one launch (start us, length us, event | category | flops | bytes accessed | tf_op | source)
XLA Modules:
  0.0 113.8 jit_solution(992961287649128907)
XLA Ops:
  0.7 2.4 %shard_map.82 = (bf16[32,5120]{1,0:T(8,128)(2,1)}, f32[1,5120]{1,0:T(1,128)}) custom-call(s32[1]{0:T(128)S(6)} %add.4.index, f32[32,5120]{1,0:T(8,128)} %bitcast.4, f32[50,5120]{1,0:T(8,128)} %scale.1, f32[50,5120]{1,0:T(8,128)} %shift.1, f32[50,5120]{1,0:T(8,128)} %gate.1), custom_call_target="tpu_custom_call" | custom-call | flops 1000000 | bytes 2000000 | tf_op jit(solution)/shard_map/pallas_call | solution.py:87
  4.8 1.6 %collective-permute-start.1 = (bf16[32,5120]{1,0:T(8,128)(2,1)S(1)}, bf16[32,5120]{1,0:T(8,128)(2,1)S(1)}, u32[]{:S(2)}, u32[]{:S(2)}) collective-permute-start(bf16[32,5120]{1,0:T(8,128)(2,1)S(1)} %copy-done.3), channel_id=1, source_target_pairs={{0,8},{1,9},{2,10},{3,11},{4,12},{5,13},{6,14},{7,15},{8,16},{9,17... | collective-permute-start | bytes 983048 | tf_op jit(solution)/shard_map/ppermute | solution.py:39
  6.4 2.1 %collective-permute-start.2 = (bf16[32,5120]{1,0:T(8,128)(2,1)S(1)}, bf16[32,5120]{1,0:T(8,128)(2,1)S(1)}, u32[]{:S(2)}, u32[]{:S(2)}) collective-permute-start(bf16[32,5120]{1,0:T(8,128)(2,1)S(1)} %copy-done.3), channel_id=1, source_target_pairs={{0,24},{1,25},{2,26},{3,27},{4,28},{5,29},{6,30},{7,31},{8,0},{9,1... | collective-permute-start | bytes 983048 | tf_op jit(solution)/shard_map/ppermute | solution.py:39
  9.9 3.5 %collective-permute-done.1.refs_1_ = bf16[32,5120]{1,0:T(8,128)(2,1)S(1)} collective-permute-done((bf16[32,5120]{1,0:T(8,128)(2,1)S(1)}, bf16[32,5120]{1,0:T(8,128)(2,1)S(1)}, u32[]{:S(2)}, u32[]{:S(2)}) %collective-permute-start.1) | collective-permute-done | bytes 327712 | tf_op jit(solution)/shard_map/ppermute | solution.py:39
  13.3 2.8 %collective-permute-done.2.refs_2_ = bf16[32,5120]{1,0:T(8,128)(2,1)S(1)} collective-permute-done((bf16[32,5120]{1,0:T(8,128)(2,1)S(1)}, bf16[32,5120]{1,0:T(8,128)(2,1)S(1)}, u32[]{:S(2)}, u32[]{:S(2)}) %collective-permute-start.2) | collective-permute-done | bytes 327712 | tf_op jit(solution)/shard_map/ppermute | solution.py:39
  16.1 1.9 %collective-permute-done.3.refs_3_ = bf16[32,5120]{1,0:T(8,128)(2,1)S(1)} collective-permute-done((bf16[32,5120]{1,0:T(8,128)(2,1)S(1)}, bf16[32,5120]{1,0:T(8,128)(2,1)S(1)}, u32[]{:S(2)}, u32[]{:S(2)}) %collective-permute-start.3) | collective-permute-done | bytes 327712 | tf_op jit(solution)/shard_map/ppermute | solution.py:39
  22.4 2.5 %collective-permute-start.11 = (bf16[2,2560,128]{2,1,0:T(8,128)(2,1)S(1)}, bf16[2,2560,128]{2,1,0:T(8,128)(2,1)S(1)}, u32[]{:S(2)}, u32[]{:S(2)}) collective-permute-start(bf16[2,2560,128]{2,1,0:T(8,128)(2,1)S(1)} %shard_map.88.refs_4_.refs_3_), channel_id=1, source_target_pairs={{0,32},{1,33},{2,34},{3,35},{4,36},{5,37},{6,38},{7,39},{8,40},{9,... | collective-permute-start | bytes 3932168 | tf_op jit(solution)/shard_map/ppermute | solution.py:39
  25.6 9.8 %collective-permute-done.8.refs_6_.mine = bf16[2,2560,128]{2,1,0:T(8,128)(2,1)S(1)} collective-permute-done((bf16[2,2560,128]{2,1,0:T(8,128)(2,1)S(1)}, bf16[2,2560,128]{2,1,0:T(8,128)(2,1)S(1)}, u32[]{:S(2)}, u32[]{:S(2)}) %collective-permute-start.8) | collective-permute-done | bytes 1310752 | tf_op jit(solution)/shard_map/ppermute | solution.py:39
  35.4 2.1 %collective-permute-start.9 = (bf16[2,2560,128]{2,1,0:T(8,128)(2,1)S(1)}, bf16[2,2560,128]{2,1,0:T(8,128)(2,1)S(1)}, u32[]{:S(2)}, u32[]{:S(2)}) collective-permute-start(bf16[2,2560,128]{2,1,0:T(8,128)(2,1)S(1)} %collective-permute-done.8.refs_6_.mine), channel_id=1, source_target_pairs={{0,32},{1,33},{2,34},{3,35},{4,36},{5,37},{6,38},{7,39},{8,40},{9,... | collective-permute-start | bytes 3932168 | tf_op jit(solution)/shard_map/ppermute | solution.py:39
  40.6 2.2 %shard_map.89.refs_0_ = bf16[384,512]{1,0:T(8,128)(2,1)S(1)} custom-call(s32[1]{0:T(128)} %bitcast.2.core, bf16[128,5120]{1,0:T(8,128)(2,1)S(1)} %shard_map.83.refs_0_, bf16[128,5120]{1,0:T(8,128)(2,1)S(1)} %collective-permute-done.4.one.refs_1_, bf16[128,5120]{1,0:T(8,128)(2,1)S(1)} %collective-permute-done.5.two.refs_2_, ...), custom_call_target="tpu_custom_call" | custom-call | flops 2013265920 | bytes 1000000 | tf_op jit(solution)/shard_map/pallas_call | solution.py:219
  42.8 2.3 %collective-permute-start.12 = (bf16[384,512]{1,0:T(8,128)(2,1)S(1)}, bf16[384,512]{1,0:T(8,128)(2,1)S(1)}, u32[]{:S(2)}, u32[]{:S(2)}) collective-permute-start(bf16[384,512]{1,0:T(8,128)(2,1)S(1)} %shard_map.89.refs_0_), channel_id=1, source_target_pairs={{0,4},{1,5},{2,6},{3,7},{4,0},{5,1},{6,2},{7,3},{8,12},{9,13},{10,... | collective-permute-start | bytes 1179656 | tf_op jit(solution)/shard_map/ppermute | solution.py:39
  45.1 3.7 %collective-permute-done.6.refs_3_.refs_0_ = bf16[64,5120]{1,0:T(8,128)(2,1)S(1)} collective-permute-done((bf16[64,5120]{1,0:T(8,128)(2,1)S(1)}, bf16[64,5120]{1,0:T(8,128)(2,1)S(1)}, u32[]{:S(2)}, u32[]{:S(2)}) %collective-permute-start.6) | collective-permute-done | bytes 655392 | tf_op jit(solution)/shard_map/ppermute | solution.py:39
  49.7 2.3 %collective-permute-start.13 = (bf16[128,512]{1,0:T(8,128)(2,1)S(1)}, bf16[128,512]{1,0:T(8,128)(2,1)S(1)}, u32[]{:S(2)}, u32[]{:S(2)}) collective-permute-start(bf16[128,512]{1,0:T(8,128)(2,1)S(1)} %shard_map.90.refs_1_), channel_id=1, source_target_pairs={{0,4},{1,5},{2,6},{3,7},{4,0},{5,1},{6,2},{7,3},{8,12},{9,13},{10,... | collective-permute-start | bytes 393224 | tf_op jit(solution)/shard_map/ppermute | solution.py:39
  52.0 1.5 %shard_map.86 = (bf16[128,256]{1,0:T(8,128)(2,1)S(1)}, bf16[256,256]{1,0:T(8,128)(2,1)S(1)}, bf16[128,256]{1,0:T(8,128)(2,1)S(1)}) custom-call(s32[1]{0:T(128)} %bitcast.2.core, bf16[128,5120]{1,0:T(8,128)(2,1)S(1)} %shard_map.83.refs_0_, bf16[128,5120]{1,0:T(8,128)(2,1)S(1)} %collective-permute-done.4.one.refs_1_, ...), custom_call_target="tpu_custom_call" | custom-call | flops 1342177280 | bytes 1000000 | tf_op jit(solution)/shard_map/pallas_call | solution.py:219
  53.5 2.6 %collective-permute-done.13.refs_3_ = bf16[128,512]{1,0:T(8,128)(2,1)S(1)} collective-permute-done((bf16[128,512]{1,0:T(8,128)(2,1)S(1)}, bf16[128,512]{1,0:T(8,128)(2,1)S(1)}, u32[]{:S(2)}, u32[]{:S(2)}) %collective-permute-start.13) | collective-permute-done | bytes 131104 | tf_op jit(solution)/shard_map/ppermute | solution.py:39
  57.5 2.7 %collective-permute-start.17 = (bf16[64,5120]{1,0:T(8,128)(2,1)S(1)}, bf16[64,5120]{1,0:T(8,128)(2,1)S(1)}, u32[]{:S(2)}, u32[]{:S(2)}) collective-permute-start(bf16[64,5120]{1,0:T(8,128)(2,1)S(1)} %get-tuple-element.39), channel_id=1, source_target_pairs={{0,3},{1,0},{2,1},{3,2},{4,7},{5,4},{6,5},{7,6},{8,11},{9,8},{10,9... | collective-permute-start | bytes 1966088 | tf_op jit(solution)/shard_map/ppermute | solution.py:39
  60.2 1.9 %shard_map.94 = (bf16[64,5120]{1,0:T(8,128)(2,1)S(1)}, bf16[64,5120]{1,0:T(8,128)(2,1)S(1)}, bf16[64,5120]{1,0:T(8,128)(2,1)S(1)}, bf16[64,5120]{1,0:T(8,128)(2,1)S(1)}) custom-call(s32[1]{0:T(128)} %bitcast.2.core, bf16[256,256]{1,0:T(8,128)(2,1)S(1)} %get-tuple-element.36.queries, bf16[128,5120]{1,0:T(8,128)(2,1)S(1)} %copy-done.1, ...), custom_call_target="tpu_custom_call" | custom-call | flops 939524096 | bytes 1000000 | tf_op jit(solution)/shard_map/pallas_call | solution.py:273
  63.7 4.8 %collective-permute-done.16.low = bf16[64,5120]{1,0:T(8,128)(2,1)S(1)} collective-permute-done((bf16[64,5120]{1,0:T(8,128)(2,1)S(1)}, bf16[64,5120]{1,0:T(8,128)(2,1)S(1)}, u32[]{:S(2)}, u32[]{:S(2)}) %collective-permute-start.16) | collective-permute-done | bytes 655392 | tf_op jit(solution)/shard_map/ppermute | solution.py:39
  68.8 2.7 %collective-permute-start.21 = (bf16[64,5120]{1,0:T(8,128)(2,1)S(1)}, bf16[64,5120]{1,0:T(8,128)(2,1)S(1)}, u32[]{:S(2)}, u32[]{:S(2)}) collective-permute-start(bf16[64,5120]{1,0:T(8,128)(2,1)S(1)} %get-tuple-element.43), channel_id=1, source_target_pairs={{0,3},{1,0},{2,1},{3,2},{4,7},{5,4},{6,5},{7,6},{8,11},{9,8},{10,9... | collective-permute-start | bytes 1966088 | tf_op jit(solution)/shard_map/ppermute | solution.py:39
  74.3 7.0 %collective-permute-done.14.own_start = f32[16,5120]{1,0:T(8,128)S(1)} collective-permute-done((f32[16,5120]{1,0:T(8,128)S(1)}, f32[16,5120]{1,0:T(8,128)S(1)}, u32[]{:S(2)}, u32[]{:S(2)}) %collective-permute-start.14) | collective-permute-done | bytes 327712 | tf_op jit(solution)/shard_map/ppermute | solution.py:39
  81.2 5.4 %collective-permute-start.15 = (f32[16,5120]{1,0:T(8,128)S(1)}, f32[16,5120]{1,0:T(8,128)S(1)}, u32[]{:S(2)}, u32[]{:S(2)}) collective-permute-start(f32[16,5120]{1,0:T(8,128)S(1)} %collective-permute-done.14.own_start), channel_id=1, source_target_pairs={{0,32},{1,33},{2,34},{3,35},{4,36},{5,37},{6,38},{7,39},{8,40},{9,... | collective-permute-start | bytes 983048 | tf_op jit(solution)/shard_map/ppermute | solution.py:39
  87.3 2.7 %collective-permute-start.23 = (bf16[32,5120]{1,0:T(8,128)(2,1)S(1)}, bf16[32,5120]{1,0:T(8,128)(2,1)S(1)}, u32[]{:S(2)}, u32[]{:S(2)}) collective-permute-start(bf16[32,5120]{1,0:T(8,128)(2,1)S(1)} %get-tuple-element.46), channel_id=1, source_target_pairs={{0,24},{1,25},{2,26},{3,27},{4,28},{5,29},{6,30},{7,31},{8,0},{9,1... | collective-permute-start | bytes 983048 | tf_op jit(solution)/shard_map/ppermute | solution.py:39
  89.9 8.3 %collective-permute-done.22.one = bf16[32,5120]{1,0:T(8,128)(2,1)S(1)} collective-permute-done((bf16[32,5120]{1,0:T(8,128)(2,1)S(1)}, bf16[32,5120]{1,0:T(8,128)(2,1)S(1)}, u32[]{:S(2)}, u32[]{:S(2)}) %collective-permute-start.22) | collective-permute-done | bytes 327712 | tf_op jit(solution)/shard_map/ppermute | solution.py:39
  103.0 7.5 %collective-permute-done.26.own_sum = bf16[16,5120]{1,0:T(8,128)(2,1)S(1)} collective-permute-done((bf16[16,5120]{1,0:T(8,128)(2,1)S(1)}, bf16[16,5120]{1,0:T(8,128)(2,1)S(1)}, u32[]{:S(2)}, u32[]{:S(2)}) %collective-permute-start.26) | collective-permute-done | bytes 163872 | tf_op jit(solution)/shard_map/ppermute | solution.py:39
  (64 shorter events, 26.7 us)
Async XLA Ops:
  4.6 17.8 %collective-permute-start.10 = (bf16[2,2560,128]{2,1,0:T(8,128)(2,1)S(1)}, bf16[2,2560,128]{2,1,0:T(8,128)(2,1)S(1)}, u32[]{:S(2)}, u32[]{:S(2)}) collective-permute-start(bf16[2,2560,128]{2,1,0:T(8,128)(2,1)S(1)} %shard_map.87), channel_id=1, source_target_pairs={{0,4},{1,5},{2,6},{3,7},{4,0},{5,1},{6,2},{7,3},{8,12},{9,13},{10,... | collective-permute-start | bytes 3932168 | tf_op jit(solution)/shard_map/ppermute | solution.py:39
  4.8 8.5 %collective-permute-start.1 = (bf16[32,5120]{1,0:T(8,128)(2,1)S(1)}, bf16[32,5120]{1,0:T(8,128)(2,1)S(1)}, u32[]{:S(2)}, u32[]{:S(2)}) collective-permute-start(bf16[32,5120]{1,0:T(8,128)(2,1)S(1)} %copy-done.3), channel_id=1, source_target_pairs={{0,8},{1,9},{2,10},{3,11},{4,12},{5,13},{6,14},{7,15},{8,16},{9,17... | collective-permute-start | bytes 983048 | tf_op jit(solution)/shard_map/ppermute | solution.py:39
  6.4 9.7 %collective-permute-start.2 = (bf16[32,5120]{1,0:T(8,128)(2,1)S(1)}, bf16[32,5120]{1,0:T(8,128)(2,1)S(1)}, u32[]{:S(2)}, u32[]{:S(2)}) collective-permute-start(bf16[32,5120]{1,0:T(8,128)(2,1)S(1)} %copy-done.3), channel_id=1, source_target_pairs={{0,24},{1,25},{2,26},{3,27},{4,28},{5,29},{6,30},{7,31},{8,0},{9,1... | collective-permute-start | bytes 983048 | tf_op jit(solution)/shard_map/ppermute | solution.py:39
  8.6 9.4 %collective-permute-start.3 = (bf16[32,5120]{1,0:T(8,128)(2,1)S(1)}, bf16[32,5120]{1,0:T(8,128)(2,1)S(1)}, u32[]{:S(2)}, u32[]{:S(2)}) collective-permute-start(bf16[32,5120]{1,0:T(8,128)(2,1)S(1)} %copy-done.3), channel_id=1, source_target_pairs={{0,16},{1,17},{2,18},{3,19},{4,20},{5,21},{6,22},{7,23},{8,24},{9,... | collective-permute-start | bytes 983048 | tf_op jit(solution)/shard_map/ppermute | solution.py:39
  18.4 17.0 %collective-permute-start.8 = (bf16[2,2560,128]{2,1,0:T(8,128)(2,1)S(1)}, bf16[2,2560,128]{2,1,0:T(8,128)(2,1)S(1)}, u32[]{:S(2)}, u32[]{:S(2)}) collective-permute-start(bf16[2,2560,128]{2,1,0:T(8,128)(2,1)S(1)} %shard_map.85), channel_id=1, source_target_pairs={{0,4},{1,5},{2,6},{3,7},{4,0},{5,1},{6,2},{7,3},{8,12},{9,13},{10,... | collective-permute-start | bytes 3932168 | tf_op jit(solution)/shard_map/ppermute | solution.py:39
  19.6 18.0 %collective-permute-start.4 = (bf16[128,5120]{1,0:T(8,128)(2,1)S(1)}, bf16[128,5120]{1,0:T(8,128)(2,1)S(1)}, u32[]{:S(2)}, u32[]{:S(2)}) collective-permute-start(bf16[128,5120]{1,0:T(8,128)(2,1)S(1)} %shard_map.83.refs_0_), channel_id=1, source_target_pairs={{0,1},{1,2},{2,3},{3,0},{4,5},{5,6},{6,7},{7,4},{8,9},{9,10},{10,1... | collective-permute-start | bytes 3932168 | tf_op jit(solution)/shard_map/ppermute | solution.py:39
  20.9 16.8 %collective-permute-start.5 = (bf16[128,5120]{1,0:T(8,128)(2,1)S(1)}, bf16[128,5120]{1,0:T(8,128)(2,1)S(1)}, u32[]{:S(2)}, u32[]{:S(2)}) collective-permute-start(bf16[128,5120]{1,0:T(8,128)(2,1)S(1)} %shard_map.83.refs_0_), channel_id=1, source_target_pairs={{0,3},{1,0},{2,1},{3,2},{4,7},{5,4},{6,5},{7,6},{8,11},{9,8},{10,9... | collective-permute-start | bytes 3932168 | tf_op jit(solution)/shard_map/ppermute | solution.py:39
  22.4 18.2 %collective-permute-start.11 = (bf16[2,2560,128]{2,1,0:T(8,128)(2,1)S(1)}, bf16[2,2560,128]{2,1,0:T(8,128)(2,1)S(1)}, u32[]{:S(2)}, u32[]{:S(2)}) collective-permute-start(bf16[2,2560,128]{2,1,0:T(8,128)(2,1)S(1)} %shard_map.88.refs_4_.refs_3_), channel_id=1, source_target_pairs={{0,32},{1,33},{2,34},{3,35},{4,36},{5,37},{6,38},{7,39},{8,40},{9,... | collective-permute-start | bytes 3932168 | tf_op jit(solution)/shard_map/ppermute | solution.py:39
  24.9 12.6 %collective-permute-start = (f32[32,5120]{1,0:T(8,128)S(1)}, f32[32,5120]{1,0:T(8,128)S(1)}, u32[]{:S(2)}, u32[]{:S(2)}) collective-permute-start(f32[32,5120]{1,0:T(8,128)S(1)} %bitcast.5), channel_id=1, source_target_pairs={{0,32},{1,33},{2,34},{3,35},{4,36},{5,37},{6,38},{7,39},{8,40},{9,... | collective-permute-start | bytes 1966088 | tf_op jit(solution)/shard_map/ppermute | solution.py:39
  35.4 16.5 %collective-permute-start.9 = (bf16[2,2560,128]{2,1,0:T(8,128)(2,1)S(1)}, bf16[2,2560,128]{2,1,0:T(8,128)(2,1)S(1)}, u32[]{:S(2)}, u32[]{:S(2)}) collective-permute-start(bf16[2,2560,128]{2,1,0:T(8,128)(2,1)S(1)} %collective-permute-done.8.refs_6_.mine), channel_id=1, source_target_pairs={{0,32},{1,33},{2,34},{3,35},{4,36},{5,37},{6,38},{7,39},{8,40},{9,... | collective-permute-start | bytes 3932168 | tf_op jit(solution)/shard_map/ppermute | solution.py:39
  37.8 11.0 %collective-permute-start.6 = (bf16[64,5120]{1,0:T(8,128)(2,1)S(1)}, bf16[64,5120]{1,0:T(8,128)(2,1)S(1)}, u32[]{:S(2)}, u32[]{:S(2)}) collective-permute-start(bf16[64,5120]{1,0:T(8,128)(2,1)S(1)} %get-tuple-element.29), channel_id=1, source_target_pairs={{0,1},{1,2},{2,3},{3,0},{4,5},{5,6},{6,7},{7,4},{8,9},{9,10},{10,1... | collective-permute-start | bytes 1966088 | tf_op jit(solution)/shard_map/ppermute | solution.py:39
  39.0 9.7 %collective-permute-start.7 = (bf16[64,5120]{1,0:T(8,128)(2,1)S(1)}, bf16[64,5120]{1,0:T(8,128)(2,1)S(1)}, u32[]{:S(2)}, u32[]{:S(2)}) collective-permute-start(bf16[64,5120]{1,0:T(8,128)(2,1)S(1)} %get-tuple-element.30), channel_id=1, source_target_pairs={{0,3},{1,0},{2,1},{3,2},{4,7},{5,4},{6,5},{7,6},{8,11},{9,8},{10,9... | collective-permute-start | bytes 1966088 | tf_op jit(solution)/shard_map/ppermute | solution.py:39
  42.8 13.3 %collective-permute-start.12 = (bf16[384,512]{1,0:T(8,128)(2,1)S(1)}, bf16[384,512]{1,0:T(8,128)(2,1)S(1)}, u32[]{:S(2)}, u32[]{:S(2)}) collective-permute-start(bf16[384,512]{1,0:T(8,128)(2,1)S(1)} %shard_map.89.refs_0_), channel_id=1, source_target_pairs={{0,4},{1,5},{2,6},{3,7},{4,0},{5,1},{6,2},{7,3},{8,12},{9,13},{10,... | collective-permute-start | bytes 1179656 | tf_op jit(solution)/shard_map/ppermute | solution.py:39
  57.4 11.0 %collective-permute-start.16 = (bf16[64,5120]{1,0:T(8,128)(2,1)S(1)}, bf16[64,5120]{1,0:T(8,128)(2,1)S(1)}, u32[]{:S(2)}, u32[]{:S(2)}) collective-permute-start(bf16[64,5120]{1,0:T(8,128)(2,1)S(1)} %get-tuple-element.32.until), channel_id=1, source_target_pairs={{0,1},{1,2},{2,3},{3,0},{4,5},{5,6},{6,7},{7,4},{8,9},{9,10},{10,1... | collective-permute-start | bytes 1966088 | tf_op jit(solution)/shard_map/ppermute | solution.py:39
  57.5 10.9 %collective-permute-start.17 = (bf16[64,5120]{1,0:T(8,128)(2,1)S(1)}, bf16[64,5120]{1,0:T(8,128)(2,1)S(1)}, u32[]{:S(2)}, u32[]{:S(2)}) collective-permute-start(bf16[64,5120]{1,0:T(8,128)(2,1)S(1)} %get-tuple-element.39), channel_id=1, source_target_pairs={{0,3},{1,0},{2,1},{3,2},{4,7},{5,4},{6,5},{7,6},{8,11},{9,8},{10,9... | collective-permute-start | bytes 1966088 | tf_op jit(solution)/shard_map/ppermute | solution.py:39
  62.1 24.5 %collective-permute-start.19 = (bf16[64,5120]{1,0:T(8,128)(2,1)S(1)}, bf16[64,5120]{1,0:T(8,128)(2,1)S(1)}, u32[]{:S(2)}, u32[]{:S(2)}) collective-permute-start(bf16[64,5120]{1,0:T(8,128)(2,1)S(1)} %get-tuple-element.41), channel_id=1, source_target_pairs={{0,3},{1,0},{2,1},{3,2},{4,7},{5,4},{6,5},{7,6},{8,11},{9,8},{10,9... | collective-permute-start | bytes 1966088 | tf_op jit(solution)/shard_map/ppermute | solution.py:39
  62.2 24.5 %collective-permute-start.20 = (bf16[64,5120]{1,0:T(8,128)(2,1)S(1)}, bf16[64,5120]{1,0:T(8,128)(2,1)S(1)}, u32[]{:S(2)}, u32[]{:S(2)}) collective-permute-start(bf16[64,5120]{1,0:T(8,128)(2,1)S(1)} %get-tuple-element.42), channel_id=1, source_target_pairs={{0,1},{1,2},{2,3},{3,0},{4,5},{5,6},{6,7},{7,4},{8,9},{9,10},{10,1... | collective-permute-start | bytes 1966088 | tf_op jit(solution)/shard_map/ppermute | solution.py:39
  68.8 17.9 %collective-permute-start.18 = (bf16[64,5120]{1,0:T(8,128)(2,1)S(1)}, bf16[64,5120]{1,0:T(8,128)(2,1)S(1)}, u32[]{:S(2)}, u32[]{:S(2)}) collective-permute-start(bf16[64,5120]{1,0:T(8,128)(2,1)S(1)} %get-tuple-element.40), channel_id=1, source_target_pairs={{0,1},{1,2},{2,3},{3,0},{4,5},{5,6},{6,7},{7,4},{8,9},{9,10},{10,1... | collective-permute-start | bytes 1966088 | tf_op jit(solution)/shard_map/ppermute | solution.py:39
  68.8 17.9 %collective-permute-start.21 = (bf16[64,5120]{1,0:T(8,128)(2,1)S(1)}, bf16[64,5120]{1,0:T(8,128)(2,1)S(1)}, u32[]{:S(2)}, u32[]{:S(2)}) collective-permute-start(bf16[64,5120]{1,0:T(8,128)(2,1)S(1)} %get-tuple-element.43), channel_id=1, source_target_pairs={{0,3},{1,0},{2,1},{3,2},{4,7},{5,4},{6,5},{7,6},{8,11},{9,8},{10,9... | collective-permute-start | bytes 1966088 | tf_op jit(solution)/shard_map/ppermute | solution.py:39
  71.6 9.6 %collective-permute-start.14 = (f32[16,5120]{1,0:T(8,128)S(1)}, f32[16,5120]{1,0:T(8,128)S(1)}, u32[]{:S(2)}, u32[]{:S(2)}) collective-permute-start(f32[16,5120]{1,0:T(8,128)S(1)} %shard_map.92), channel_id=1, source_target_pairs={{0,64},{1,65},{2,66},{3,67},{4,68},{5,69},{6,70},{7,71},{8,72},{9,... | collective-permute-start | bytes 983048 | tf_op jit(solution)/shard_map/ppermute | solution.py:39
  81.2 8.7 %collective-permute-start.15 = (f32[16,5120]{1,0:T(8,128)S(1)}, f32[16,5120]{1,0:T(8,128)S(1)}, u32[]{:S(2)}, u32[]{:S(2)}) collective-permute-start(f32[16,5120]{1,0:T(8,128)S(1)} %collective-permute-done.14.own_start), channel_id=1, source_target_pairs={{0,32},{1,33},{2,34},{3,35},{4,36},{5,37},{6,38},{7,39},{8,40},{9,... | collective-permute-start | bytes 983048 | tf_op jit(solution)/shard_map/ppermute | solution.py:39
  87.2 11.0 %collective-permute-start.22 = (bf16[32,5120]{1,0:T(8,128)(2,1)S(1)}, bf16[32,5120]{1,0:T(8,128)(2,1)S(1)}, u32[]{:S(2)}, u32[]{:S(2)}) collective-permute-start(bf16[32,5120]{1,0:T(8,128)(2,1)S(1)} %get-tuple-element.45), channel_id=1, source_target_pairs={{0,8},{1,9},{2,10},{3,11},{4,12},{5,13},{6,14},{7,15},{8,16},{9,17... | collective-permute-start | bytes 983048 | tf_op jit(solution)/shard_map/ppermute | solution.py:39
  87.3 10.9 %collective-permute-start.23 = (bf16[32,5120]{1,0:T(8,128)(2,1)S(1)}, bf16[32,5120]{1,0:T(8,128)(2,1)S(1)}, u32[]{:S(2)}, u32[]{:S(2)}) collective-permute-start(bf16[32,5120]{1,0:T(8,128)(2,1)S(1)} %get-tuple-element.46), channel_id=1, source_target_pairs={{0,24},{1,25},{2,26},{3,27},{4,28},{5,29},{6,30},{7,31},{8,0},{9,1... | collective-permute-start | bytes 983048 | tf_op jit(solution)/shard_map/ppermute | solution.py:39
  101.7 8.8 %collective-permute-start.26 = (bf16[16,5120]{1,0:T(8,128)(2,1)S(1)}, bf16[16,5120]{1,0:T(8,128)(2,1)S(1)}, u32[]{:S(2)}, u32[]{:S(2)}) collective-permute-start(bf16[16,5120]{1,0:T(8,128)(2,1)S(1)} %shard_map.98), channel_id=1, source_target_pairs={{0,64},{1,65},{2,66},{3,67},{4,68},{5,69},{6,70},{7,71},{8,72},{9,... | collective-permute-start | bytes 491528 | tf_op jit(solution)/shard_map/ppermute | solution.py:39
  (11 other events, 80.3 us)

commit v7 on v6

--- a/solution.py
+++ b/solution.py
@@ -63,12 +63,8 @@
     return (yh if core == 0 else 1 - yh, core, x, 1 - yl, z)
 
 
-def to_later_half(yh, core, x, yl, z):
-    return (1, core, x, yl, z) if yh == 0 else None
-
-
-def to_later_core(yh, core, x, yl, z):
-    return (0, 1, x, yl, z) if yh == 0 and core == 0 else None
+def to_other_half(yh, core, x, yl, z):
+    return (1 - yh, core, x, yl, z)
 
 
 def modulate_kernel(index, state, scale, shift, gate, out, gates):
@@ -429,7 +425,7 @@
     place, core, index = group[None], core[None], window_start + group
     state = trajectory[0]
     modulated, gates = modulate(index, state, scale_table, shift_table, gate_table)
-    near_start = send(state, to_later_core)
+    near_start = send(state, to_other_core)
     minus, plus, opposite = [send(modulated, first_axis(s)) for s in (1, -1, 2)]
     near = stack(modulated, minus, plus, opposite)
     before, after = send(near, second_axis(1)), send(near, second_axis(-1))
@@ -458,7 +454,7 @@
 
     outs = (out_weight, qo_mine, qo_theirs)
     last_low, last_high = attend(core, last_q, kv, far, *outs, [size] * 2)
-    own_start = send(start_half(place, state, near_start, last_low), to_later_half)
+    own_start = send(start_half(place, state, near_start, last_low), to_other_half)
     from_low, from_high = send(last_low, second_axis(1)), send(last_high, second_axis(-1))
     before_low, before_high, after_low, after_high = attend(
         core, side_q, kv, far, *outs, [size] * 4
@@ -471,12 +467,12 @@
         near_low, near_high, low_1, low_2, high_1, high_2
     )
     arrived = [
-        send(value, first_axis(s)) for value, s in ((to_plus, 1), (to_minus, -1), (to_opposite, 2))
+        send(value, first_axis(s)) for value, s in ((to_opposite, 2), (to_plus, 1), (to_minus, -1))
     ]
     far_start = send(own_start, to_other_core)
     drift, term = drifts(index, step_sizes, total, arrived, gates, far_start)
     beside = send(term, to_other_core)
-    own_sum = send(both_half(place, drift, beside), to_later_half)
+    own_sum = send(both_half(place, drift, beside), to_other_half)
     far_sum = send(own_sum, to_other_core)
     return finish(
         place, state, near_start, own_start, far_start, drift, beside, own_sum, far_sum

time: 114 us -> 113 us (level)
  waiting for transfers between devices: 54.2 us -> 51.7 us
    ppermute x28, waiting for transfers between devices: 54.2 us -> 51.7 us  [send(): return lax.ppermute(value, ('tm', 'seq'), moves(rule))]
  transfers between devices with their start and end apart: 28 -> 28, of which waited for: 13 -> 14; matrix products, arithmetic and copies ran while one was open for 0% -> 0% of each run, Pallas kernels for 8% -> 8%
where the time goes in v7:
time: 113 us; the launch traced here: 112 us
  waiting for transfers between devices  51.7 us (46%)
  starting transfers between devices  42.6 us (38%)
  Pallas kernels  15.4 us (14%)
    ppermute x28, waiting for transfers between devices, send(): return lax.ppermute(value, ('tm', 'seq'), moves(rule))  51.7 us
    ppermute x28, starting transfers between devices, send(): return lax.ppermute(value, ('tm', 'seq'), moves(rule))  42.6 us
    pallas_call x3, Pallas kernels, project(): pl.pallas_call(functools.partial(project_kernel, len(pieces), kinds, rows...  4.66 us
    pallas_call x3, Pallas kernels, attend(): pl.pallas_call(functools.partial(attend_kernel, len(near), cuts), out_sha...  4.63 us
    pallas_call x1, Pallas kernels, modulate(): pl.pallas_call(modulate_kernel, grid_spec=pltpu.PrefetchScalarGridSpec(nu...  2.39 us
  transfers between devices with their start and end apart: 28, of which 14 were waited for; matrix products, arithmetic and copies ran while one was open for 0% of the time, Pallas kernels for 8%

profile of v7, /device:TPU:17, one launch (start us, length us, event | category | flops | bytes accessed | tf_op | source)
XLA Modules:
  0.0 111.7 jit_solution(8890839066684022417)
XLA Ops:
  0.7 2.4 %shard_map.82 = (bf16[32,5120]{1,0:T(8,128)(2,1)}, f32[1,5120]{1,0:T(1,128)}) custom-call(s32[1]{0:T(128)S(6)} %add.4.index, f32[32,5120]{1,0:T(8,128)} %bitcast.4, f32[50,5120]{1,0:T(8,128)} %scale.1, f32[50,5120]{1,0:T(8,128)} %shift.1, f32[50,5120]{1,0:T(8,128)} %gate.1), custom_call_target="tpu_custom_call" | custom-call | flops 1000000 | bytes 2000000 | tf_op jit(solution)/shard_map/pallas_call | solution.py:83
  6.4 2.1 %collective-permute-start.2 = (bf16[32,5120]{1,0:T(8,128)(2,1)S(1)}, bf16[32,5120]{1,0:T(8,128)(2,1)S(1)}, u32[]{:S(2)}, u32[]{:S(2)}) collective-permute-start(bf16[32,5120]{1,0:T(8,128)(2,1)S(1)} %copy-done.3), channel_id=1, source_target_pairs={{0,24},{1,25},{2,26},{3,27},{4,28},{5,29},{6,30},{7,31},{8,0},{9,1... | collective-permute-start | bytes 983048 | tf_op jit(solution)/shard_map/ppermute | solution.py:39
  9.9 3.5 %collective-permute-done.1.refs_1_ = bf16[32,5120]{1,0:T(8,128)(2,1)S(1)} collective-permute-done((bf16[32,5120]{1,0:T(8,128)(2,1)S(1)}, bf16[32,5120]{1,0:T(8,128)(2,1)S(1)}, u32[]{:S(2)}, u32[]{:S(2)}) %collective-permute-start.1) | collective-permute-done | bytes 327712 | tf_op jit(solution)/shard_map/ppermute | solution.py:39
  13.3 2.8 %collective-permute-done.2.refs_2_ = bf16[32,5120]{1,0:T(8,128)(2,1)S(1)} collective-permute-done((bf16[32,5120]{1,0:T(8,128)(2,1)S(1)}, bf16[32,5120]{1,0:T(8,128)(2,1)S(1)}, u32[]{:S(2)}, u32[]{:S(2)}) %collective-permute-start.2) | collective-permute-done | bytes 327712 | tf_op jit(solution)/shard_map/ppermute | solution.py:39
  16.1 1.9 %collective-permute-done.3.refs_3_ = bf16[32,5120]{1,0:T(8,128)(2,1)S(1)} collective-permute-done((bf16[32,5120]{1,0:T(8,128)(2,1)S(1)}, bf16[32,5120]{1,0:T(8,128)(2,1)S(1)}, u32[]{:S(2)}, u32[]{:S(2)}) %collective-permute-start.3) | collective-permute-done | bytes 327712 | tf_op jit(solution)/shard_map/ppermute | solution.py:39
  22.4 2.5 %collective-permute-start.11 = (bf16[2,2560,128]{2,1,0:T(8,128)(2,1)S(1)}, bf16[2,2560,128]{2,1,0:T(8,128)(2,1)S(1)}, u32[]{:S(2)}, u32[]{:S(2)}) collective-permute-start(bf16[2,2560,128]{2,1,0:T(8,128)(2,1)S(1)} %shard_map.88.refs_4_.refs_3_), channel_id=1, source_target_pairs={{0,32},{1,33},{2,34},{3,35},{4,36},{5,37},{6,38},{7,39},{8,40},{9,... | collective-permute-start | bytes 3932168 | tf_op jit(solution)/shard_map/ppermute | solution.py:39
  25.0 10.4 %collective-permute-done.8.refs_6_.mine = bf16[2,2560,128]{2,1,0:T(8,128)(2,1)S(1)} collective-permute-done((bf16[2,2560,128]{2,1,0:T(8,128)(2,1)S(1)}, bf16[2,2560,128]{2,1,0:T(8,128)(2,1)S(1)}, u32[]{:S(2)}, u32[]{:S(2)}) %collective-permute-start.8) | collective-permute-done | bytes 1310752 | tf_op jit(solution)/shard_map/ppermute | solution.py:39
  35.4 2.1 %collective-permute-start.9 = (bf16[2,2560,128]{2,1,0:T(8,128)(2,1)S(1)}, bf16[2,2560,128]{2,1,0:T(8,128)(2,1)S(1)}, u32[]{:S(2)}, u32[]{:S(2)}) collective-permute-start(bf16[2,2560,128]{2,1,0:T(8,128)(2,1)S(1)} %collective-permute-done.8.refs_6_.mine), channel_id=1, source_target_pairs={{0,32},{1,33},{2,34},{3,35},{4,36},{5,37},{6,38},{7,39},{8,40},{9,... | collective-permute-start | bytes 3932168 | tf_op jit(solution)/shard_map/ppermute | solution.py:39
  40.6 2.2 %shard_map.89.refs_0_ = bf16[384,512]{1,0:T(8,128)(2,1)S(1)} custom-call(s32[1]{0:T(128)} %bitcast.2.core, bf16[128,5120]{1,0:T(8,128)(2,1)S(1)} %shard_map.83.refs_0_, bf16[128,5120]{1,0:T(8,128)(2,1)S(1)} %collective-permute-done.4.one.refs_1_, bf16[128,5120]{1,0:T(8,128)(2,1)S(1)} %collective-permute-done.5.two.refs_2_, ...), custom_call_target="tpu_custom_call" | custom-call | flops 2013265920 | bytes 1000000 | tf_op jit(solution)/shard_map/pallas_call | solution.py:215
  42.8 2.3 %collective-permute-start.12 = (bf16[384,512]{1,0:T(8,128)(2,1)S(1)}, bf16[384,512]{1,0:T(8,128)(2,1)S(1)}, u32[]{:S(2)}, u32[]{:S(2)}) collective-permute-start(bf16[384,512]{1,0:T(8,128)(2,1)S(1)} %shard_map.89.refs_0_), channel_id=1, source_target_pairs={{0,4},{1,5},{2,6},{3,7},{4,0},{5,1},{6,2},{7,3},{8,12},{9,13},{10,... | collective-permute-start | bytes 1179656 | tf_op jit(solution)/shard_map/ppermute | solution.py:39
  45.1 3.7 %collective-permute-done.6.refs_3_.refs_0_ = bf16[64,5120]{1,0:T(8,128)(2,1)S(1)} collective-permute-done((bf16[64,5120]{1,0:T(8,128)(2,1)S(1)}, bf16[64,5120]{1,0:T(8,128)(2,1)S(1)}, u32[]{:S(2)}, u32[]{:S(2)}) %collective-permute-start.6) | collective-permute-done | bytes 655392 | tf_op jit(solution)/shard_map/ppermute | solution.py:39
  49.7 2.3 %collective-permute-start.13 = (bf16[128,512]{1,0:T(8,128)(2,1)S(1)}, bf16[128,512]{1,0:T(8,128)(2,1)S(1)}, u32[]{:S(2)}, u32[]{:S(2)}) collective-permute-start(bf16[128,512]{1,0:T(8,128)(2,1)S(1)} %shard_map.90.refs_1_), channel_id=1, source_target_pairs={{0,4},{1,5},{2,6},{3,7},{4,0},{5,1},{6,2},{7,3},{8,12},{9,13},{10,... | collective-permute-start | bytes 393224 | tf_op jit(solution)/shard_map/ppermute | solution.py:39
  53.5 2.6 %collective-permute-done.13.refs_3_ = bf16[128,512]{1,0:T(8,128)(2,1)S(1)} collective-permute-done((bf16[128,512]{1,0:T(8,128)(2,1)S(1)}, bf16[128,512]{1,0:T(8,128)(2,1)S(1)}, u32[]{:S(2)}, u32[]{:S(2)}) %collective-permute-start.13) | collective-permute-done | bytes 131104 | tf_op jit(solution)/shard_map/ppermute | solution.py:39
  57.5 2.7 %collective-permute-start.17 = (bf16[64,5120]{1,0:T(8,128)(2,1)S(1)}, bf16[64,5120]{1,0:T(8,128)(2,1)S(1)}, u32[]{:S(2)}, u32[]{:S(2)}) collective-permute-start(bf16[64,5120]{1,0:T(8,128)(2,1)S(1)} %get-tuple-element.39), channel_id=1, source_target_pairs={{0,3},{1,0},{2,1},{3,2},{4,7},{5,4},{6,5},{7,6},{8,11},{9,8},{10,9... | collective-permute-start | bytes 1966088 | tf_op jit(solution)/shard_map/ppermute | solution.py:39
  60.2 1.9 %shard_map.94 = (bf16[64,5120]{1,0:T(8,128)(2,1)S(1)}, bf16[64,5120]{1,0:T(8,128)(2,1)S(1)}, bf16[64,5120]{1,0:T(8,128)(2,1)S(1)}, bf16[64,5120]{1,0:T(8,128)(2,1)S(1)}) custom-call(s32[1]{0:T(128)} %bitcast.2.core, bf16[256,256]{1,0:T(8,128)(2,1)S(1)} %get-tuple-element.36.queries, bf16[128,5120]{1,0:T(8,128)(2,1)S(1)} %copy-done.1, ...), custom_call_target="tpu_custom_call" | custom-call | flops 939524096 | bytes 1000000 | tf_op jit(solution)/shard_map/pallas_call | solution.py:269
  63.7 4.8 %collective-permute-done.16.low = bf16[64,5120]{1,0:T(8,128)(2,1)S(1)} collective-permute-done((bf16[64,5120]{1,0:T(8,128)(2,1)S(1)}, bf16[64,5120]{1,0:T(8,128)(2,1)S(1)}, u32[]{:S(2)}, u32[]{:S(2)}) %collective-permute-start.16) | collective-permute-done | bytes 655392 | tf_op jit(solution)/shard_map/ppermute | solution.py:39
  68.8 2.7 %collective-permute-start.21 = (bf16[64,5120]{1,0:T(8,128)(2,1)S(1)}, bf16[64,5120]{1,0:T(8,128)(2,1)S(1)}, u32[]{:S(2)}, u32[]{:S(2)}) collective-permute-start(bf16[64,5120]{1,0:T(8,128)(2,1)S(1)} %get-tuple-element.43), channel_id=1, source_target_pairs={{0,3},{1,0},{2,1},{3,2},{4,7},{5,4},{6,5},{7,6},{8,11},{9,8},{10,9... | collective-permute-start | bytes 1966088 | tf_op jit(solution)/shard_map/ppermute | solution.py:39
  74.0 5.4 %collective-permute-done.14.own_start = f32[16,5120]{1,0:T(8,128)S(1)} collective-permute-done((f32[16,5120]{1,0:T(8,128)S(1)}, f32[16,5120]{1,0:T(8,128)S(1)}, u32[]{:S(2)}, u32[]{:S(2)}) %collective-permute-start.14) | collective-permute-done | bytes 327712 | tf_op jit(solution)/shard_map/ppermute | solution.py:39
  79.4 5.4 %collective-permute-start.15 = (f32[16,5120]{1,0:T(8,128)S(1)}, f32[16,5120]{1,0:T(8,128)S(1)}, u32[]{:S(2)}, u32[]{:S(2)}) collective-permute-start(f32[16,5120]{1,0:T(8,128)S(1)} %collective-permute-done.14.own_start), channel_id=1, source_target_pairs={{0,32},{1,33},{2,34},{3,35},{4,36},{5,37},{6,38},{7,39},{8,40},{9,... | collective-permute-start | bytes 983048 | tf_op jit(solution)/shard_map/ppermute | solution.py:39
  87.4 1.9 %collective-permute-start.24 = (bf16[32,5120]{1,0:T(8,128)(2,1)S(1)}, bf16[32,5120]{1,0:T(8,128)(2,1)S(1)}, u32[]{:S(2)}, u32[]{:S(2)}) collective-permute-start(bf16[32,5120]{1,0:T(8,128)(2,1)S(1)} %get-tuple-element.47), channel_id=1, source_target_pairs={{0,24},{1,25},{2,26},{3,27},{4,28},{5,29},{6,30},{7,31},{8,0},{9,1... | collective-permute-start | bytes 983048 | tf_op jit(solution)/shard_map/ppermute | solution.py:39
  89.3 4.0 %collective-permute-done.22.one = bf16[32,5120]{1,0:T(8,128)(2,1)S(1)} collective-permute-done((bf16[32,5120]{1,0:T(8,128)(2,1)S(1)}, bf16[32,5120]{1,0:T(8,128)(2,1)S(1)}, u32[]{:S(2)}, u32[]{:S(2)}) %collective-permute-start.22) | collective-permute-done | bytes 327712 | tf_op jit(solution)/shard_map/ppermute | solution.py:39
  93.2 3.5 %collective-permute-done.23.two = bf16[32,5120]{1,0:T(8,128)(2,1)S(1)} collective-permute-done((bf16[32,5120]{1,0:T(8,128)(2,1)S(1)}, bf16[32,5120]{1,0:T(8,128)(2,1)S(1)}, u32[]{:S(2)}, u32[]{:S(2)}) %collective-permute-start.23) | collective-permute-done | bytes 327712 | tf_op jit(solution)/shard_map/ppermute | solution.py:39
  97.5 2.6 %collective-permute-start.25 = (bf16[32,5120]{1,0:T(8,128)(2,1)S(1)}, bf16[32,5120]{1,0:T(8,128)(2,1)S(1)}, u32[]{:S(2)}, u32[]{:S(2)}) collective-permute-start(bf16[32,5120]{1,0:T(8,128)(2,1)S(1)} %get-tuple-element.50), channel_id=1, source_target_pairs={{0,32},{1,33},{2,34},{3,35},{4,36},{5,37},{6,38},{7,39},{8,40},{9,... | collective-permute-start | bytes 983048 | tf_op jit(solution)/shard_map/ppermute | solution.py:39
  101.5 6.9 %collective-permute-done.26.own_sum = bf16[16,5120]{1,0:T(8,128)(2,1)S(1)} collective-permute-done((bf16[16,5120]{1,0:T(8,128)(2,1)S(1)}, bf16[16,5120]{1,0:T(8,128)(2,1)S(1)}, u32[]{:S(2)}, u32[]{:S(2)}) %collective-permute-start.26) | collective-permute-done | bytes 163872 | tf_op jit(solution)/shard_map/ppermute | solution.py:39
  (64 shorter events, 28.3 us)
Async XLA Ops:
  4.6 17.8 %collective-permute-start.10 = (bf16[2,2560,128]{2,1,0:T(8,128)(2,1)S(1)}, bf16[2,2560,128]{2,1,0:T(8,128)(2,1)S(1)}, u32[]{:S(2)}, u32[]{:S(2)}) collective-permute-start(bf16[2,2560,128]{2,1,0:T(8,128)(2,1)S(1)} %shard_map.87), channel_id=1, source_target_pairs={{0,4},{1,5},{2,6},{3,7},{4,0},{5,1},{6,2},{7,3},{8,12},{9,13},{10,... | collective-permute-start | bytes 3932168 | tf_op jit(solution)/shard_map/ppermute | solution.py:39
  4.8 8.5 %collective-permute-start.1 = (bf16[32,5120]{1,0:T(8,128)(2,1)S(1)}, bf16[32,5120]{1,0:T(8,128)(2,1)S(1)}, u32[]{:S(2)}, u32[]{:S(2)}) collective-permute-start(bf16[32,5120]{1,0:T(8,128)(2,1)S(1)} %copy-done.3), channel_id=1, source_target_pairs={{0,8},{1,9},{2,10},{3,11},{4,12},{5,13},{6,14},{7,15},{8,16},{9,17... | collective-permute-start | bytes 983048 | tf_op jit(solution)/shard_map/ppermute | solution.py:39
  6.4 9.7 %collective-permute-start.2 = (bf16[32,5120]{1,0:T(8,128)(2,1)S(1)}, bf16[32,5120]{1,0:T(8,128)(2,1)S(1)}, u32[]{:S(2)}, u32[]{:S(2)}) collective-permute-start(bf16[32,5120]{1,0:T(8,128)(2,1)S(1)} %copy-done.3), channel_id=1, source_target_pairs={{0,24},{1,25},{2,26},{3,27},{4,28},{5,29},{6,30},{7,31},{8,0},{9,1... | collective-permute-start | bytes 983048 | tf_op jit(solution)/shard_map/ppermute | solution.py:39
  8.6 9.4 %collective-permute-start.3 = (bf16[32,5120]{1,0:T(8,128)(2,1)S(1)}, bf16[32,5120]{1,0:T(8,128)(2,1)S(1)}, u32[]{:S(2)}, u32[]{:S(2)}) collective-permute-start(bf16[32,5120]{1,0:T(8,128)(2,1)S(1)} %copy-done.3), channel_id=1, source_target_pairs={{0,16},{1,17},{2,18},{3,19},{4,20},{5,21},{6,22},{7,23},{8,24},{9,... | collective-permute-start | bytes 983048 | tf_op jit(solution)/shard_map/ppermute | solution.py:39
  18.4 17.0 %collective-permute-start.8 = (bf16[2,2560,128]{2,1,0:T(8,128)(2,1)S(1)}, bf16[2,2560,128]{2,1,0:T(8,128)(2,1)S(1)}, u32[]{:S(2)}, u32[]{:S(2)}) collective-permute-start(bf16[2,2560,128]{2,1,0:T(8,128)(2,1)S(1)} %shard_map.85), channel_id=1, source_target_pairs={{0,4},{1,5},{2,6},{3,7},{4,0},{5,1},{6,2},{7,3},{8,12},{9,13},{10,... | collective-permute-start | bytes 3932168 | tf_op jit(solution)/shard_map/ppermute | solution.py:39
  19.6 18.0 %collective-permute-start.4 = (bf16[128,5120]{1,0:T(8,128)(2,1)S(1)}, bf16[128,5120]{1,0:T(8,128)(2,1)S(1)}, u32[]{:S(2)}, u32[]{:S(2)}) collective-permute-start(bf16[128,5120]{1,0:T(8,128)(2,1)S(1)} %shard_map.83.refs_0_), channel_id=1, source_target_pairs={{0,1},{1,2},{2,3},{3,0},{4,5},{5,6},{6,7},{7,4},{8,9},{9,10},{10,1... | collective-permute-start | bytes 3932168 | tf_op jit(solution)/shard_map/ppermute | solution.py:39
  20.9 16.8 %collective-permute-start.5 = (bf16[128,5120]{1,0:T(8,128)(2,1)S(1)}, bf16[128,5120]{1,0:T(8,128)(2,1)S(1)}, u32[]{:S(2)}, u32[]{:S(2)}) collective-permute-start(bf16[128,5120]{1,0:T(8,128)(2,1)S(1)} %shard_map.83.refs_0_), channel_id=1, source_target_pairs={{0,3},{1,0},{2,1},{3,2},{4,7},{5,4},{6,5},{7,6},{8,11},{9,8},{10,9... | collective-permute-start | bytes 3932168 | tf_op jit(solution)/shard_map/ppermute | solution.py:39
  22.4 18.2 %collective-permute-start.11 = (bf16[2,2560,128]{2,1,0:T(8,128)(2,1)S(1)}, bf16[2,2560,128]{2,1,0:T(8,128)(2,1)S(1)}, u32[]{:S(2)}, u32[]{:S(2)}) collective-permute-start(bf16[2,2560,128]{2,1,0:T(8,128)(2,1)S(1)} %shard_map.88.refs_4_.refs_3_), channel_id=1, source_target_pairs={{0,32},{1,33},{2,34},{3,35},{4,36},{5,37},{6,38},{7,39},{8,40},{9,... | collective-permute-start | bytes 3932168 | tf_op jit(solution)/shard_map/ppermute | solution.py:39
  24.9 12.6 %collective-permute-start = (f32[32,5120]{1,0:T(8,128)S(1)}, f32[32,5120]{1,0:T(8,128)S(1)}, u32[]{:S(2)}, u32[]{:S(2)}) collective-permute-start(f32[32,5120]{1,0:T(8,128)S(1)} %bitcast.5), channel_id=1, source_target_pairs={{0,32},{1,33},{2,34},{3,35},{4,36},{5,37},{6,38},{7,39},{8,40},{9,... | collective-permute-start | bytes 1966088 | tf_op jit(solution)/shard_map/ppermute | solution.py:39
  35.4 16.5 %collective-permute-start.9 = (bf16[2,2560,128]{2,1,0:T(8,128)(2,1)S(1)}, bf16[2,2560,128]{2,1,0:T(8,128)(2,1)S(1)}, u32[]{:S(2)}, u32[]{:S(2)}) collective-permute-start(bf16[2,2560,128]{2,1,0:T(8,128)(2,1)S(1)} %collective-permute-done.8.refs_6_.mine), channel_id=1, source_target_pairs={{0,32},{1,33},{2,34},{3,35},{4,36},{5,37},{6,38},{7,39},{8,40},{9,... | collective-permute-start | bytes 3932168 | tf_op jit(solution)/shard_map/ppermute | solution.py:39
  37.8 11.0 %collective-permute-start.6 = (bf16[64,5120]{1,0:T(8,128)(2,1)S(1)}, bf16[64,5120]{1,0:T(8,128)(2,1)S(1)}, u32[]{:S(2)}, u32[]{:S(2)}) collective-permute-start(bf16[64,5120]{1,0:T(8,128)(2,1)S(1)} %get-tuple-element.29), channel_id=1, source_target_pairs={{0,1},{1,2},{2,3},{3,0},{4,5},{5,6},{6,7},{7,4},{8,9},{9,10},{10,1... | collective-permute-start | bytes 1966088 | tf_op jit(solution)/shard_map/ppermute | solution.py:39
  39.0 9.7 %collective-permute-start.7 = (bf16[64,5120]{1,0:T(8,128)(2,1)S(1)}, bf16[64,5120]{1,0:T(8,128)(2,1)S(1)}, u32[]{:S(2)}, u32[]{:S(2)}) collective-permute-start(bf16[64,5120]{1,0:T(8,128)(2,1)S(1)} %get-tuple-element.30), channel_id=1, source_target_pairs={{0,3},{1,0},{2,1},{3,2},{4,7},{5,4},{6,5},{7,6},{8,11},{9,8},{10,9... | collective-permute-start | bytes 1966088 | tf_op jit(solution)/shard_map/ppermute | solution.py:39
  42.8 13.3 %collective-permute-start.12 = (bf16[384,512]{1,0:T(8,128)(2,1)S(1)}, bf16[384,512]{1,0:T(8,128)(2,1)S(1)}, u32[]{:S(2)}, u32[]{:S(2)}) collective-permute-start(bf16[384,512]{1,0:T(8,128)(2,1)S(1)} %shard_map.89.refs_0_), channel_id=1, source_target_pairs={{0,4},{1,5},{2,6},{3,7},{4,0},{5,1},{6,2},{7,3},{8,12},{9,13},{10,... | collective-permute-start | bytes 1179656 | tf_op jit(solution)/shard_map/ppermute | solution.py:39
  57.4 11.0 %collective-permute-start.16 = (bf16[64,5120]{1,0:T(8,128)(2,1)S(1)}, bf16[64,5120]{1,0:T(8,128)(2,1)S(1)}, u32[]{:S(2)}, u32[]{:S(2)}) collective-permute-start(bf16[64,5120]{1,0:T(8,128)(2,1)S(1)} %get-tuple-element.32.until), channel_id=1, source_target_pairs={{0,1},{1,2},{2,3},{3,0},{4,5},{5,6},{6,7},{7,4},{8,9},{9,10},{10,1... | collective-permute-start | bytes 1966088 | tf_op jit(solution)/shard_map/ppermute | solution.py:39
  57.5 10.9 %collective-permute-start.17 = (bf16[64,5120]{1,0:T(8,128)(2,1)S(1)}, bf16[64,5120]{1,0:T(8,128)(2,1)S(1)}, u32[]{:S(2)}, u32[]{:S(2)}) collective-permute-start(bf16[64,5120]{1,0:T(8,128)(2,1)S(1)} %get-tuple-element.39), channel_id=1, source_target_pairs={{0,3},{1,0},{2,1},{3,2},{4,7},{5,4},{6,5},{7,6},{8,11},{9,8},{10,9... | collective-permute-start | bytes 1966088 | tf_op jit(solution)/shard_map/ppermute | solution.py:39
  62.1 22.7 %collective-permute-start.19 = (bf16[64,5120]{1,0:T(8,128)(2,1)S(1)}, bf16[64,5120]{1,0:T(8,128)(2,1)S(1)}, u32[]{:S(2)}, u32[]{:S(2)}) collective-permute-start(bf16[64,5120]{1,0:T(8,128)(2,1)S(1)} %get-tuple-element.41), channel_id=1, source_target_pairs={{0,3},{1,0},{2,1},{3,2},{4,7},{5,4},{6,5},{7,6},{8,11},{9,8},{10,9... | collective-permute-start | bytes 1966088 | tf_op jit(solution)/shard_map/ppermute | solution.py:39
  62.2 22.7 %collective-permute-start.20 = (bf16[64,5120]{1,0:T(8,128)(2,1)S(1)}, bf16[64,5120]{1,0:T(8,128)(2,1)S(1)}, u32[]{:S(2)}, u32[]{:S(2)}) collective-permute-start(bf16[64,5120]{1,0:T(8,128)(2,1)S(1)} %get-tuple-element.42), channel_id=1, source_target_pairs={{0,1},{1,2},{2,3},{3,0},{4,5},{5,6},{6,7},{7,4},{8,9},{9,10},{10,1... | collective-permute-start | bytes 1966088 | tf_op jit(solution)/shard_map/ppermute | solution.py:39
  68.8 16.1 %collective-permute-start.18 = (bf16[64,5120]{1,0:T(8,128)(2,1)S(1)}, bf16[64,5120]{1,0:T(8,128)(2,1)S(1)}, u32[]{:S(2)}, u32[]{:S(2)}) collective-permute-start(bf16[64,5120]{1,0:T(8,128)(2,1)S(1)} %get-tuple-element.40), channel_id=1, source_target_pairs={{0,1},{1,2},{2,3},{3,0},{4,5},{5,6},{6,7},{7,4},{8,9},{9,10},{10,1... | collective-permute-start | bytes 1966088 | tf_op jit(solution)/shard_map/ppermute | solution.py:39
  68.8 16.0 %collective-permute-start.21 = (bf16[64,5120]{1,0:T(8,128)(2,1)S(1)}, bf16[64,5120]{1,0:T(8,128)(2,1)S(1)}, u32[]{:S(2)}, u32[]{:S(2)}) collective-permute-start(bf16[64,5120]{1,0:T(8,128)(2,1)S(1)} %get-tuple-element.43), channel_id=1, source_target_pairs={{0,3},{1,0},{2,1},{3,2},{4,7},{5,4},{6,5},{7,6},{8,11},{9,8},{10,9... | collective-permute-start | bytes 1966088 | tf_op jit(solution)/shard_map/ppermute | solution.py:39
  71.6 7.8 %collective-permute-start.14 = (f32[16,5120]{1,0:T(8,128)S(1)}, f32[16,5120]{1,0:T(8,128)S(1)}, u32[]{:S(2)}, u32[]{:S(2)}) collective-permute-start(f32[16,5120]{1,0:T(8,128)S(1)} %shard_map.92), channel_id=1, source_target_pairs={{0,64},{1,65},{2,66},{3,67},{4,68},{5,69},{6,70},{7,71},{8,72},{9,... | collective-permute-start | bytes 983048 | tf_op jit(solution)/shard_map/ppermute | solution.py:39
  79.4 9.9 %collective-permute-start.15 = (f32[16,5120]{1,0:T(8,128)S(1)}, f32[16,5120]{1,0:T(8,128)S(1)}, u32[]{:S(2)}, u32[]{:S(2)}) collective-permute-start(f32[16,5120]{1,0:T(8,128)S(1)} %collective-permute-done.14.own_start), channel_id=1, source_target_pairs={{0,32},{1,33},{2,34},{3,35},{4,36},{5,37},{6,38},{7,39},{8,40},{9,... | collective-permute-start | bytes 983048 | tf_op jit(solution)/shard_map/ppermute | solution.py:39
  85.4 7.8 %collective-permute-start.22 = (bf16[32,5120]{1,0:T(8,128)(2,1)S(1)}, bf16[32,5120]{1,0:T(8,128)(2,1)S(1)}, u32[]{:S(2)}, u32[]{:S(2)}) collective-permute-start(bf16[32,5120]{1,0:T(8,128)(2,1)S(1)} %get-tuple-element.45), channel_id=1, source_target_pairs={{0,16},{1,17},{2,18},{3,19},{4,20},{5,21},{6,22},{7,23},{8,24},{9,... | collective-permute-start | bytes 983048 | tf_op jit(solution)/shard_map/ppermute | solution.py:39
  86.6 10.1 %collective-permute-start.23 = (bf16[32,5120]{1,0:T(8,128)(2,1)S(1)}, bf16[32,5120]{1,0:T(8,128)(2,1)S(1)}, u32[]{:S(2)}, u32[]{:S(2)}) collective-permute-start(bf16[32,5120]{1,0:T(8,128)(2,1)S(1)} %get-tuple-element.46), channel_id=1, source_target_pairs={{0,8},{1,9},{2,10},{3,11},{4,12},{5,13},{6,14},{7,15},{8,16},{9,17... | collective-permute-start | bytes 983048 | tf_op jit(solution)/shard_map/ppermute | solution.py:39
  87.4 9.3 %collective-permute-start.24 = (bf16[32,5120]{1,0:T(8,128)(2,1)S(1)}, bf16[32,5120]{1,0:T(8,128)(2,1)S(1)}, u32[]{:S(2)}, u32[]{:S(2)}) collective-permute-start(bf16[32,5120]{1,0:T(8,128)(2,1)S(1)} %get-tuple-element.47), channel_id=1, source_target_pairs={{0,24},{1,25},{2,26},{3,27},{4,28},{5,29},{6,30},{7,31},{8,0},{9,1... | collective-permute-start | bytes 983048 | tf_op jit(solution)/shard_map/ppermute | solution.py:39
  (11 other events, 80.8 us)

commit v8 on v7

--- a/solution.py
+++ b/solution.py
@@ -429,7 +429,7 @@
     minus, plus, opposite = [send(modulated, first_axis(s)) for s in (1, -1, 2)]
     near = stack(modulated, minus, plus, opposite)
     before, after = send(near, second_axis(1)), send(near, second_axis(-1))
-    kv_mine = send(pack((1, 2), core, qkv_weight, modulated), to_both_sides)
+    kv_mine = send(pack((1, 2), core, qkv_weight, gates), to_both_sides)
     qo_mine = send(pack((0, 3), core, qkv_weight, out_weight, minus, plus, opposite), to_both_sides)
     before_half, after_half = first_and_second_half(before, after, near_start)
     last = [send(before_half, second_axis(1)), send(after_half, second_axis(-1))]

time: 113 us -> 112 us (level)
  no operation moved by 1% of the time
where the time goes in v8:
time: 112 us; the launch traced here: 111 us
  waiting for transfers between devices  51.5 us (46%)
  starting transfers between devices  42.7 us (38%)
  Pallas kernels  15.4 us (14%)
  local copies, waits for them, and re-layouts  1.13 us (1%)
    ppermute x28, waiting for transfers between devices, send(): return lax.ppermute(value, ('tm', 'seq'), moves(rule))  51.5 us
    ppermute x28, starting transfers between devices, send(): return lax.ppermute(value, ('tm', 'seq'), moves(rule))  42.7 us
    pallas_call x3, Pallas kernels, project(): pl.pallas_call(functools.partial(project_kernel, len(pieces), kinds, rows...  4.65 us
    pallas_call x3, Pallas kernels, attend(): pl.pallas_call(functools.partial(attend_kernel, len(near), cuts), out_sha...  4.63 us
    pallas_call x1, Pallas kernels, modulate(): pl.pallas_call(modulate_kernel, grid_spec=pltpu.PrefetchScalarGridSpec(nu...  2.39 us
  transfers between devices with their start and end apart: 28, of which 14 were waited for; matrix products, arithmetic and copies ran while one was open for 0% of the time, Pallas kernels for 8%

profile of v8, /device:TPU:17, one launch (start us, length us, event | category | flops | bytes accessed | tf_op | source)
XLA Modules:
  0.0 111.5 jit_solution(961670712194983446)
XLA Ops:
  0.7 2.4 %shard_map.82 = (bf16[32,5120]{1,0:T(8,128)(2,1)}, f32[1,5120]{1,0:T(1,128)}) custom-call(s32[1]{0:T(128)S(6)} %add.4.index, f32[32,5120]{1,0:T(8,128)} %bitcast.4, f32[50,5120]{1,0:T(8,128)} %scale.1, f32[50,5120]{1,0:T(8,128)} %shift.1, f32[50,5120]{1,0:T(8,128)} %gate.1), custom_call_target="tpu_custom_call" | custom-call | flops 1000000 | bytes 2000000 | tf_op jit(solution)/shard_map/pallas_call | solution.py:83
  6.5 2.1 %collective-permute-start.2 = (bf16[32,5120]{1,0:T(8,128)(2,1)S(1)}, bf16[32,5120]{1,0:T(8,128)(2,1)S(1)}, u32[]{:S(2)}, u32[]{:S(2)}) collective-permute-start(bf16[32,5120]{1,0:T(8,128)(2,1)S(1)} %copy-done.3), channel_id=1, source_target_pairs={{0,24},{1,25},{2,26},{3,27},{4,28},{5,29},{6,30},{7,31},{8,0},{9,1... | collective-permute-start | bytes 983048 | tf_op jit(solution)/shard_map/ppermute | solution.py:39
  9.9 3.5 %collective-permute-done.1.refs_1_ = bf16[32,5120]{1,0:T(8,128)(2,1)S(1)} collective-permute-done((bf16[32,5120]{1,0:T(8,128)(2,1)S(1)}, bf16[32,5120]{1,0:T(8,128)(2,1)S(1)}, u32[]{:S(2)}, u32[]{:S(2)}) %collective-permute-start.1) | collective-permute-done | bytes 327712 | tf_op jit(solution)/shard_map/ppermute | solution.py:39
  13.4 2.8 %collective-permute-done.2.refs_2_ = bf16[32,5120]{1,0:T(8,128)(2,1)S(1)} collective-permute-done((bf16[32,5120]{1,0:T(8,128)(2,1)S(1)}, bf16[32,5120]{1,0:T(8,128)(2,1)S(1)}, u32[]{:S(2)}, u32[]{:S(2)}) %collective-permute-start.2) | collective-permute-done | bytes 327712 | tf_op jit(solution)/shard_map/ppermute | solution.py:39
  16.1 1.9 %collective-permute-done.3.refs_3_ = bf16[32,5120]{1,0:T(8,128)(2,1)S(1)} collective-permute-done((bf16[32,5120]{1,0:T(8,128)(2,1)S(1)}, bf16[32,5120]{1,0:T(8,128)(2,1)S(1)}, u32[]{:S(2)}, u32[]{:S(2)}) %collective-permute-start.3) | collective-permute-done | bytes 327712 | tf_op jit(solution)/shard_map/ppermute | solution.py:39
  22.1 2.5 %collective-permute-start.11 = (bf16[2,2560,128]{2,1,0:T(8,128)(2,1)S(1)}, bf16[2,2560,128]{2,1,0:T(8,128)(2,1)S(1)}, u32[]{:S(2)}, u32[]{:S(2)}) collective-permute-start(bf16[2,2560,128]{2,1,0:T(8,128)(2,1)S(1)} %shard_map.88.refs_4_.refs_3_), channel_id=1, source_target_pairs={{0,32},{1,33},{2,34},{3,35},{4,36},{5,37},{6,38},{7,39},{8,40},{9,... | collective-permute-start | bytes 3932168 | tf_op jit(solution)/shard_map/ppermute | solution.py:39
  24.8 10.6 %collective-permute-done.8.refs_6_.mine = bf16[2,2560,128]{2,1,0:T(8,128)(2,1)S(1)} collective-permute-done((bf16[2,2560,128]{2,1,0:T(8,128)(2,1)S(1)}, bf16[2,2560,128]{2,1,0:T(8,128)(2,1)S(1)}, u32[]{:S(2)}, u32[]{:S(2)}) %collective-permute-start.8) | collective-permute-done | bytes 1310752 | tf_op jit(solution)/shard_map/ppermute | solution.py:39
  35.3 1.9 %collective-permute-start.9 = (bf16[2,2560,128]{2,1,0:T(8,128)(2,1)S(1)}, bf16[2,2560,128]{2,1,0:T(8,128)(2,1)S(1)}, u32[]{:S(2)}, u32[]{:S(2)}) collective-permute-start(bf16[2,2560,128]{2,1,0:T(8,128)(2,1)S(1)} %collective-permute-done.8.refs_6_.mine), channel_id=1, source_target_pairs={{0,32},{1,33},{2,34},{3,35},{4,36},{5,37},{6,38},{7,39},{8,40},{9,... | collective-permute-start | bytes 3932168 | tf_op jit(solution)/shard_map/ppermute | solution.py:39
  40.3 2.2 %shard_map.89.refs_0_ = bf16[384,512]{1,0:T(8,128)(2,1)S(1)} custom-call(s32[1]{0:T(128)} %bitcast.2.core, bf16[128,5120]{1,0:T(8,128)(2,1)S(1)} %shard_map.83.refs_0_, bf16[128,5120]{1,0:T(8,128)(2,1)S(1)} %collective-permute-done.4.one.refs_1_, bf16[128,5120]{1,0:T(8,128)(2,1)S(1)} %collective-permute-done.5.two.refs_2_, ...), custom_call_target="tpu_custom_call" | custom-call | flops 2013265920 | bytes 1000000 | tf_op jit(solution)/shard_map/pallas_call | solution.py:215
  42.6 2.3 %collective-permute-start.12 = (bf16[384,512]{1,0:T(8,128)(2,1)S(1)}, bf16[384,512]{1,0:T(8,128)(2,1)S(1)}, u32[]{:S(2)}, u32[]{:S(2)}) collective-permute-start(bf16[384,512]{1,0:T(8,128)(2,1)S(1)} %shard_map.89.refs_0_), channel_id=1, source_target_pairs={{0,4},{1,5},{2,6},{3,7},{4,0},{5,1},{6,2},{7,3},{8,12},{9,13},{10,... | collective-permute-start | bytes 1179656 | tf_op jit(solution)/shard_map/ppermute | solution.py:39
  44.9 3.7 %collective-permute-done.6.refs_3_.refs_0_ = bf16[64,5120]{1,0:T(8,128)(2,1)S(1)} collective-permute-done((bf16[64,5120]{1,0:T(8,128)(2,1)S(1)}, bf16[64,5120]{1,0:T(8,128)(2,1)S(1)}, u32[]{:S(2)}, u32[]{:S(2)}) %collective-permute-start.6) | collective-permute-done | bytes 655392 | tf_op jit(solution)/shard_map/ppermute | solution.py:39
  49.4 2.3 %collective-permute-start.13 = (bf16[128,512]{1,0:T(8,128)(2,1)S(1)}, bf16[128,512]{1,0:T(8,128)(2,1)S(1)}, u32[]{:S(2)}, u32[]{:S(2)}) collective-permute-start(bf16[128,512]{1,0:T(8,128)(2,1)S(1)} %shard_map.90.refs_1_), channel_id=1, source_target_pairs={{0,4},{1,5},{2,6},{3,7},{4,0},{5,1},{6,2},{7,3},{8,12},{9,13},{10,... | collective-permute-start | bytes 393224 | tf_op jit(solution)/shard_map/ppermute | solution.py:39
  53.2 2.6 %collective-permute-done.13.refs_3_ = bf16[128,512]{1,0:T(8,128)(2,1)S(1)} collective-permute-done((bf16[128,512]{1,0:T(8,128)(2,1)S(1)}, bf16[128,512]{1,0:T(8,128)(2,1)S(1)}, u32[]{:S(2)}, u32[]{:S(2)}) %collective-permute-start.13) | collective-permute-done | bytes 131104 | tf_op jit(solution)/shard_map/ppermute | solution.py:39
  57.2 2.7 %collective-permute-start.17 = (bf16[64,5120]{1,0:T(8,128)(2,1)S(1)}, bf16[64,5120]{1,0:T(8,128)(2,1)S(1)}, u32[]{:S(2)}, u32[]{:S(2)}) collective-permute-start(bf16[64,5120]{1,0:T(8,128)(2,1)S(1)} %get-tuple-element.40), channel_id=1, source_target_pairs={{0,3},{1,0},{2,1},{3,2},{4,7},{5,4},{6,5},{7,6},{8,11},{9,8},{10,9... | collective-permute-start | bytes 1966088 | tf_op jit(solution)/shard_map/ppermute | solution.py:39
  59.9 1.9 %shard_map.94 = (bf16[64,5120]{1,0:T(8,128)(2,1)S(1)}, bf16[64,5120]{1,0:T(8,128)(2,1)S(1)}, bf16[64,5120]{1,0:T(8,128)(2,1)S(1)}, bf16[64,5120]{1,0:T(8,128)(2,1)S(1)}) custom-call(s32[1]{0:T(128)} %bitcast.2.core, bf16[256,256]{1,0:T(8,128)(2,1)S(1)} %get-tuple-element.37.queries, bf16[128,5120]{1,0:T(8,128)(2,1)S(1)} %copy-done.1, ...), custom_call_target="tpu_custom_call" | custom-call | flops 939524096 | bytes 1000000 | tf_op jit(solution)/shard_map/pallas_call | solution.py:269
  63.4 4.8 %collective-permute-done.16.low = bf16[64,5120]{1,0:T(8,128)(2,1)S(1)} collective-permute-done((bf16[64,5120]{1,0:T(8,128)(2,1)S(1)}, bf16[64,5120]{1,0:T(8,128)(2,1)S(1)}, u32[]{:S(2)}, u32[]{:S(2)}) %collective-permute-start.16) | collective-permute-done | bytes 655392 | tf_op jit(solution)/shard_map/ppermute | solution.py:39
  68.6 2.7 %collective-permute-start.21 = (bf16[64,5120]{1,0:T(8,128)(2,1)S(1)}, bf16[64,5120]{1,0:T(8,128)(2,1)S(1)}, u32[]{:S(2)}, u32[]{:S(2)}) collective-permute-start(bf16[64,5120]{1,0:T(8,128)(2,1)S(1)} %get-tuple-element.44), channel_id=1, source_target_pairs={{0,3},{1,0},{2,1},{3,2},{4,7},{5,4},{6,5},{7,6},{8,11},{9,8},{10,9... | collective-permute-start | bytes 1966088 | tf_op jit(solution)/shard_map/ppermute | solution.py:39
  74.1 5.0 %collective-permute-done.14.own_start = f32[16,5120]{1,0:T(8,128)S(1)} collective-permute-done((f32[16,5120]{1,0:T(8,128)S(1)}, f32[16,5120]{1,0:T(8,128)S(1)}, u32[]{:S(2)}, u32[]{:S(2)}) %collective-permute-start.14) | collective-permute-done | bytes 327712 | tf_op jit(solution)/shard_map/ppermute | solution.py:39
  79.2 5.5 %collective-permute-start.15 = (f32[16,5120]{1,0:T(8,128)S(1)}, f32[16,5120]{1,0:T(8,128)S(1)}, u32[]{:S(2)}, u32[]{:S(2)}) collective-permute-start(f32[16,5120]{1,0:T(8,128)S(1)} %collective-permute-done.14.own_start), channel_id=1, source_target_pairs={{0,32},{1,33},{2,34},{3,35},{4,36},{5,37},{6,38},{7,39},{8,40},{9,... | collective-permute-start | bytes 983048 | tf_op jit(solution)/shard_map/ppermute | solution.py:39
  87.1 1.9 %collective-permute-start.24 = (bf16[32,5120]{1,0:T(8,128)(2,1)S(1)}, bf16[32,5120]{1,0:T(8,128)(2,1)S(1)}, u32[]{:S(2)}, u32[]{:S(2)}) collective-permute-start(bf16[32,5120]{1,0:T(8,128)(2,1)S(1)} %get-tuple-element.48), channel_id=1, source_target_pairs={{0,24},{1,25},{2,26},{3,27},{4,28},{5,29},{6,30},{7,31},{8,0},{9,1... | collective-permute-start | bytes 983048 | tf_op jit(solution)/shard_map/ppermute | solution.py:39
  89.0 3.9 %collective-permute-done.22.one = bf16[32,5120]{1,0:T(8,128)(2,1)S(1)} collective-permute-done((bf16[32,5120]{1,0:T(8,128)(2,1)S(1)}, bf16[32,5120]{1,0:T(8,128)(2,1)S(1)}, u32[]{:S(2)}, u32[]{:S(2)}) %collective-permute-start.22) | collective-permute-done | bytes 327712 | tf_op jit(solution)/shard_map/ppermute | solution.py:39
  93.0 3.5 %collective-permute-done.23.two = bf16[32,5120]{1,0:T(8,128)(2,1)S(1)} collective-permute-done((bf16[32,5120]{1,0:T(8,128)(2,1)S(1)}, bf16[32,5120]{1,0:T(8,128)(2,1)S(1)}, u32[]{:S(2)}, u32[]{:S(2)}) %collective-permute-start.23) | collective-permute-done | bytes 327712 | tf_op jit(solution)/shard_map/ppermute | solution.py:39
  97.2 2.6 %collective-permute-start.25 = (bf16[32,5120]{1,0:T(8,128)(2,1)S(1)}, bf16[32,5120]{1,0:T(8,128)(2,1)S(1)}, u32[]{:S(2)}, u32[]{:S(2)}) collective-permute-start(bf16[32,5120]{1,0:T(8,128)(2,1)S(1)} %get-tuple-element.50), channel_id=1, source_target_pairs={{0,32},{1,33},{2,34},{3,35},{4,36},{5,37},{6,38},{7,39},{8,40},{9,... | collective-permute-start | bytes 983048 | tf_op jit(solution)/shard_map/ppermute | solution.py:39
  101.3 6.8 %collective-permute-done.26.own_sum = bf16[16,5120]{1,0:T(8,128)(2,1)S(1)} collective-permute-done((bf16[16,5120]{1,0:T(8,128)(2,1)S(1)}, bf16[16,5120]{1,0:T(8,128)(2,1)S(1)}, u32[]{:S(2)}, u32[]{:S(2)}) %collective-permute-start.26) | collective-permute-done | bytes 163872 | tf_op jit(solution)/shard_map/ppermute | solution.py:39
  (64 shorter events, 28.5 us)
Async XLA Ops:
  4.3 17.8 %collective-permute-start.10 = (bf16[2,2560,128]{2,1,0:T(8,128)(2,1)S(1)}, bf16[2,2560,128]{2,1,0:T(8,128)(2,1)S(1)}, u32[]{:S(2)}, u32[]{:S(2)}) collective-permute-start(bf16[2,2560,128]{2,1,0:T(8,128)(2,1)S(1)} %shard_map.87), channel_id=1, source_target_pairs={{0,4},{1,5},{2,6},{3,7},{4,0},{5,1},{6,2},{7,3},{8,12},{9,13},{10,... | collective-permute-start | bytes 3932168 | tf_op jit(solution)/shard_map/ppermute | solution.py:39
  4.8 8.5 %collective-permute-start.1 = (bf16[32,5120]{1,0:T(8,128)(2,1)S(1)}, bf16[32,5120]{1,0:T(8,128)(2,1)S(1)}, u32[]{:S(2)}, u32[]{:S(2)}) collective-permute-start(bf16[32,5120]{1,0:T(8,128)(2,1)S(1)} %copy-done.3), channel_id=1, source_target_pairs={{0,8},{1,9},{2,10},{3,11},{4,12},{5,13},{6,14},{7,15},{8,16},{9,17... | collective-permute-start | bytes 983048 | tf_op jit(solution)/shard_map/ppermute | solution.py:39
  6.5 9.7 %collective-permute-start.2 = (bf16[32,5120]{1,0:T(8,128)(2,1)S(1)}, bf16[32,5120]{1,0:T(8,128)(2,1)S(1)}, u32[]{:S(2)}, u32[]{:S(2)}) collective-permute-start(bf16[32,5120]{1,0:T(8,128)(2,1)S(1)} %copy-done.3), channel_id=1, source_target_pairs={{0,24},{1,25},{2,26},{3,27},{4,28},{5,29},{6,30},{7,31},{8,0},{9,1... | collective-permute-start | bytes 983048 | tf_op jit(solution)/shard_map/ppermute | solution.py:39
  8.6 9.4 %collective-permute-start.3 = (bf16[32,5120]{1,0:T(8,128)(2,1)S(1)}, bf16[32,5120]{1,0:T(8,128)(2,1)S(1)}, u32[]{:S(2)}, u32[]{:S(2)}) collective-permute-start(bf16[32,5120]{1,0:T(8,128)(2,1)S(1)} %copy-done.3), channel_id=1, source_target_pairs={{0,16},{1,17},{2,18},{3,19},{4,20},{5,21},{6,22},{7,23},{8,24},{9,... | collective-permute-start | bytes 983048 | tf_op jit(solution)/shard_map/ppermute | solution.py:39
  18.5 16.8 %collective-permute-start.8 = (bf16[2,2560,128]{2,1,0:T(8,128)(2,1)S(1)}, bf16[2,2560,128]{2,1,0:T(8,128)(2,1)S(1)}, u32[]{:S(2)}, u32[]{:S(2)}) collective-permute-start(bf16[2,2560,128]{2,1,0:T(8,128)(2,1)S(1)} %shard_map.85), channel_id=1, source_target_pairs={{0,4},{1,5},{2,6},{3,7},{4,0},{5,1},{6,2},{7,3},{8,12},{9,13},{10,... | collective-permute-start | bytes 3932168 | tf_op jit(solution)/shard_map/ppermute | solution.py:39
  19.4 18.0 %collective-permute-start.4 = (bf16[128,5120]{1,0:T(8,128)(2,1)S(1)}, bf16[128,5120]{1,0:T(8,128)(2,1)S(1)}, u32[]{:S(2)}, u32[]{:S(2)}) collective-permute-start(bf16[128,5120]{1,0:T(8,128)(2,1)S(1)} %shard_map.83.refs_0_), channel_id=1, source_target_pairs={{0,1},{1,2},{2,3},{3,0},{4,5},{5,6},{6,7},{7,4},{8,9},{9,10},{10,1... | collective-permute-start | bytes 3932168 | tf_op jit(solution)/shard_map/ppermute | solution.py:39
  20.7 16.8 %collective-permute-start.5 = (bf16[128,5120]{1,0:T(8,128)(2,1)S(1)}, bf16[128,5120]{1,0:T(8,128)(2,1)S(1)}, u32[]{:S(2)}, u32[]{:S(2)}) collective-permute-start(bf16[128,5120]{1,0:T(8,128)(2,1)S(1)} %shard_map.83.refs_0_), channel_id=1, source_target_pairs={{0,3},{1,0},{2,1},{3,2},{4,7},{5,4},{6,5},{7,6},{8,11},{9,8},{10,9... | collective-permute-start | bytes 3932168 | tf_op jit(solution)/shard_map/ppermute | solution.py:39
  22.1 18.2 %collective-permute-start.11 = (bf16[2,2560,128]{2,1,0:T(8,128)(2,1)S(1)}, bf16[2,2560,128]{2,1,0:T(8,128)(2,1)S(1)}, u32[]{:S(2)}, u32[]{:S(2)}) collective-permute-start(bf16[2,2560,128]{2,1,0:T(8,128)(2,1)S(1)} %shard_map.88.refs_4_.refs_3_), channel_id=1, source_target_pairs={{0,32},{1,33},{2,34},{3,35},{4,36},{5,37},{6,38},{7,39},{8,40},{9,... | collective-permute-start | bytes 3932168 | tf_op jit(solution)/shard_map/ppermute | solution.py:39
  24.7 12.6 %collective-permute-start = (f32[32,5120]{1,0:T(8,128)S(1)}, f32[32,5120]{1,0:T(8,128)S(1)}, u32[]{:S(2)}, u32[]{:S(2)}) collective-permute-start(f32[32,5120]{1,0:T(8,128)S(1)} %bitcast.5), channel_id=1, source_target_pairs={{0,32},{1,33},{2,34},{3,35},{4,36},{5,37},{6,38},{7,39},{8,40},{9,... | collective-permute-start | bytes 1966088 | tf_op jit(solution)/shard_map/ppermute | solution.py:39
  35.3 16.4 %collective-permute-start.9 = (bf16[2,2560,128]{2,1,0:T(8,128)(2,1)S(1)}, bf16[2,2560,128]{2,1,0:T(8,128)(2,1)S(1)}, u32[]{:S(2)}, u32[]{:S(2)}) collective-permute-start(bf16[2,2560,128]{2,1,0:T(8,128)(2,1)S(1)} %collective-permute-done.8.refs_6_.mine), channel_id=1, source_target_pairs={{0,32},{1,33},{2,34},{3,35},{4,36},{5,37},{6,38},{7,39},{8,40},{9,... | collective-permute-start | bytes 3932168 | tf_op jit(solution)/shard_map/ppermute | solution.py:39
  37.5 11.0 %collective-permute-start.6 = (bf16[64,5120]{1,0:T(8,128)(2,1)S(1)}, bf16[64,5120]{1,0:T(8,128)(2,1)S(1)}, u32[]{:S(2)}, u32[]{:S(2)}) collective-permute-start(bf16[64,5120]{1,0:T(8,128)(2,1)S(1)} %get-tuple-element.29), channel_id=1, source_target_pairs={{0,1},{1,2},{2,3},{3,0},{4,5},{5,6},{6,7},{7,4},{8,9},{9,10},{10,1... | collective-permute-start | bytes 1966088 | tf_op jit(solution)/shard_map/ppermute | solution.py:39
  38.8 9.7 %collective-permute-start.7 = (bf16[64,5120]{1,0:T(8,128)(2,1)S(1)}, bf16[64,5120]{1,0:T(8,128)(2,1)S(1)}, u32[]{:S(2)}, u32[]{:S(2)}) collective-permute-start(bf16[64,5120]{1,0:T(8,128)(2,1)S(1)} %get-tuple-element.30), channel_id=1, source_target_pairs={{0,3},{1,0},{2,1},{3,2},{4,7},{5,4},{6,5},{7,6},{8,11},{9,8},{10,9... | collective-permute-start | bytes 1966088 | tf_op jit(solution)/shard_map/ppermute | solution.py:39
  42.6 13.3 %collective-permute-start.12 = (bf16[384,512]{1,0:T(8,128)(2,1)S(1)}, bf16[384,512]{1,0:T(8,128)(2,1)S(1)}, u32[]{:S(2)}, u32[]{:S(2)}) collective-permute-start(bf16[384,512]{1,0:T(8,128)(2,1)S(1)} %shard_map.89.refs_0_), channel_id=1, source_target_pairs={{0,4},{1,5},{2,6},{3,7},{4,0},{5,1},{6,2},{7,3},{8,12},{9,13},{10,... | collective-permute-start | bytes 1179656 | tf_op jit(solution)/shard_map/ppermute | solution.py:39
  57.2 11.0 %collective-permute-start.16 = (bf16[64,5120]{1,0:T(8,128)(2,1)S(1)}, bf16[64,5120]{1,0:T(8,128)(2,1)S(1)}, u32[]{:S(2)}, u32[]{:S(2)}) collective-permute-start(bf16[64,5120]{1,0:T(8,128)(2,1)S(1)} %get-tuple-element.33.until), channel_id=1, source_target_pairs={{0,1},{1,2},{2,3},{3,0},{4,5},{5,6},{6,7},{7,4},{8,9},{9,10},{10,1... | collective-permute-start | bytes 1966088 | tf_op jit(solution)/shard_map/ppermute | solution.py:39
  57.2 10.9 %collective-permute-start.17 = (bf16[64,5120]{1,0:T(8,128)(2,1)S(1)}, bf16[64,5120]{1,0:T(8,128)(2,1)S(1)}, u32[]{:S(2)}, u32[]{:S(2)}) collective-permute-start(bf16[64,5120]{1,0:T(8,128)(2,1)S(1)} %get-tuple-element.40), channel_id=1, source_target_pairs={{0,3},{1,0},{2,1},{3,2},{4,7},{5,4},{6,5},{7,6},{8,11},{9,8},{10,9... | collective-permute-start | bytes 1966088 | tf_op jit(solution)/shard_map/ppermute | solution.py:39
  61.9 22.7 %collective-permute-start.19 = (bf16[64,5120]{1,0:T(8,128)(2,1)S(1)}, bf16[64,5120]{1,0:T(8,128)(2,1)S(1)}, u32[]{:S(2)}, u32[]{:S(2)}) collective-permute-start(bf16[64,5120]{1,0:T(8,128)(2,1)S(1)} %get-tuple-element.42), channel_id=1, source_target_pairs={{0,3},{1,0},{2,1},{3,2},{4,7},{5,4},{6,5},{7,6},{8,11},{9,8},{10,9... | collective-permute-start | bytes 1966088 | tf_op jit(solution)/shard_map/ppermute | solution.py:39
  61.9 22.7 %collective-permute-start.20 = (bf16[64,5120]{1,0:T(8,128)(2,1)S(1)}, bf16[64,5120]{1,0:T(8,128)(2,1)S(1)}, u32[]{:S(2)}, u32[]{:S(2)}) collective-permute-start(bf16[64,5120]{1,0:T(8,128)(2,1)S(1)} %get-tuple-element.43), channel_id=1, source_target_pairs={{0,1},{1,2},{2,3},{3,0},{4,5},{5,6},{6,7},{7,4},{8,9},{9,10},{10,1... | collective-permute-start | bytes 1966088 | tf_op jit(solution)/shard_map/ppermute | solution.py:39
  68.5 16.1 %collective-permute-start.18 = (bf16[64,5120]{1,0:T(8,128)(2,1)S(1)}, bf16[64,5120]{1,0:T(8,128)(2,1)S(1)}, u32[]{:S(2)}, u32[]{:S(2)}) collective-permute-start(bf16[64,5120]{1,0:T(8,128)(2,1)S(1)} %get-tuple-element.41), channel_id=1, source_target_pairs={{0,1},{1,2},{2,3},{3,0},{4,5},{5,6},{6,7},{7,4},{8,9},{9,10},{10,1... | collective-permute-start | bytes 1966088 | tf_op jit(solution)/shard_map/ppermute | solution.py:39
  68.6 16.1 %collective-permute-start.21 = (bf16[64,5120]{1,0:T(8,128)(2,1)S(1)}, bf16[64,5120]{1,0:T(8,128)(2,1)S(1)}, u32[]{:S(2)}, u32[]{:S(2)}) collective-permute-start(bf16[64,5120]{1,0:T(8,128)(2,1)S(1)} %get-tuple-element.44), channel_id=1, source_target_pairs={{0,3},{1,0},{2,1},{3,2},{4,7},{5,4},{6,5},{7,6},{8,11},{9,8},{10,9... | collective-permute-start | bytes 1966088 | tf_op jit(solution)/shard_map/ppermute | solution.py:39
  71.3 7.8 %collective-permute-start.14 = (f32[16,5120]{1,0:T(8,128)S(1)}, f32[16,5120]{1,0:T(8,128)S(1)}, u32[]{:S(2)}, u32[]{:S(2)}) collective-permute-start(f32[16,5120]{1,0:T(8,128)S(1)} %shard_map.92), channel_id=1, source_target_pairs={{0,64},{1,65},{2,66},{3,67},{4,68},{5,69},{6,70},{7,71},{8,72},{9,... | collective-permute-start | bytes 983048 | tf_op jit(solution)/shard_map/ppermute | solution.py:39
  79.2 9.9 %collective-permute-start.15 = (f32[16,5120]{1,0:T(8,128)S(1)}, f32[16,5120]{1,0:T(8,128)S(1)}, u32[]{:S(2)}, u32[]{:S(2)}) collective-permute-start(f32[16,5120]{1,0:T(8,128)S(1)} %collective-permute-done.14.own_start), channel_id=1, source_target_pairs={{0,32},{1,33},{2,34},{3,35},{4,36},{5,37},{6,38},{7,39},{8,40},{9,... | collective-permute-start | bytes 983048 | tf_op jit(solution)/shard_map/ppermute | solution.py:39
  85.1 7.8 %collective-permute-start.22 = (bf16[32,5120]{1,0:T(8,128)(2,1)S(1)}, bf16[32,5120]{1,0:T(8,128)(2,1)S(1)}, u32[]{:S(2)}, u32[]{:S(2)}) collective-permute-start(bf16[32,5120]{1,0:T(8,128)(2,1)S(1)} %get-tuple-element.46), channel_id=1, source_target_pairs={{0,16},{1,17},{2,18},{3,19},{4,20},{5,21},{6,22},{7,23},{8,24},{9,... | collective-permute-start | bytes 983048 | tf_op jit(solution)/shard_map/ppermute | solution.py:39
  86.3 10.1 %collective-permute-start.23 = (bf16[32,5120]{1,0:T(8,128)(2,1)S(1)}, bf16[32,5120]{1,0:T(8,128)(2,1)S(1)}, u32[]{:S(2)}, u32[]{:S(2)}) collective-permute-start(bf16[32,5120]{1,0:T(8,128)(2,1)S(1)} %get-tuple-element.47), channel_id=1, source_target_pairs={{0,8},{1,9},{2,10},{3,11},{4,12},{5,13},{6,14},{7,15},{8,16},{9,17... | collective-permute-start | bytes 983048 | tf_op jit(solution)/shard_map/ppermute | solution.py:39
  87.1 9.3 %collective-permute-start.24 = (bf16[32,5120]{1,0:T(8,128)(2,1)S(1)}, bf16[32,5120]{1,0:T(8,128)(2,1)S(1)}, u32[]{:S(2)}, u32[]{:S(2)}) collective-permute-start(bf16[32,5120]{1,0:T(8,128)(2,1)S(1)} %get-tuple-element.48), channel_id=1, source_target_pairs={{0,24},{1,25},{2,26},{3,27},{4,28},{5,29},{6,30},{7,31},{8,0},{9,1... | collective-permute-start | bytes 983048 | tf_op jit(solution)/shard_map/ppermute | solution.py:39
  (11 other events, 66.8 us)

commit v9 on v8

--- a/solution.py
+++ b/solution.py
@@ -67,7 +67,8 @@
     return (1 - yh, core, x, yl, z)
 
 
-def modulate_kernel(index, state, scale, shift, gate, out, gates):
+def modulate_kernel(index, core, state, scale, shift, gate, out, gates, core_after):
+    core_after[0] = core[0]
     row = pl.ds(lax.rem(index[0], 8), 1)
     value = state[...]
     mean = jnp.mean(value * value, axis=-1, keepdims=True)
@@ -76,25 +77,26 @@
     gates[...] = gate[row, :]
 
 
-def modulate(index, state, scale, shift, gate):
+def modulate(index, core, state, scale, shift, gate):
     rows, width = state.shape
-    table = pl.BlockSpec((8, width), lambda i, index: (lax.div(index[0], 8), 0))
-    whole = pl.BlockSpec((rows, width), lambda i, index: (0, 0))
+    table = pl.BlockSpec((8, width), lambda i, index, core: (lax.div(index[0], 8), 0))
+    whole = pl.BlockSpec((rows, width), lambda i, index, core: (0, 0))
     return pl.pallas_call(
         modulate_kernel,
         grid_spec=pltpu.PrefetchScalarGridSpec(
-            num_scalar_prefetch=1,
+            num_scalar_prefetch=2,
             grid=(1,),
             in_specs=[whole, table, table, table],
-            out_specs=[whole, pl.BlockSpec((1, width), lambda i, index: (0, 0))],
+            out_specs=[whole, pl.BlockSpec((1, width), lambda i, index, core: (0, 0)), SMEM],
         ),
         out_shape=[
             jax.ShapeDtypeStruct(state.shape, BF16),
             jax.ShapeDtypeStruct((1, width), F32),
+            jax.ShapeDtypeStruct((1,), jnp.int32),
         ],
         compiler_params=WIDE,
         cost_estimate=pl.CostEstimate(flops=1000000, bytes_accessed=2000000, transcendentals=0),
-    )(index, state, scale, shift, gate)
+    )(index, core, state, scale, shift, gate)
 
 
 def pack_kernel(kinds, core, qkv, *refs):
@@ -424,12 +426,14 @@
     core = group & 1
     place, core, index = group[None], core[None], window_start + group
     state = trajectory[0]
-    modulated, gates = modulate(index, state, scale_table, shift_table, gate_table)
+    modulated, gates, core_after = modulate(
+        index, core, state, scale_table, shift_table, gate_table
+    )
     near_start = send(state, to_other_core)
     minus, plus, opposite = [send(modulated, first_axis(s)) for s in (1, -1, 2)]
     near = stack(modulated, minus, plus, opposite)
     before, after = send(near, second_axis(1)), send(near, second_axis(-1))
-    kv_mine = send(pack((1, 2), core, qkv_weight, gates), to_both_sides)
+    kv_mine = send(pack((1, 2), core_after, qkv_weight), to_both_sides)
     qo_mine = send(pack((0, 3), core, qkv_weight, out_weight, minus, plus, opposite), to_both_sides)
     before_half, after_half = first_and_second_half(before, after, near_start)
     last = [send(before_half, second_axis(1)), send(after_half, second_axis(-1))]

time: 112 us -> 112 us (level)
  no operation moved by 1% of the time
where the time goes in v9:
time: 112 us; the launch traced here: 111 us
  waiting for transfers between devices  51.7 us (46%)
  starting transfers between devices  42.7 us (38%)
  Pallas kernels  16.1 us (14%)
    ppermute x28, waiting for transfers between devices, send(): return lax.ppermute(value, ('tm', 'seq'), moves(rule))  51.7 us
    ppermute x28, starting transfers between devices, send(): return lax.ppermute(value, ('tm', 'seq'), moves(rule))  42.7 us
    pallas_call x3, Pallas kernels, project(): pl.pallas_call(functools.partial(project_kernel, len(pieces), kinds, rows...  4.65 us
    pallas_call x3, Pallas kernels, attend(): pl.pallas_call(functools.partial(attend_kernel, len(near), cuts), out_sha...  4.62 us
    pallas_call x1, Pallas kernels, modulate(): pl.pallas_call(modulate_kernel, grid_spec=pltpu.PrefetchScalarGridSpec(nu...  2.4 us
  transfers between devices with their start and end apart: 28, of which 14 were waited for; matrix products, arithmetic and copies ran while one was open for 0% of the time, Pallas kernels for 8%

profile of v9, /device:TPU:17, one launch (start us, length us, event | category | flops | bytes accessed | tf_op | source)
XLA Modules:
  0.0 111.4 jit_solution(2281486950641314070)
XLA Ops:
  0.7 2.4 %shard_map.82 = (bf16[32,5120]{1,0:T(8,128)(2,1)}, f32[1,5120]{1,0:T(1,128)}, s32[1]{0:T(128)}) custom-call(s32[1]{0:T(128)S(6)} %add.4.index, s32[1]{0:T(128)} %bitcast.2.core, f32[32,5120]{1,0:T(8,128)} %bitcast.4, f32[50,5120]{1,0:T(8,128)} %scale.1, f32[50,5120]{1,0:T(8,128)} %shift.1, f32[50,5120]{1,0:T(8,128)} %gate.1), custom_call_target="tpu_custom_call" | custom-call | flops 1000000 | bytes 2000000 | tf_op jit(solution)/shard_map/pallas_call | solution.py:84
  6.1 2.1 %collective-permute-start.2 = (bf16[32,5120]{1,0:T(8,128)(2,1)S(1)}, bf16[32,5120]{1,0:T(8,128)(2,1)S(1)}, u32[]{:S(2)}, u32[]{:S(2)}) collective-permute-start(bf16[32,5120]{1,0:T(8,128)(2,1)S(1)} %copy-done.3), channel_id=1, source_target_pairs={{0,24},{1,25},{2,26},{3,27},{4,28},{5,29},{6,30},{7,31},{8,0},{9,1... | collective-permute-start | bytes 983048 | tf_op jit(solution)/shard_map/ppermute | solution.py:39
  9.6 3.5 %collective-permute-done.1.refs_1_ = bf16[32,5120]{1,0:T(8,128)(2,1)S(1)} collective-permute-done((bf16[32,5120]{1,0:T(8,128)(2,1)S(1)}, bf16[32,5120]{1,0:T(8,128)(2,1)S(1)}, u32[]{:S(2)}, u32[]{:S(2)}) %collective-permute-start.1) | collective-permute-done | bytes 327712 | tf_op jit(solution)/shard_map/ppermute | solution.py:39
  13.0 2.8 %collective-permute-done.2.refs_2_ = bf16[32,5120]{1,0:T(8,128)(2,1)S(1)} collective-permute-done((bf16[32,5120]{1,0:T(8,128)(2,1)S(1)}, bf16[32,5120]{1,0:T(8,128)(2,1)S(1)}, u32[]{:S(2)}, u32[]{:S(2)}) %collective-permute-start.2) | collective-permute-done | bytes 327712 | tf_op jit(solution)/shard_map/ppermute | solution.py:39
  15.8 1.9 %collective-permute-done.3.refs_3_ = bf16[32,5120]{1,0:T(8,128)(2,1)S(1)} collective-permute-done((bf16[32,5120]{1,0:T(8,128)(2,1)S(1)}, bf16[32,5120]{1,0:T(8,128)(2,1)S(1)}, u32[]{:S(2)}, u32[]{:S(2)}) %collective-permute-start.3) | collective-permute-done | bytes 327712 | tf_op jit(solution)/shard_map/ppermute | solution.py:39
  22.1 2.5 %collective-permute-start.11 = (bf16[2,2560,128]{2,1,0:T(8,128)(2,1)S(1)}, bf16[2,2560,128]{2,1,0:T(8,128)(2,1)S(1)}, u32[]{:S(2)}, u32[]{:S(2)}) collective-permute-start(bf16[2,2560,128]{2,1,0:T(8,128)(2,1)S(1)} %shard_map.88.refs_4_.refs_3_), channel_id=1, source_target_pairs={{0,32},{1,33},{2,34},{3,35},{4,36},{5,37},{6,38},{7,39},{8,40},{9,... | collective-permute-start | bytes 3932168 | tf_op jit(solution)/shard_map/ppermute | solution.py:39
  24.7 10.4 %collective-permute-done.8.refs_6_.mine = bf16[2,2560,128]{2,1,0:T(8,128)(2,1)S(1)} collective-permute-done((bf16[2,2560,128]{2,1,0:T(8,128)(2,1)S(1)}, bf16[2,2560,128]{2,1,0:T(8,128)(2,1)S(1)}, u32[]{:S(2)}, u32[]{:S(2)}) %collective-permute-start.8) | collective-permute-done | bytes 1310752 | tf_op jit(solution)/shard_map/ppermute | solution.py:39
  35.1 2.1 %collective-permute-start.9 = (bf16[2,2560,128]{2,1,0:T(8,128)(2,1)S(1)}, bf16[2,2560,128]{2,1,0:T(8,128)(2,1)S(1)}, u32[]{:S(2)}, u32[]{:S(2)}) collective-permute-start(bf16[2,2560,128]{2,1,0:T(8,128)(2,1)S(1)} %collective-permute-done.8.refs_6_.mine), channel_id=1, source_target_pairs={{0,32},{1,33},{2,34},{3,35},{4,36},{5,37},{6,38},{7,39},{8,40},{9,... | collective-permute-start | bytes 3932168 | tf_op jit(solution)/shard_map/ppermute | solution.py:39
  40.3 2.2 %shard_map.89.refs_0_ = bf16[384,512]{1,0:T(8,128)(2,1)S(1)} custom-call(s32[1]{0:T(128)} %bitcast.2.core, bf16[128,5120]{1,0:T(8,128)(2,1)S(1)} %shard_map.83.refs_0_, bf16[128,5120]{1,0:T(8,128)(2,1)S(1)} %collective-permute-done.4.one.refs_1_, bf16[128,5120]{1,0:T(8,128)(2,1)S(1)} %collective-permute-done.5.two.refs_2_, ...), custom_call_target="tpu_custom_call" | custom-call | flops 2013265920 | bytes 1000000 | tf_op jit(solution)/shard_map/pallas_call | solution.py:217
  42.5 2.3 %collective-permute-start.12 = (bf16[384,512]{1,0:T(8,128)(2,1)S(1)}, bf16[384,512]{1,0:T(8,128)(2,1)S(1)}, u32[]{:S(2)}, u32[]{:S(2)}) collective-permute-start(bf16[384,512]{1,0:T(8,128)(2,1)S(1)} %shard_map.89.refs_0_), channel_id=1, source_target_pairs={{0,4},{1,5},{2,6},{3,7},{4,0},{5,1},{6,2},{7,3},{8,12},{9,13},{10,... | collective-permute-start | bytes 1179656 | tf_op jit(solution)/shard_map/ppermute | solution.py:39
  44.8 3.7 %collective-permute-done.6.refs_3_.refs_0_ = bf16[64,5120]{1,0:T(8,128)(2,1)S(1)} collective-permute-done((bf16[64,5120]{1,0:T(8,128)(2,1)S(1)}, bf16[64,5120]{1,0:T(8,128)(2,1)S(1)}, u32[]{:S(2)}, u32[]{:S(2)}) %collective-permute-start.6) | collective-permute-done | bytes 655392 | tf_op jit(solution)/shard_map/ppermute | solution.py:39
  49.4 2.3 %collective-permute-start.13 = (bf16[128,512]{1,0:T(8,128)(2,1)S(1)}, bf16[128,512]{1,0:T(8,128)(2,1)S(1)}, u32[]{:S(2)}, u32[]{:S(2)}) collective-permute-start(bf16[128,512]{1,0:T(8,128)(2,1)S(1)} %shard_map.90.refs_1_), channel_id=1, source_target_pairs={{0,4},{1,5},{2,6},{3,7},{4,0},{5,1},{6,2},{7,3},{8,12},{9,13},{10,... | collective-permute-start | bytes 393224 | tf_op jit(solution)/shard_map/ppermute | solution.py:39
  53.2 2.6 %collective-permute-done.13.refs_3_ = bf16[128,512]{1,0:T(8,128)(2,1)S(1)} collective-permute-done((bf16[128,512]{1,0:T(8,128)(2,1)S(1)}, bf16[128,512]{1,0:T(8,128)(2,1)S(1)}, u32[]{:S(2)}, u32[]{:S(2)}) %collective-permute-start.13) | collective-permute-done | bytes 131104 | tf_op jit(solution)/shard_map/ppermute | solution.py:39
  57.2 2.7 %collective-permute-start.17 = (bf16[64,5120]{1,0:T(8,128)(2,1)S(1)}, bf16[64,5120]{1,0:T(8,128)(2,1)S(1)}, u32[]{:S(2)}, u32[]{:S(2)}) collective-permute-start(bf16[64,5120]{1,0:T(8,128)(2,1)S(1)} %get-tuple-element.41), channel_id=1, source_target_pairs={{0,3},{1,0},{2,1},{3,2},{4,7},{5,4},{6,5},{7,6},{8,11},{9,8},{10,9... | collective-permute-start | bytes 1966088 | tf_op jit(solution)/shard_map/ppermute | solution.py:39
  59.9 1.9 %shard_map.94 = (bf16[64,5120]{1,0:T(8,128)(2,1)S(1)}, bf16[64,5120]{1,0:T(8,128)(2,1)S(1)}, bf16[64,5120]{1,0:T(8,128)(2,1)S(1)}, bf16[64,5120]{1,0:T(8,128)(2,1)S(1)}) custom-call(s32[1]{0:T(128)} %bitcast.2.core, bf16[256,256]{1,0:T(8,128)(2,1)S(1)} %get-tuple-element.38.queries, bf16[128,5120]{1,0:T(8,128)(2,1)S(1)} %copy-done.1, ...), custom_call_target="tpu_custom_call" | custom-call | flops 939524096 | bytes 1000000 | tf_op jit(solution)/shard_map/pallas_call | solution.py:271
  63.3 4.8 %collective-permute-done.16.low = bf16[64,5120]{1,0:T(8,128)(2,1)S(1)} collective-permute-done((bf16[64,5120]{1,0:T(8,128)(2,1)S(1)}, bf16[64,5120]{1,0:T(8,128)(2,1)S(1)}, u32[]{:S(2)}, u32[]{:S(2)}) %collective-permute-start.16) | collective-permute-done | bytes 655392 | tf_op jit(solution)/shard_map/ppermute | solution.py:39
  68.5 2.7 %collective-permute-start.21 = (bf16[64,5120]{1,0:T(8,128)(2,1)S(1)}, bf16[64,5120]{1,0:T(8,128)(2,1)S(1)}, u32[]{:S(2)}, u32[]{:S(2)}) collective-permute-start(bf16[64,5120]{1,0:T(8,128)(2,1)S(1)} %get-tuple-element.45), channel_id=1, source_target_pairs={{0,3},{1,0},{2,1},{3,2},{4,7},{5,4},{6,5},{7,6},{8,11},{9,8},{10,9... | collective-permute-start | bytes 1966088 | tf_op jit(solution)/shard_map/ppermute | solution.py:39
  73.7 5.4 %collective-permute-done.14.own_start = f32[16,5120]{1,0:T(8,128)S(1)} collective-permute-done((f32[16,5120]{1,0:T(8,128)S(1)}, f32[16,5120]{1,0:T(8,128)S(1)}, u32[]{:S(2)}, u32[]{:S(2)}) %collective-permute-start.14) | collective-permute-done | bytes 327712 | tf_op jit(solution)/shard_map/ppermute | solution.py:39
  79.1 5.5 %collective-permute-start.15 = (f32[16,5120]{1,0:T(8,128)S(1)}, f32[16,5120]{1,0:T(8,128)S(1)}, u32[]{:S(2)}, u32[]{:S(2)}) collective-permute-start(f32[16,5120]{1,0:T(8,128)S(1)} %collective-permute-done.14.own_start), channel_id=1, source_target_pairs={{0,32},{1,33},{2,34},{3,35},{4,36},{5,37},{6,38},{7,39},{8,40},{9,... | collective-permute-start | bytes 983048 | tf_op jit(solution)/shard_map/ppermute | solution.py:39
  87.1 1.9 %collective-permute-start.24 = (bf16[32,5120]{1,0:T(8,128)(2,1)S(1)}, bf16[32,5120]{1,0:T(8,128)(2,1)S(1)}, u32[]{:S(2)}, u32[]{:S(2)}) collective-permute-start(bf16[32,5120]{1,0:T(8,128)(2,1)S(1)} %get-tuple-element.49), channel_id=1, source_target_pairs={{0,24},{1,25},{2,26},{3,27},{4,28},{5,29},{6,30},{7,31},{8,0},{9,1... | collective-permute-start | bytes 983048 | tf_op jit(solution)/shard_map/ppermute | solution.py:39
  89.0 4.0 %collective-permute-done.22.one = bf16[32,5120]{1,0:T(8,128)(2,1)S(1)} collective-permute-done((bf16[32,5120]{1,0:T(8,128)(2,1)S(1)}, bf16[32,5120]{1,0:T(8,128)(2,1)S(1)}, u32[]{:S(2)}, u32[]{:S(2)}) %collective-permute-start.22) | collective-permute-done | bytes 327712 | tf_op jit(solution)/shard_map/ppermute | solution.py:39
  92.9 3.5 %collective-permute-done.23.two = bf16[32,5120]{1,0:T(8,128)(2,1)S(1)} collective-permute-done((bf16[32,5120]{1,0:T(8,128)(2,1)S(1)}, bf16[32,5120]{1,0:T(8,128)(2,1)S(1)}, u32[]{:S(2)}, u32[]{:S(2)}) %collective-permute-start.23) | collective-permute-done | bytes 327712 | tf_op jit(solution)/shard_map/ppermute | solution.py:39
  97.2 2.6 %collective-permute-start.25 = (bf16[32,5120]{1,0:T(8,128)(2,1)S(1)}, bf16[32,5120]{1,0:T(8,128)(2,1)S(1)}, u32[]{:S(2)}, u32[]{:S(2)}) collective-permute-start(bf16[32,5120]{1,0:T(8,128)(2,1)S(1)} %get-tuple-element.52), channel_id=1, source_target_pairs={{0,32},{1,33},{2,34},{3,35},{4,36},{5,37},{6,38},{7,39},{8,40},{9,... | collective-permute-start | bytes 983048 | tf_op jit(solution)/shard_map/ppermute | solution.py:39
  101.2 6.9 %collective-permute-done.26.own_sum = bf16[16,5120]{1,0:T(8,128)(2,1)S(1)} collective-permute-done((bf16[16,5120]{1,0:T(8,128)(2,1)S(1)}, bf16[16,5120]{1,0:T(8,128)(2,1)S(1)}, u32[]{:S(2)}, u32[]{:S(2)}) %collective-permute-start.26) | collective-permute-done | bytes 163872 | tf_op jit(solution)/shard_map/ppermute | solution.py:39
  (62 shorter events, 28.0 us)
Async XLA Ops:
  4.2 17.8 %collective-permute-start.10 = (bf16[2,2560,128]{2,1,0:T(8,128)(2,1)S(1)}, bf16[2,2560,128]{2,1,0:T(8,128)(2,1)S(1)}, u32[]{:S(2)}, u32[]{:S(2)}) collective-permute-start(bf16[2,2560,128]{2,1,0:T(8,128)(2,1)S(1)} %shard_map.87), channel_id=1, source_target_pairs={{0,4},{1,5},{2,6},{3,7},{4,0},{5,1},{6,2},{7,3},{8,12},{9,13},{10,... | collective-permute-start | bytes 3932168 | tf_op jit(solution)/shard_map/ppermute | solution.py:39
  4.5 8.5 %collective-permute-start.1 = (bf16[32,5120]{1,0:T(8,128)(2,1)S(1)}, bf16[32,5120]{1,0:T(8,128)(2,1)S(1)}, u32[]{:S(2)}, u32[]{:S(2)}) collective-permute-start(bf16[32,5120]{1,0:T(8,128)(2,1)S(1)} %copy-done.3), channel_id=1, source_target_pairs={{0,8},{1,9},{2,10},{3,11},{4,12},{5,13},{6,14},{7,15},{8,16},{9,17... | collective-permute-start | bytes 983048 | tf_op jit(solution)/shard_map/ppermute | solution.py:39
  6.1 9.7 %collective-permute-start.2 = (bf16[32,5120]{1,0:T(8,128)(2,1)S(1)}, bf16[32,5120]{1,0:T(8,128)(2,1)S(1)}, u32[]{:S(2)}, u32[]{:S(2)}) collective-permute-start(bf16[32,5120]{1,0:T(8,128)(2,1)S(1)} %copy-done.3), channel_id=1, source_target_pairs={{0,24},{1,25},{2,26},{3,27},{4,28},{5,29},{6,30},{7,31},{8,0},{9,1... | collective-permute-start | bytes 983048 | tf_op jit(solution)/shard_map/ppermute | solution.py:39
  8.3 9.4 %collective-permute-start.3 = (bf16[32,5120]{1,0:T(8,128)(2,1)S(1)}, bf16[32,5120]{1,0:T(8,128)(2,1)S(1)}, u32[]{:S(2)}, u32[]{:S(2)}) collective-permute-start(bf16[32,5120]{1,0:T(8,128)(2,1)S(1)} %copy-done.3), channel_id=1, source_target_pairs={{0,16},{1,17},{2,18},{3,19},{4,20},{5,21},{6,22},{7,23},{8,24},{9,... | collective-permute-start | bytes 983048 | tf_op jit(solution)/shard_map/ppermute | solution.py:39
  18.1 17.0 %collective-permute-start.8 = (bf16[2,2560,128]{2,1,0:T(8,128)(2,1)S(1)}, bf16[2,2560,128]{2,1,0:T(8,128)(2,1)S(1)}, u32[]{:S(2)}, u32[]{:S(2)}) collective-permute-start(bf16[2,2560,128]{2,1,0:T(8,128)(2,1)S(1)} %shard_map.85), channel_id=1, source_target_pairs={{0,4},{1,5},{2,6},{3,7},{4,0},{5,1},{6,2},{7,3},{8,12},{9,13},{10,... | collective-permute-start | bytes 3932168 | tf_op jit(solution)/shard_map/ppermute | solution.py:39
  19.3 18.0 %collective-permute-start.4 = (bf16[128,5120]{1,0:T(8,128)(2,1)S(1)}, bf16[128,5120]{1,0:T(8,128)(2,1)S(1)}, u32[]{:S(2)}, u32[]{:S(2)}) collective-permute-start(bf16[128,5120]{1,0:T(8,128)(2,1)S(1)} %shard_map.83.refs_0_), channel_id=1, source_target_pairs={{0,1},{1,2},{2,3},{3,0},{4,5},{5,6},{6,7},{7,4},{8,9},{9,10},{10,1... | collective-permute-start | bytes 3932168 | tf_op jit(solution)/shard_map/ppermute | solution.py:39
  20.6 16.8 %collective-permute-start.5 = (bf16[128,5120]{1,0:T(8,128)(2,1)S(1)}, bf16[128,5120]{1,0:T(8,128)(2,1)S(1)}, u32[]{:S(2)}, u32[]{:S(2)}) collective-permute-start(bf16[128,5120]{1,0:T(8,128)(2,1)S(1)} %shard_map.83.refs_0_), channel_id=1, source_target_pairs={{0,3},{1,0},{2,1},{3,2},{4,7},{5,4},{6,5},{7,6},{8,11},{9,8},{10,9... | collective-permute-start | bytes 3932168 | tf_op jit(solution)/shard_map/ppermute | solution.py:39
  22.1 18.2 %collective-permute-start.11 = (bf16[2,2560,128]{2,1,0:T(8,128)(2,1)S(1)}, bf16[2,2560,128]{2,1,0:T(8,128)(2,1)S(1)}, u32[]{:S(2)}, u32[]{:S(2)}) collective-permute-start(bf16[2,2560,128]{2,1,0:T(8,128)(2,1)S(1)} %shard_map.88.refs_4_.refs_3_), channel_id=1, source_target_pairs={{0,32},{1,33},{2,34},{3,35},{4,36},{5,37},{6,38},{7,39},{8,40},{9,... | collective-permute-start | bytes 3932168 | tf_op jit(solution)/shard_map/ppermute | solution.py:39
  24.6 12.6 %collective-permute-start = (f32[32,5120]{1,0:T(8,128)S(1)}, f32[32,5120]{1,0:T(8,128)S(1)}, u32[]{:S(2)}, u32[]{:S(2)}) collective-permute-start(f32[32,5120]{1,0:T(8,128)S(1)} %bitcast.5), channel_id=1, source_target_pairs={{0,32},{1,33},{2,34},{3,35},{4,36},{5,37},{6,38},{7,39},{8,40},{9,... | collective-permute-start | bytes 1966088 | tf_op jit(solution)/shard_map/ppermute | solution.py:39
  35.1 16.5 %collective-permute-start.9 = (bf16[2,2560,128]{2,1,0:T(8,128)(2,1)S(1)}, bf16[2,2560,128]{2,1,0:T(8,128)(2,1)S(1)}, u32[]{:S(2)}, u32[]{:S(2)}) collective-permute-start(bf16[2,2560,128]{2,1,0:T(8,128)(2,1)S(1)} %collective-permute-done.8.refs_6_.mine), channel_id=1, source_target_pairs={{0,32},{1,33},{2,34},{3,35},{4,36},{5,37},{6,38},{7,39},{8,40},{9,... | collective-permute-start | bytes 3932168 | tf_op jit(solution)/shard_map/ppermute | solution.py:39
  37.4 11.0 %collective-permute-start.6 = (bf16[64,5120]{1,0:T(8,128)(2,1)S(1)}, bf16[64,5120]{1,0:T(8,128)(2,1)S(1)}, u32[]{:S(2)}, u32[]{:S(2)}) collective-permute-start(bf16[64,5120]{1,0:T(8,128)(2,1)S(1)} %get-tuple-element.30), channel_id=1, source_target_pairs={{0,1},{1,2},{2,3},{3,0},{4,5},{5,6},{6,7},{7,4},{8,9},{9,10},{10,1... | collective-permute-start | bytes 1966088 | tf_op jit(solution)/shard_map/ppermute | solution.py:39
  38.7 9.7 %collective-permute-start.7 = (bf16[64,5120]{1,0:T(8,128)(2,1)S(1)}, bf16[64,5120]{1,0:T(8,128)(2,1)S(1)}, u32[]{:S(2)}, u32[]{:S(2)}) collective-permute-start(bf16[64,5120]{1,0:T(8,128)(2,1)S(1)} %get-tuple-element.31), channel_id=1, source_target_pairs={{0,3},{1,0},{2,1},{3,2},{4,7},{5,4},{6,5},{7,6},{8,11},{9,8},{10,9... | collective-permute-start | bytes 1966088 | tf_op jit(solution)/shard_map/ppermute | solution.py:39
  42.5 13.3 %collective-permute-start.12 = (bf16[384,512]{1,0:T(8,128)(2,1)S(1)}, bf16[384,512]{1,0:T(8,128)(2,1)S(1)}, u32[]{:S(2)}, u32[]{:S(2)}) collective-permute-start(bf16[384,512]{1,0:T(8,128)(2,1)S(1)} %shard_map.89.refs_0_), channel_id=1, source_target_pairs={{0,4},{1,5},{2,6},{3,7},{4,0},{5,1},{6,2},{7,3},{8,12},{9,13},{10,... | collective-permute-start | bytes 1179656 | tf_op jit(solution)/shard_map/ppermute | solution.py:39
  57.1 11.0 %collective-permute-start.16 = (bf16[64,5120]{1,0:T(8,128)(2,1)S(1)}, bf16[64,5120]{1,0:T(8,128)(2,1)S(1)}, u32[]{:S(2)}, u32[]{:S(2)}) collective-permute-start(bf16[64,5120]{1,0:T(8,128)(2,1)S(1)} %get-tuple-element.34.until), channel_id=1, source_target_pairs={{0,1},{1,2},{2,3},{3,0},{4,5},{5,6},{6,7},{7,4},{8,9},{9,10},{10,1... | collective-permute-start | bytes 1966088 | tf_op jit(solution)/shard_map/ppermute | solution.py:39
  57.2 10.9 %collective-permute-start.17 = (bf16[64,5120]{1,0:T(8,128)(2,1)S(1)}, bf16[64,5120]{1,0:T(8,128)(2,1)S(1)}, u32[]{:S(2)}, u32[]{:S(2)}) collective-permute-start(bf16[64,5120]{1,0:T(8,128)(2,1)S(1)} %get-tuple-element.41), channel_id=1, source_target_pairs={{0,3},{1,0},{2,1},{3,2},{4,7},{5,4},{6,5},{7,6},{8,11},{9,8},{10,9... | collective-permute-start | bytes 1966088 | tf_op jit(solution)/shard_map/ppermute | solution.py:39
  61.8 22.7 %collective-permute-start.19 = (bf16[64,5120]{1,0:T(8,128)(2,1)S(1)}, bf16[64,5120]{1,0:T(8,128)(2,1)S(1)}, u32[]{:S(2)}, u32[]{:S(2)}) collective-permute-start(bf16[64,5120]{1,0:T(8,128)(2,1)S(1)} %get-tuple-element.43), channel_id=1, source_target_pairs={{0,3},{1,0},{2,1},{3,2},{4,7},{5,4},{6,5},{7,6},{8,11},{9,8},{10,9... | collective-permute-start | bytes 1966088 | tf_op jit(solution)/shard_map/ppermute | solution.py:39
  61.9 22.7 %collective-permute-start.20 = (bf16[64,5120]{1,0:T(8,128)(2,1)S(1)}, bf16[64,5120]{1,0:T(8,128)(2,1)S(1)}, u32[]{:S(2)}, u32[]{:S(2)}) collective-permute-start(bf16[64,5120]{1,0:T(8,128)(2,1)S(1)} %get-tuple-element.44), channel_id=1, source_target_pairs={{0,1},{1,2},{2,3},{3,0},{4,5},{5,6},{6,7},{7,4},{8,9},{9,10},{10,1... | collective-permute-start | bytes 1966088 | tf_op jit(solution)/shard_map/ppermute | solution.py:39
  68.4 16.1 %collective-permute-start.18 = (bf16[64,5120]{1,0:T(8,128)(2,1)S(1)}, bf16[64,5120]{1,0:T(8,128)(2,1)S(1)}, u32[]{:S(2)}, u32[]{:S(2)}) collective-permute-start(bf16[64,5120]{1,0:T(8,128)(2,1)S(1)} %get-tuple-element.42), channel_id=1, source_target_pairs={{0,1},{1,2},{2,3},{3,0},{4,5},{5,6},{6,7},{7,4},{8,9},{9,10},{10,1... | collective-permute-start | bytes 1966088 | tf_op jit(solution)/shard_map/ppermute | solution.py:39
  68.5 16.1 %collective-permute-start.21 = (bf16[64,5120]{1,0:T(8,128)(2,1)S(1)}, bf16[64,5120]{1,0:T(8,128)(2,1)S(1)}, u32[]{:S(2)}, u32[]{:S(2)}) collective-permute-start(bf16[64,5120]{1,0:T(8,128)(2,1)S(1)} %get-tuple-element.45), channel_id=1, source_target_pairs={{0,3},{1,0},{2,1},{3,2},{4,7},{5,4},{6,5},{7,6},{8,11},{9,8},{10,9... | collective-permute-start | bytes 1966088 | tf_op jit(solution)/shard_map/ppermute | solution.py:39
  71.3 7.8 %collective-permute-start.14 = (f32[16,5120]{1,0:T(8,128)S(1)}, f32[16,5120]{1,0:T(8,128)S(1)}, u32[]{:S(2)}, u32[]{:S(2)}) collective-permute-start(f32[16,5120]{1,0:T(8,128)S(1)} %shard_map.92), channel_id=1, source_target_pairs={{0,64},{1,65},{2,66},{3,67},{4,68},{5,69},{6,70},{7,71},{8,72},{9,... | collective-permute-start | bytes 983048 | tf_op jit(solution)/shard_map/ppermute | solution.py:39
  79.1 9.9 %collective-permute-start.15 = (f32[16,5120]{1,0:T(8,128)S(1)}, f32[16,5120]{1,0:T(8,128)S(1)}, u32[]{:S(2)}, u32[]{:S(2)}) collective-permute-start(f32[16,5120]{1,0:T(8,128)S(1)} %collective-permute-done.14.own_start), channel_id=1, source_target_pairs={{0,32},{1,33},{2,34},{3,35},{4,36},{5,37},{6,38},{7,39},{8,40},{9,... | collective-permute-start | bytes 983048 | tf_op jit(solution)/shard_map/ppermute | solution.py:39
  85.1 7.8 %collective-permute-start.22 = (bf16[32,5120]{1,0:T(8,128)(2,1)S(1)}, bf16[32,5120]{1,0:T(8,128)(2,1)S(1)}, u32[]{:S(2)}, u32[]{:S(2)}) collective-permute-start(bf16[32,5120]{1,0:T(8,128)(2,1)S(1)} %get-tuple-element.47), channel_id=1, source_target_pairs={{0,16},{1,17},{2,18},{3,19},{4,20},{5,21},{6,22},{7,23},{8,24},{9,... | collective-permute-start | bytes 983048 | tf_op jit(solution)/shard_map/ppermute | solution.py:39
  86.3 10.1 %collective-permute-start.23 = (bf16[32,5120]{1,0:T(8,128)(2,1)S(1)}, bf16[32,5120]{1,0:T(8,128)(2,1)S(1)}, u32[]{:S(2)}, u32[]{:S(2)}) collective-permute-start(bf16[32,5120]{1,0:T(8,128)(2,1)S(1)} %get-tuple-element.48), channel_id=1, source_target_pairs={{0,8},{1,9},{2,10},{3,11},{4,12},{5,13},{6,14},{7,15},{8,16},{9,17... | collective-permute-start | bytes 983048 | tf_op jit(solution)/shard_map/ppermute | solution.py:39
  87.1 9.3 %collective-permute-start.24 = (bf16[32,5120]{1,0:T(8,128)(2,1)S(1)}, bf16[32,5120]{1,0:T(8,128)(2,1)S(1)}, u32[]{:S(2)}, u32[]{:S(2)}) collective-permute-start(bf16[32,5120]{1,0:T(8,128)(2,1)S(1)} %get-tuple-element.49), channel_id=1, source_target_pairs={{0,24},{1,25},{2,26},{3,27},{4,28},{5,29},{6,30},{7,31},{8,0},{9,1... | collective-permute-start | bytes 983048 | tf_op jit(solution)/shard_map/ppermute | solution.py:39
  (10 other events, 66.8 us)
